TPU v7x, 128 devices: a whole 4x4x4 slice. The times are simulated.
128 devices in a mesh: row: 8 (over x, core), col: 8 (over y, z_lo), rep: 2 (over z_hi).
Axes of the slice: x: 4, y: 4, z: 4 (z_hi: 2, z_lo: 2; z = z_hi * 2 + z_lo), core: 2. Of those that a mesh axis runs over, the one named last changes fastest.
Arguments:
- atom_feats: bfloat16 [2, 3072, 128], P('rep', ('row', 'col')), may hold values from -6 to 6
- atom_token: int32 [2, 3072], P('rep', ('row', 'col')), may hold values from 0 to 383, as said below
- atom_counts: int32 [2, 384], P('rep'), may hold values from 1 to 15, as said below
- restype: int32 [2, 384], P('rep'), may hold values from 0 to 31
- pair_in: bfloat16 [2, 384, 384, 128], P('rep', 'row', 'col'), may hold values from -6 to 6
- pair_mask: int32 [2, 384, 384], P('rep', 'row', 'col'), may hold values 0 or 1
- w_atom: bfloat16 [128, 384], replicated, may hold values from -0.5 to 0.5
- w_restype: bfloat16 [32, 384], replicated, may hold values from -6 to 6
- w_pair: bfloat16 [384, 256], replicated, may hold values from -0.3125 to 0.3125
- ln_tri: float32 [2, 128], replicated, may hold values from 0.5 to 1.5
- w_tri_in: bfloat16 [2, 128, 640], replicated, may hold values from -0.5 to 0.5
- ln_tri_out: float32 [2, 128], replicated, may hold values from 0.5 to 1.5
- w_tri_out: bfloat16 [2, 128, 128], replicated, may hold values from -0.5 to 0.5
- ln_trans: float32 [128], replicated, may hold values from 0.5 to 1.5
- w_up: bfloat16 [128, 1024], replicated, may hold values from -0.5 to 0.5
- w_down: bfloat16 [512, 128], replicated, may hold values from -0.25 to 0.25
- d_pair: bfloat16 [2, 384, 384, 128], P('rep', 'row', 'col'), may hold values from -0.03125 to 0.03125
Outputs:
- pair_out: bfloat16 [2, 384, 384, 128], P('rep', 'row', 'col')
- grad_down: float32 [512, 128], P(('row', 'col', 'rep'))
Inputs may be any that keep to these rules, and one draw needn't show every extreme that they name: `atom_counts`: every token has 1 to 15 atoms and a complex's counts sum to 3072; the tokens fall into pairs whose counts sum to 16. Atoms are listed token after token: in each complex atom_token never falls and names token t on exactly atom_counts[t] atoms.
All inputs are finite; a program needn't handle non-finite values. No bound on the sum of `pair_mask` on one device may be relied on, other than what follows from the above.
Results may differ from a plain program's by a relative error of at most 0.027.
Values may be sent and summed in bfloat16 or wider, within the bound.
No kernel may reach another device: no remote copies, remote signals or barrier semaphores. Data moves between devices by JAX's collectives and lax.ppermute only.
A program may use at most 128 MiB of HBM per device.

v0:
```python
import functools

import jax
import jax.numpy as jnp
from jax import lax
from jax.experimental import pallas as pl
from jax.experimental.pallas import tpu as pltpu
from jax.sharding import PartitionSpec as P

F32, BF16 = jnp.float32, jnp.bfloat16
LANES = 128
PARAMS = pltpu.CompilerParams(vmem_limit_bytes=40 * 2**20)


def nt(a, b):
    return lax.dot_general(a, b, (((1,), (1,)), ((), ())), preferred_element_type=F32)


def nn(a, b):
    return lax.dot_general(a, b, (((1,), (0,)), ((), ())), preferred_element_type=F32)


def tn(a, b):
    return lax.dot_general(a, b, (((0,), (0,)), ((), ())), preferred_element_type=F32)


def norm(values, scales, axis):
    average = jnp.mean(values, axis=axis, keepdims=True)
    centred = values - average
    variance = jnp.mean(centred * centred, axis=axis, keepdims=True)
    return centred * lax.rsqrt(variance + 1e-05) * scales


def sigmoid(x):
    return jax.nn.sigmoid(x)


def exchange(value, axes):
    return lax.all_to_all(value, axes, 0, 0, tiled=True)


def send_group(g, normed, weights, mask_row, wide, devices):
    proj = nt(weights, normed)
    half = proj.shape[0] // 2
    sides = sigmoid(proj[:half]) * proj[half:] * mask_row
    rows = wide.shape[0] // devices
    parts = sides.shape[1] // LANES
    kinds = half // devices
    for kind in range(kinds):
        for q in range(parts):
            wide[pl.ds((g * kinds + kind) * parts + q, devices, stride=rows), :] = sides[
                kind * devices : (kind + 1) * devices, q * LANES : (q + 1) * LANES
            ]


def front_kernel(feats, tokens, w_atom, w_restype, w_pair, pair_in, mask, gain, weights, send, sides, wide):
    tok = pair_in.shape[0]
    width = pair_in.shape[2]
    devices = send.shape[0]
    starts, ends = tokens[:, 0:1], tokens[:, 1:2]
    counts, types = tokens[:, 2:3], tokens[:, 3:4]
    chunk = 512

    def pool(n, sums):
        at = pl.multiple_of(n * chunk, chunk)
        act = jnp.maximum(nn(feats[pl.ds(at, chunk), :], w_atom[...]), 0.0).astype(BF16)
        atoms = lax.broadcasted_iota(jnp.int32, (2 * tok, chunk), 1) + at
        owners = jnp.where((atoms >= starts) & (atoms < ends), 1.0, 0.0).astype(BF16)
        return sums + nn(owners, act)

    sums = lax.fori_loop(
        0, feats.shape[0] // chunk, pool, jnp.zeros((2 * tok, w_atom.shape[1]), F32)
    )
    kinds = lax.broadcasted_iota(jnp.int32, (2 * tok, w_restype.shape[0]), 1)
    embedded = nn(jnp.where(kinds == types, 1.0, 0.0).astype(BF16), w_restype[...])
    single = (sums / counts.astype(F32) + embedded).astype(BF16)
    sides[:tok, :] = nn(single[:tok], w_pair[:, :width]).astype(BF16)
    sides[tok:, :] = nn(single[tok:], w_pair[:, width:]).astype(BF16)
    right = sides[tok:, :].astype(F32)

    def group(g, carry):
        at = pl.multiple_of(g * 8, 8)
        left = sides[pl.ds(at, 8), :].astype(F32)
        block = pair_in[pl.ds(at, 8)].astype(F32) + left[:, None, :] + right[None]
        block = block.astype(BF16).astype(F32).reshape(8 * tok, width)
        normed = norm(block, gain[...], -1).astype(BF16)
        send_group(g, normed, weights[...], mask[pl.ds(g, 1), :], wide, devices)
        return carry

    lax.fori_loop(0, tok // 8, group, 0)
    send[...] = wide[...].astype(BF16).reshape(send.shape)


def first_gate_kernel(pair_in, sides, gain, w_gate, pair, gate):
    tok = pair_in.shape[0]
    width = pair_in.shape[2]
    left = sides[:tok, :].astype(F32)

    def group(g, carry):
        at = pl.multiple_of(g * 8, 8)
        right = sides[pl.ds(tok + at, 8), :].astype(F32)
        block = pair_in[pl.ds(at, 8)].astype(F32) + left[None] + right[:, None, :]
        block = block.astype(BF16).reshape(8 * tok, width)
        rows = pl.ds(pl.multiple_of(g * 8 * tok, 8 * tok), 8 * tok)
        pair[rows, :] = block
        normed = norm(block.astype(F32), gain[...], -1).astype(BF16)
        gate[rows, :] = sigmoid(nn(normed, w_gate[...]))
        return carry

    lax.fori_loop(0, tok // 8, group, 0)


def gate_kernel(pair, gain, w_gate, gate):
    span = 384

    def group(g, carry):
        rows = pl.ds(pl.multiple_of(g * span, span), span)
        normed = norm(pair[rows, :].astype(F32), gain[...], -1).astype(BF16)
        gate[rows, :] = sigmoid(nn(normed, w_gate[...]))
        return carry

    lax.fori_loop(0, pair.shape[0] // span, group, 0)


def windows_of(parts, tok):
    lane = lax.broadcasted_iota(jnp.int32, parts[0].shape, 1)
    out = []
    for w in range(len(parts) * LANES // tok):
        q, off = divmod(w * tok, LANES)
        value = parts[q] if off == 0 else pltpu.roll(parts[q], LANES - off, 1)
        if off + tok > LANES:
            value = jnp.where(lane < LANES - off, value, pltpu.roll(parts[q + 1], LANES - off, 1))
        out.append(value)
    return out


def triangle_kernel(tok, blocks, x, out, xf, lhs, rhs, moved, of):
    devices = x.shape[0]
    share = out.shape[1] * LANES // (tok * tok)
    parts = 3
    groups = tok // 8
    kinds = 2 * share
    side_len = blocks * tok
    xf[...] = x[...].astype(F32).reshape(xf.shape)
    lane = lax.broadcasted_iota(jnp.int32, (tok, LANES), 1)
    per_block = devices // blocks * x.shape[1]

    def unpack(b, carry):
        cols = pl.ds(pl.multiple_of(b * LANES, LANES), LANES)
        for kind in range(kinds):
            side, e = divmod(kind, share)
            tiles = [
                xf[pl.ds(b * per_block + kind * parts + q, tok, stride=kinds * parts), :]
                for q in range(parts)
            ]
            for w, value in enumerate(windows_of(tiles, tok)):
                if side == 0:
                    rhs[e, w * tok : (w + 1) * tok, cols] = jnp.where(lane < tok, value, 0.0).astype(BF16)
                else:
                    lhs[e, w * tok : (w + 1) * tok, cols] = value.astype(BF16)
        return carry

    lax.fori_loop(0, blocks, unpack, 0)

    source = lax.broadcasted_iota(jnp.int32, (side_len, blocks * LANES), 0)
    target = lax.broadcasted_iota(jnp.int32, (side_len, blocks * LANES), 1)
    block, spot = target // LANES, target % LANES
    wanted = (spot % 8) * tok + block * groups + spot // 8
    place = jnp.where((source == wanted) & (spot < tok), 1.0, 0.0).astype(BF16)
    for e in range(share):
        product = nt(lhs[e], rhs[e]).astype(BF16)
        moved[e] = nn(product, place)

    def pack(b, carry):
        cols = pl.ds(pl.multiple_of(b * LANES, LANES), LANES)
        for e in range(share):
            tiles = [None] * parts
            for w in range(8):
                value = moved[e, w * tok : (w + 1) * tok, cols]
                q, off = divmod(w * tok, LANES)
                first = value if off == 0 else pltpu.roll(value, off, 1)
                tiles[q] = first if tiles[q] is None else jnp.where(lane >= off, first, tiles[q])
                if off + tok > LANES:
                    tiles[q + 1] = first
            for q in range(parts):
                at = b * blocks * out.shape[1] + e * parts + q
                of[pl.ds(at, tok, stride=share * parts), :] = tiles[q]
        return carry

    lax.fori_loop(0, blocks, pack, 0)
    out[...] = of[...].astype(BF16).reshape(out.shape)


def updated_group(g, tri, wide, gain, w_out, pair, gate, rows):
    devices, each = tri.shape[0], tri.shape[1]
    parts = 3
    share = w_out.shape[0] // devices
    changes = []
    for q in range(parts):
        tile = jnp.concatenate(
            [
                wide[pl.ds(g * share * parts + e * parts + q, devices, stride=each), :]
                for e in range(share)
            ],
            axis=0,
        )
        normed = norm(tile, gain[...], 0).astype(BF16)
        changes.append(tn(normed, w_out[...]))
    change = jnp.concatenate(changes, axis=0)
    return (pair[rows, :].astype(F32) + gate[rows, :] * change).astype(BF16)


def middle_kernel(tri, pair, gate, gain_out, w_out, mask, gain, weights, send, pair_new, thin, wide):
    devices = tri.shape[0]
    thin[...] = tri[...].astype(F32).reshape(thin.shape)
    span = 384

    def group(g, carry):
        rows = pl.ds(pl.multiple_of(g * span, span), span)
        block = updated_group(g, tri, thin, gain_out, w_out, pair, gate, rows)
        pair_new[rows, :] = block
        normed = norm(block.astype(F32), gain[...], -1).astype(BF16)
        send_group(g, normed, weights[...], mask[pl.ds(g, 1), :], wide, devices)
        return carry

    lax.fori_loop(0, pair.shape[0] // span, group, 0)
    send[...] = wide[...].astype(BF16).reshape(send.shape)


def last_kernel(tri, pair, gate, gain_out, w_out, gain, w_up, d_pair, grad, hidden, pair_new, thin, total):
    thin[...] = tri[...].astype(F32).reshape(thin.shape)
    total[...] = jnp.zeros_like(total)
    span = 384
    expand = total.shape[0]

    def group(g, carry):
        rows = pl.ds(pl.multiple_of(g * span, span), span)
        block = updated_group(g, tri, thin, gain_out, w_out, pair, gate, rows)
        pair_new[rows, :] = block
        normed = norm(block.astype(F32), gain[...], -1).astype(BF16)
        up = nt(w_up[...], normed)
        first = up[:expand]
        units = (first * sigmoid(first) * up[expand:]).astype(BF16)
        hidden[g] = units
        total[...] += nn(units, d_pair[rows, :])
        return carry

    lax.fori_loop(0, pair.shape[0] // span, group, 0)
    grad[...] = total[...]


def down_kernel(hidden, pair, w_down, out, wide):
    tok = out.shape[0]
    span = hidden.shape[2]
    each = span // tok

    def group(g, carry):
        rows = pl.ds(pl.multiple_of(g * span, span), span)
        result = pair[rows, :].astype(F32) + tn(hidden[g], w_down[...])
        for n in range(each):
            wide[pl.ds(g * each + n, tok, stride=tok), :] = result[n * tok : (n + 1) * tok]
        return carry

    lax.fori_loop(0, hidden.shape[0], group, 0)
    out[...] = wide[...].astype(BF16).reshape(out.shape)


def call(kernel, outs, scratch, name, cost, *args):
    return pl.pallas_call(
        kernel,
        out_shape=outs,
        in_specs=[pl.BlockSpec(memory_space=pltpu.VMEM)] * len(args),
        out_specs=jax.tree.map(lambda _: pl.BlockSpec(memory_space=pltpu.VMEM), outs),
        scratch_shapes=scratch,
        compiler_params=PARAMS,
        name=name,
        cost_estimate=pl.CostEstimate(flops=cost, bytes_accessed=4 * 2**20, transcendentals=10**6),
    )(*args)


def local(
    atom_feats,
    atom_token,
    atom_counts,
    restype,
    pair_in,
    pair_mask,
    w_atom,
    w_restype,
    w_pair,
    ln_tri,
    w_tri_in,
    ln_tri_out,
    w_tri_out,
    ln_trans,
    w_up,
    w_down,
    d_pair,
):
    n_row, n_col = lax.axis_size("row"), lax.axis_size("col")
    devices = n_row * n_col
    tok = pair_in.shape[1]
    width = pair_in.shape[3]
    inner = w_tri_out.shape[1]
    expand = w_down.shape[0]
    share = inner // devices
    count = tok * tok
    groups = tok // 8
    span = 8 * tok
    row_start = lax.axis_index("row") * tok
    col_start = lax.axis_index("col") * tok

    feats = exchange(jnp.broadcast_to(atom_feats, (devices,) + atom_feats.shape[1:]), ("row", "col"))
    feats = feats.reshape(-1, feats.shape[-1])

    ends = jnp.cumsum(atom_counts[0])
    table = jnp.stack([ends - atom_counts[0], ends, atom_counts[0], restype[0]], axis=1)
    tokens = jnp.concatenate(
        [lax.dynamic_slice_in_dim(table, start, tok, 0) for start in (row_start, col_start)], 0
    )
    valid = pair_mask[0].astype(F32)
    masks = [valid.reshape(groups, span), valid.T.reshape(groups, span)]
    turned_in = pair_in[0].transpose(1, 0, 2)
    turned_grad = d_pair[0].transpose(1, 0, 2).reshape(count, width)
    w_sides = (
        w_tri_in[:, :, : 4 * inner]
        .reshape(2, width, 2, 2, devices, share)
        .transpose(0, 3, 2, 5, 4, 1)
        .reshape(2, 4 * inner, width)
    )
    w_gates = w_tri_in[:, :, 4 * inner :]
    w_up_turned = w_up.T

    def by_owner(values, update):
        if update == 0:
            order = values.reshape((n_col, n_row, share) + values.shape[1:]).swapaxes(0, 1)
        else:
            order = values.reshape((n_row, n_col, share) + values.shape[1:])
        return jnp.moveaxis(order, 2, 0).reshape(values.shape)

    w_outs = [by_owner(w_tri_out[u], u) for u in range(2)]
    gains_out = [by_owner(ln_tri_out[u][:, None], u) for u in range(2)]
    gains = [ln_tri[0:1], ln_tri[1:2], ln_trans[None]]

    shape = jax.ShapeDtypeStruct
    rows_out = 2 * share * count // LANES
    rows_back = share * count // LANES
    send_shape = shape((devices, rows_out, LANES), BF16)
    back_shape = shape((devices, rows_back, LANES), BF16)
    wide = pltpu.VMEM((devices * rows_out, LANES), F32)
    thin = pltpu.VMEM((devices * rows_back, LANES), F32)
    flat = shape((count, width), BF16)
    flat_wide = shape((count, width), F32)
    cost = 400 * 10**6

    def triangle(value):
        blocks = n_row
        return call(
            functools.partial(triangle_kernel, tok, blocks),
            back_shape,
            [
                wide,
                pltpu.VMEM((share, blocks * tok, blocks * LANES), BF16),
                pltpu.VMEM((share, blocks * tok, blocks * LANES), BF16),
                pltpu.VMEM((share, blocks * tok, blocks * LANES), F32),
                thin,
            ],
            "triangle",
            cost,
            value,
        )

    send, sides = call(
        front_kernel,
        (send_shape, shape((2 * tok, width), BF16)),
        [wide],
        "front",
        cost,
        feats,
        tokens,
        w_atom,
        w_restype,
        w_pair,
        pair_in[0],
        masks[0],
        gains[0],
        w_sides[0],
    )
    arrived = exchange(send, ("col", "row"))
    pair, gate = call(
        first_gate_kernel,
        (flat, flat_wide),
        [],
        "first_gate",
        cost,
        turned_in,
        sides,
        gains[0],
        w_gates[0],
    )
    tri = exchange(triangle(arrived), ("row", "col"))
    send, pair = call(
        middle_kernel,
        (send_shape, flat),
        [thin, wide],
        "middle",
        cost,
        tri,
        pair,
        gate,
        gains_out[0],
        w_outs[0],
        masks[1],
        gains[1],
        w_sides[1],
    )
    arrived = exchange(send, ("row", "col"))
    gate = call(gate_kernel, flat_wide, [], "gate", cost, pair, gains[1], w_gates[1])
    tri = exchange(triangle(arrived), ("row", "col"))
    grad, hidden, pair = call(
        last_kernel,
        (shape((expand, width), F32), shape((groups, expand, span), BF16), flat),
        [thin, pltpu.VMEM((expand, width), F32)],
        "last",
        2 * cost,
        tri,
        pair,
        gate,
        gains_out[1],
        w_outs[1],
        gains[2],
        w_up_turned,
        turned_grad,
    )
    everyone = devices * lax.axis_size("rep")
    grad = exchange(grad.reshape(everyone, expand // everyone, width), ("row", "col", "rep"))
    result = call(
        down_kernel,
        shape((tok, tok, width), BF16),
        [pltpu.VMEM((count, width), F32)],
        "down",
        cost,
        hidden,
        pair,
        w_down,
    )
    return (result[None], jnp.sum(grad, axis=0))


def solution(mesh):
    return jax.shard_map(
        local,
        mesh=mesh,
        in_specs=(
            P("rep", ("row", "col"), None),
            P("rep", ("row", "col")),
            P("rep", None),
            P("rep", None),
            P("rep", "row", "col", None),
            P("rep", "row", "col"),
            P(),
            P(),
            P(),
            P(),
            P(),
            P(),
            P(),
            P(),
            P(),
            P(),
            P("rep", "row", "col", None),
        ),
        out_specs=(P("rep", "row", "col", None), P(("row", "col", "rep"), None)),
        check_vma=False,
    )
```

profile of v0, /device:TPU:1, one launch (start us, length us, event | category | flops | bytes accessed | tf_op | source)
XLA Modules:
  0.0 165.7 jit_solution(4531017641638522376)
XLA Ops:
  0.7 1.7 %broadcast_in_dim.14 = bf16[64,48,128]{2,1,0:T(8,128)(2,1)} broadcast(bf16[48,128]{1,0:T(8,128)(2,1)} %bitcast.77), dimensions={1,2} | broadcast | bytes 798720 | tf_op jit(solution)/shard_map/broadcast_in_dim | solution.py:313
  2.4 10.5 %all-to-all-start = ((bf16[64,48,128]{2,1,0:T(8,128)(2,1)}), bf16[64,48,128]{2,1,0:T(8,128)(2,1)S(1)}, u32[]{:S(2)}, u32[]{:S(2)}) async-start(bf16[64,48,128]{2,1,0:T(8,128)(2,1)} %broadcast_in_dim.14), calls=%async_computation | async-start | bytes 1572864 | tf_op jit(solution)/shard_map/all_to_all | solution.py:39
  13.0 0.3 reduce-window.9
  14.0 0.2 copy.65
  14.2 0.2 fusion
  14.4 13.6 %all-to-all-done = bf16[64,48,128]{2,1,0:T(8,128)(2,1)S(1)} async-done(((bf16[64,48,128]{2,1,0:T(8,128)(2,1)}), bf16[64,48,128]{2,1,0:T(8,128)(2,1)S(1)}, u32[]{:S(2)}, u32[]{:S(2)}) %all-to-all-start) | async-done | bytes 786464 | tf_op jit(solution)/shard_map/all_to_all | solution.py:39
  28.0 7.3 %front.1 = (bf16[64,72,128]{2,1,0:T(8,128)(2,1)}, bf16[96,128]{1,0:T(8,128)(2,1)S(1)}) custom-call(bf16[3072,128]{1,0:T(8,128)(2,1)S(1)} %bitcast.60, s32[96,4]{1,0:T(8,128)S(1)} %copy.52.tokens, bf16[128,384]{1,0:T(8,128)(2,1)S(1)} %copy-done.12, bf16[32,384]{1,0:T(8,128)(2,1)S(1)} %copy-done.13, bf16[384,256]{1,0:T(8,128)(2,1)S(1)} %copy-done.11, ...), custom_call_target="tpu_custom_call" | custom-call | flops 400000000 | bytes 4194304 | tf_op jit(solution)/shard_map/front/pallas_call | solution.py:269
  35.4 4.5 %all-to-all-start.1 = ((bf16[64,72,128]{2,1,0:T(8,128)(2,1)}), bf16[64,72,128]{2,1,0:T(8,128)(2,1)S(1)}, u32[]{:S(2)}, u32[]{:S(2)}) async-start(bf16[64,72,128]{2,1,0:T(8,128)(2,1)} %get-tuple-element.11), calls=%async_computation.1 | async-start | bytes 2359296 | tf_op jit(solution)/shard_map/all_to_all | solution.py:39
  40.0 19.4 %all-to-all-done.1.x = bf16[64,72,128]{2,1,0:T(8,128)(2,1)S(1)} async-done(((bf16[64,72,128]{2,1,0:T(8,128)(2,1)}), bf16[64,72,128]{2,1,0:T(8,128)(2,1)S(1)}, u32[]{:S(2)}, u32[]{:S(2)}) %all-to-all-start.1) | async-done | bytes 1179680 | tf_op jit(solution)/shard_map/all_to_all | solution.py:39
  59.4 5.9 %triangle.2 = bf16[64,36,128]{2,1,0:T(8,128)(2,1)} custom-call(bf16[64,72,128]{2,1,0:T(8,128)(2,1)S(1)} %all-to-all-done.1.x), custom_call_target="tpu_custom_call" | custom-call | flops 400000000 | bytes 4194304 | tf_op jit(solution)/shard_map/triangle/pallas_call | solution.py:269
  65.3 4.9 %all-to-all-start.2 = ((bf16[64,36,128]{2,1,0:T(8,128)(2,1)}), bf16[64,36,128]{2,1,0:T(8,128)(2,1)S(1)}, u32[]{:S(2)}, u32[]{:S(2)}) async-start(bf16[64,36,128]{2,1,0:T(8,128)(2,1)} %triangle.2), calls=%async_computation.2 | async-start | bytes 1310720 | tf_op jit(solution)/shard_map/all_to_all | solution.py:39
  70.9 2.1 %first_gate.1 = (bf16[2304,128]{1,0:T(8,128)(2,1)S(1)}, f32[2304,128]{1,0:T(8,128)S(1)}) custom-call(bf16[48,48,128]{2,1,0:T(8,128)(2,1)S(1)} %bitcast.62, bf16[96,128]{1,0:T(8,128)(2,1)S(1)} %get-tuple-element.12.sides, f32[1,128]{1,0:T(1,128)S(1)} %get-tuple-element.35.gain, bf16[128,128]{1,0:T(8,128)(2,1)S(1)} %get-tuple-element.25.w_gate), custom_call_target="tpu_custom_call" | custom-call | flops 400000000 | bytes 4194304 | tf_op jit(solution)/shard_map/first_gate/pallas_call | solution.py:269
  73.0 11.0 %all-to-all-done.2.tri = bf16[64,36,128]{2,1,0:T(8,128)(2,1)S(1)} async-done(((bf16[64,36,128]{2,1,0:T(8,128)(2,1)}), bf16[64,36,128]{2,1,0:T(8,128)(2,1)S(1)}, u32[]{:S(2)}, u32[]{:S(2)}) %all-to-all-start.2) | async-done | bytes 589856 | tf_op jit(solution)/shard_map/all_to_all | solution.py:39
  84.0 4.9 %middle.1 = (bf16[64,72,128]{2,1,0:T(8,128)(2,1)S(1)}, bf16[2304,128]{1,0:T(8,128)(2,1)S(1)}) custom-call(bf16[64,36,128]{2,1,0:T(8,128)(2,1)S(1)} %all-to-all-done.2.tri, bf16[2304,128]{1,0:T(8,128)(2,1)S(1)} %get-tuple-element.13.pair, f32[2304,128]{1,0:T(8,128)S(1)} %get-tuple-element.14.gate, f32[128,1]{1,0:T(8,128)S(1)} %reshape.104.gain_out, ...), custom_call_target="tpu_custom_call" | custom-call | flops 400000000 | bytes 4194304 | tf_op jit(solution)/shard_map/middle/pallas_call | solution.py:269
  88.9 23.4 %all_to_all.30.x = bf16[64,72,128]{2,1,0:T(8,128)(2,1)S(1)} all-to-all(bf16[64,72,128]{2,1,0:T(8,128)(2,1)S(1)} %get-tuple-element.15), channel_id=1, replica_groups=mesh['row'=8,'col'=8,'rep'=2] {'row','col'}, dimensions={0} | all-to-all | bytes 2359296 | tf_op jit(solution)/shard_map/all_to_all | solution.py:39
  112.3 5.9 %triangle.3 = bf16[64,36,128]{2,1,0:T(8,128)(2,1)} custom-call(bf16[64,72,128]{2,1,0:T(8,128)(2,1)S(1)} %all_to_all.30.x), custom_call_target="tpu_custom_call" | custom-call | flops 400000000 | bytes 4194304 | tf_op jit(solution)/shard_map/triangle/pallas_call | solution.py:269
  118.3 4.7 %all-to-all-start.4 = ((bf16[64,36,128]{2,1,0:T(8,128)(2,1)}), bf16[64,36,128]{2,1,0:T(8,128)(2,1)S(1)}, u32[]{:S(2)}, u32[]{:S(2)}) async-start(bf16[64,36,128]{2,1,0:T(8,128)(2,1)} %triangle.3), calls=%async_computation.4 | async-start | bytes 1310720 | tf_op jit(solution)/shard_map/all_to_all | solution.py:39
  123.5 1.0 copy.62
  124.5 2.1 %gate.1 = f32[2304,128]{1,0:T(8,128)S(1)} custom-call(bf16[2304,128]{1,0:T(8,128)(2,1)S(1)} %get-tuple-element.16.pair, f32[1,128]{1,0:T(1,128)S(1)} %get-tuple-element.34.gain, bf16[128,128]{1,0:T(8,128)(2,1)S(1)} %get-tuple-element.24.w_gate), custom_call_target="tpu_custom_call" | custom-call | flops 400000000 | bytes 4194304 | tf_op jit(solution)/shard_map/gate/pallas_call | solution.py:269
  126.5 1.0 copy-done.1
  127.6 9.2 %all-to-all-done.4.tri = bf16[64,36,128]{2,1,0:T(8,128)(2,1)S(1)} async-done(((bf16[64,36,128]{2,1,0:T(8,128)(2,1)}), bf16[64,36,128]{2,1,0:T(8,128)(2,1)S(1)}, u32[]{:S(2)}, u32[]{:S(2)}) %all-to-all-start.4) | async-done | bytes 589856 | tf_op jit(solution)/shard_map/all_to_all | solution.py:39
  136.8 1.1 copy-done
  137.8 1.3 copy-done.2
  139.1 1.1 copy-done.7
  140.2 6.2 %last.1 = (f32[512,128]{1,0:T(8,128)S(1)}, bf16[6,512,384]{2,1,0:T(8,128)(2,1)S(1)}, bf16[2304,128]{1,0:T(8,128)(2,1)S(1)}) custom-call(bf16[64,36,128]{2,1,0:T(8,128)(2,1)S(1)} %all-to-all-done.4.tri, bf16[2304,128]{1,0:T(8,128)(2,1)S(1)} %copy-done.7, f32[2304,128]{1,0:T(8,128)S(1)} %copy-done.2, f32[128,1]{1,0:T(8,128)S(1)} %reshape.105.gain_out, ...), custom_call_target="tpu_custom_call" | custom-call | flops 800000000 | bytes 4194304 | tf_op jit(solution)/shard_map/last/pallas_call | solution.py:269
  146.4 0.8 copy-done.3
  147.2 0.7 copy-done.8
  147.9 6.0 %all-to-all-start.5 = ((f32[128,4,128]{2,1,0:T(4,128)}), f32[128,4,128]{2,1,0:T(4,128)S(1)}, u32[]{:S(2)}, u32[]{:S(2)}) async-start(f32[128,4,128]{2,1,0:T(4,128)} %bitcast.64), calls=%async_computation.5 | async-start | bytes 524288 | tf_op jit(solution)/shard_map/all_to_all | solution.py:39
  153.9 1.1 copy-done.4
  155.0 2.8 %down.1 = bf16[48,48,128]{2,1,0:T(8,128)(2,1)} custom-call(bf16[6,512,384]{2,1,0:T(8,128)(2,1)S(1)} %get-tuple-element.17.hidden, bf16[2304,128]{1,0:T(8,128)(2,1)S(1)} %copy-done.4, bf16[512,128]{1,0:T(8,128)(2,1)S(1)} %copy-done.9), custom_call_target="tpu_custom_call" | custom-call | flops 400000000 | bytes 4194304 | tf_op jit(solution)/shard_map/down/pallas_call | solution.py:269
  157.8 7.2 %all-to-all-done.5 = f32[128,4,128]{2,1,0:T(4,128)S(1)} async-done(((f32[128,4,128]{2,1,0:T(4,128)}), f32[128,4,128]{2,1,0:T(4,128)S(1)}, u32[]{:S(2)}, u32[]{:S(2)}) %all-to-all-start.5) | async-done | bytes 262176 | tf_op jit(solution)/shard_map/all_to_all | solution.py:39
  165.0 0.7 reduce_sum.9
  (71 shorter events, 2.0 us)
Async XLA Ops:
  0.6 12.3 %copy-start.19 = (s32[1,384]{1,0:T(1,128)S(1)}, s32[1,384]{1,0:T(1,128)}, u32[]{:S(2)}) copy-start(s32[1,384]{1,0:T(1,128)} %param.18) | copy-start | bytes 4612
  0.6 13.0 %copy-start.20 = (s32[1,384]{1,0:T(1,128)S(1)}, s32[1,384]{1,0:T(1,128)}, u32[]{:S(2)}) copy-start(s32[1,384]{1,0:T(1,128)} %param.19) | copy-start | bytes 4612
  0.7 13.2 %copy-start.18 = (s32[1,48,48]{2,1,0:T(8,128)S(1)}, s32[1,48,48]{2,1,0:T(8,128)}, u32[]{:S(2)}) copy-start(s32[1,48,48]{2,1,0:T(8,128)} %param.21) | copy-start | bytes 27652
  2.4 11.6 %slice-start = ((bf16[2,128,640]{2,1,0:T(8,128)(2,1)}), bf16[2,128,512]{2,1,0:T(8,128)(2,1)S(1)}, s32[]{:S(2)}) async-start(bf16[2,128,640]{2,1,0:T(8,128)(2,1)} %param.26), calls=%async_computation.6 | async-start | bytes 524288 | tf_op jit(solution)/shard_map/slice | solution.py:326
  2.4 25.6 %all-to-all-start = ((bf16[64,48,128]{2,1,0:T(8,128)(2,1)}), bf16[64,48,128]{2,1,0:T(8,128)(2,1)S(1)}, u32[]{:S(2)}, u32[]{:S(2)}) async-start(bf16[64,48,128]{2,1,0:T(8,128)(2,1)} %broadcast_in_dim.14), calls=%async_computation | async-start | bytes 1572864 | tf_op jit(solution)/shard_map/all_to_all | solution.py:39
  12.9 1.5 copy-start.21
  12.9 15.1 %copy-start.5 = (bf16[1,48,48,128]{3,2,1,0:T(8,128)(2,1)S(1)}, bf16[1,48,48,128]{3,2,1,0:T(8,128)(2,1)}, u32[]{:S(2)}) copy-start(bf16[1,48,48,128]{3,2,1,0:T(8,128)(2,1)} %param.20) | copy-start | bytes 1769476
  12.9 15.1 %copy-start.11 = (bf16[384,256]{1,0:T(8,128)(2,1)S(1)}, bf16[384,256]{1,0:T(8,128)(2,1)}, u32[]{:S(2)}) copy-start(bf16[384,256]{1,0:T(8,128)(2,1)} %w_pair.1) | copy-start | bytes 589828
  12.9 15.1 %copy-start.12 = (bf16[128,384]{1,0:T(8,128)(2,1)S(1)}, bf16[128,384]{1,0:T(8,128)(2,1)}, u32[]{:S(2)}) copy-start(bf16[128,384]{1,0:T(8,128)(2,1)} %w_atom.1) | copy-start | bytes 294916
  12.9 15.1 %copy-start.13 = (bf16[32,384]{1,0:T(8,128)(2,1)S(1)}, bf16[32,384]{1,0:T(8,128)(2,1)}, u32[]{:S(2)}) copy-start(bf16[32,384]{1,0:T(8,128)(2,1)} %w_restype.1) | copy-start | bytes 73732
  35.4 24.0 %all-to-all-start.1 = ((bf16[64,72,128]{2,1,0:T(8,128)(2,1)}), bf16[64,72,128]{2,1,0:T(8,128)(2,1)S(1)}, u32[]{:S(2)}, u32[]{:S(2)}) async-start(bf16[64,72,128]{2,1,0:T(8,128)(2,1)} %get-tuple-element.11), calls=%async_computation.1 | async-start | bytes 2359296 | tf_op jit(solution)/shard_map/all_to_all | solution.py:39
  40.0 30.2 %copy-start.22 = (f32[2,128]{1,0:T(2,128)S(1)}, f32[2,128]{1,0:T(2,128)}, u32[]{:S(2)}) copy-start(f32[2,128]{1,0:T(2,128)} %param.27) | copy-start | bytes 3076
  65.3 5.5 %copy-start.17 = (bf16[2,128,128]{2,1,0:T(8,128)(2,1)S(1)}, bf16[2,128,128]{2,1,0:T(8,128)(2,1)}, u32[]{:S(2)}) copy-start(bf16[2,128,128]{2,1,0:T(8,128)(2,1)} %param.28) | copy-start | bytes 196612
  65.3 5.5 %copy-start.14 = (bf16[2,128,640]{2,1,0:T(8,128)(2,1)S(1)}, bf16[2,128,640]{2,1,0:T(8,128)(2,1)}, u32[]{:S(2)}) copy-start(bf16[2,128,640]{2,1,0:T(8,128)(2,1)} %param.26) | copy-start | bytes 983044
  65.3 18.7 %all-to-all-start.2 = ((bf16[64,36,128]{2,1,0:T(8,128)(2,1)}), bf16[64,36,128]{2,1,0:T(8,128)(2,1)S(1)}, u32[]{:S(2)}, u32[]{:S(2)}) async-start(bf16[64,36,128]{2,1,0:T(8,128)(2,1)} %triangle.2), calls=%async_computation.2 | async-start | bytes 1310720 | tf_op jit(solution)/shard_map/all_to_all | solution.py:39
  88.9 35.6 %copy-start.6 = (bf16[2304,128]{1,0:T(8,128)(2,1)}, bf16[2304,128]{1,0:T(8,128)(2,1)S(1)}, u32[]{:S(2)}) copy-start(bf16[2304,128]{1,0:T(8,128)(2,1)S(1)} %get-tuple-element.16.pair) | copy-start | bytes 1769476
  118.3 5.0 %copy-start.16 = (bf16[128,1024]{1,0:T(8,128)(2,1)S(1)}, bf16[128,1024]{1,0:T(8,128)(2,1)}, u32[]{:S(2)}) copy-start(bf16[128,1024]{1,0:T(8,128)(2,1)} %param.30) | copy-start | bytes 786436
  118.3 5.2 %copy-start.15 = (bf16[1,48,48,128]{3,2,1,0:T(8,128)(2,1)S(1)}, bf16[1,48,48,128]{3,2,1,0:T(8,128)(2,1)}, u32[]{:S(2)}) copy-start(bf16[1,48,48,128]{3,2,1,0:T(8,128)(2,1)} %param.32) | copy-start | bytes 1769476
  118.3 18.5 %all-to-all-start.4 = ((bf16[64,36,128]{2,1,0:T(8,128)(2,1)}), bf16[64,36,128]{2,1,0:T(8,128)(2,1)S(1)}, u32[]{:S(2)}, u32[]{:S(2)}) async-start(bf16[64,36,128]{2,1,0:T(8,128)(2,1)} %triangle.3), calls=%async_computation.4 | async-start | bytes 1310720 | tf_op jit(solution)/shard_map/all_to_all | solution.py:39
  124.5 12.3 %copy-start.10 = (f32[128]{0:T(128)S(1)}, f32[128]{0:T(128)}, u32[]{:S(2)}) copy-start(f32[128]{0:T(128)} %param.29) | copy-start | bytes 1540
  126.5 1.1 copy-start.1
  136.8 1.1 copy-start
  137.8 1.3 copy-start.2
  139.1 1.1 copy-start.7
  140.2 13.7 %copy-start.9 = (bf16[512,128]{1,0:T(8,128)(2,1)S(1)}, bf16[512,128]{1,0:T(8,128)(2,1)}, u32[]{:S(2)}) copy-start(bf16[512,128]{1,0:T(8,128)(2,1)} %w_down.1) | copy-start | bytes 393220
  146.3 0.8 copy-start.3
  147.2 0.7 copy-start.8
  147.9 17.1 %all-to-all-start.5 = ((f32[128,4,128]{2,1,0:T(4,128)}), f32[128,4,128]{2,1,0:T(4,128)S(1)}, u32[]{:S(2)}, u32[]{:S(2)}) async-start(f32[128,4,128]{2,1,0:T(4,128)} %bitcast.64), calls=%async_computation.5 | async-start | bytes 524288 | tf_op jit(solution)/shard_map/all_to_all | solution.py:39
  153.9 1.1 copy-start.4
where the time goes:
time: 167 us; the launch traced here: 166 us
  waiting for transfers between devices  60.4 us (36%)
  Pallas kernels  37.2 us (22%)
  starting transfers between devices  30.6 us (18%)
  blocking collectives  23.4 us (14%)
  local copies, waits for them, and re-layouts  11.9 us (7%)
    all_to_all x5, waiting for transfers between devices, exchange(): return lax.all_to_all(value, axes, 0, 0, tiled=True)  60.4 us
    pallas_call x8, Pallas kernels, call(): pl.pallas_call(kernel, out_shape=outs, in_specs=[pl.BlockSpec(memory_spac...  37.2 us
    all_to_all x5, starting transfers between devices, exchange(): return lax.all_to_all(value, axes, 0, 0, tiled=True)  30.6 us
    all_to_all x1, blocking collectives, exchange(): return lax.all_to_all(value, axes, 0, 0, tiled=True)  23.4 us
    unnamed x49, local copies, waits for them, and re-layouts  7.59 us
  transfers between devices with their start and end apart: 5, of which 5 were waited for; matrix products, arithmetic and copies ran while one was open for 2% of the time, Pallas kernels for 4%

commit v1 on v0

v1 whole, which is shorter than its diff:
```python
import functools

import jax
import jax.numpy as jnp
from jax import lax
from jax.experimental import pallas as pl
from jax.experimental.pallas import tpu as pltpu
from jax.sharding import PartitionSpec as P

F32, BF16 = jnp.float32, jnp.bfloat16
LANES = 128
UNROLL = 6
PARAMS = pltpu.CompilerParams(vmem_limit_bytes=20 * 2**20)


def nt(a, b):
    return lax.dot_general(a, b, (((1,), (1,)), ((), ())), preferred_element_type=F32)


def nn(a, b):
    return lax.dot_general(a, b, (((1,), (0,)), ((), ())), preferred_element_type=F32)


def norm(values, scales, axis):
    average = jnp.mean(values, axis=axis, keepdims=True)
    centred = values - average
    variance = jnp.mean(centred * centred, axis=axis, keepdims=True)
    return centred * lax.rsqrt(variance + 1e-05) * scales


def sigmoid(x):
    return jax.nn.sigmoid(x)


def exchange(value, axes):
    return lax.all_to_all(value, axes, 0, 0, tiled=True)


def send_group(g, normed, weights, mask_row, wide, devices):
    proj = nn(weights, normed)
    half = proj.shape[0] // 2
    sides = sigmoid(proj[:half]) * proj[half:] * mask_row
    rows = wide.shape[0] // devices
    parts = sides.shape[1] // LANES
    kinds = half // devices
    for kind in range(kinds):
        for q in range(parts):
            wide[pl.ds((g * kinds + kind) * parts + q, devices, stride=rows), :] = sides[
                kind * devices : (kind + 1) * devices, q * LANES : (q + 1) * LANES
            ]


def spread_kernel(value, out, copies, sems):
    several = copies.shape[0]
    copies[...] = jnp.broadcast_to(value[...], copies.shape)
    moves = [
        pltpu.make_async_copy(copies, out.at[pl.ds(n * several, several)], sems.at[n])
        for n in range(out.shape[0] // several)
    ]
    for move in moves:
        move.start()
    for move in moves:
        move.wait()


def prepare_kernel(place, pair_in, counts, types, plain, tokens, bounds, wide, made, sem):
    tok, width = pair_in.shape[0], pair_in.shape[2]
    span = 8 * tok
    wide[...] = pair_in[...].astype(F32).reshape(wide.shape)

    def turn(g, carry):
        rows = pl.ds(pl.multiple_of(g * span, span), span)
        made[g] = wide[rows, :].T.astype(BF16)
        return carry

    lax.fori_loop(0, tok // 8, turn, 0)
    move = pltpu.make_async_copy(made, plain, sem)
    move.start()
    shape = (2 * tok, counts.shape[1])
    slot = lax.broadcasted_iota(jnp.int32, shape, 0)
    mine = jnp.where(slot < tok, place[0] * tok + slot, place[1] * tok + slot - tok)
    token = lax.broadcasted_iota(jnp.int32, shape, 1)
    numbers = jnp.broadcast_to(counts[...].astype(F32), shape)
    kinds = jnp.broadcast_to(types[...].astype(F32), shape)

    def total(wanted, values):
        return jnp.sum(jnp.where(wanted, values, 0.0), axis=1, keepdims=True)

    columns = [
        total(token < mine, numbers),
        total(token <= mine, numbers),
        total(token == mine, numbers),
        total(token == mine, kinds),
    ]
    lane = lax.broadcasted_iota(jnp.int32, tokens.shape, 1)
    table = jnp.zeros(tokens.shape, F32)
    for n, column in enumerate(columns):
        table = jnp.where(lane == n, column, table)
    tokens[...] = table.astype(jnp.int32)
    every = lax.broadcasted_iota(jnp.int32, counts.shape, 1)
    for k in range(2):
        first = place[k] * tok
        start = jnp.sum(jnp.where(every < first, counts[...], 0))
        bounds[2 * k] = start // 16 * 16
        bounds[2 * k + 1] = jnp.sum(jnp.where(every < first + tok, counts[...], 0))
    move.wait()


def turned_rows(g, source, tok):
    rows = [source[pl.ds(g * 8 + n, tok, stride=tok), :] for n in range(8)]
    return jnp.concatenate(rows, axis=0)


def turn_kernel(d_pair, out, wide, made, sem):
    tok = d_pair.shape[0]
    span = 8 * tok
    wide[...] = d_pair[...].astype(F32).reshape(wide.shape)

    def grads(g, carry):
        rows = pl.ds(pl.multiple_of(g * span, span), span)
        made[rows, :] = turned_rows(g, wide, tok).astype(BF16)
        return carry

    lax.fori_loop(0, tok // 8, grads, 0)
    move = pltpu.make_async_copy(made, out, sem)
    move.start()
    move.wait()


def added_sides(g, sides, tok, turned):
    shape = (2 * tok, 8 * tok)
    source = lax.broadcasted_iota(jnp.int32, shape, 0)
    token = lax.broadcasted_iota(jnp.int32, shape, 1)
    high, low = g * 8 + token // tok, token % tok
    left, right = (low, high) if turned else (high, low)
    wanted = (source == left) | (source == right + tok)
    return nn(sides, jnp.where(wanted, 1.0, 0.0).astype(BF16))


def front_kernel(bounds, feats, tokens, w_atom, w_restype, w_pair, plain, mask, gain, weights, send, sides, wide, pair_in, sem):
    groups, width, span = plain.shape
    tok = span // 8
    devices = send.shape[0]
    move = pltpu.make_async_copy(plain, pair_in, sem)
    move.start()
    chunk = 384
    last = feats.shape[0] - chunk

    def pool(n, sums):
        out = []
        for k in range(2):
            base = bounds[2 * k] + n * chunk
            at = pl.multiple_of(jnp.minimum(base, last), 16)
            act = jnp.maximum(nn(feats[pl.ds(at, chunk), :], w_atom[...]), 0.0).astype(BF16)
            atoms = lax.broadcasted_iota(jnp.int32, (tok, chunk), 1) + at
            starts = tokens[k * tok : (k + 1) * tok, 0:1]
            ends = tokens[k * tok : (k + 1) * tok, 1:2]
            mine = (atoms >= jnp.maximum(starts, base)) & (atoms < ends)
            out.append(sums[k] + nn(jnp.where(mine, 1.0, 0.0).astype(BF16), act))
        return tuple(out)

    steps = jnp.maximum(bounds[1] - bounds[0], bounds[3] - bounds[2])
    zero = jnp.zeros((tok, w_atom.shape[1]), F32)
    sums = lax.fori_loop(0, (steps + chunk - 1) // chunk, pool, (zero, zero))
    counts, types = tokens[:, 2:3], tokens[:, 3:4]
    kinds = lax.broadcasted_iota(jnp.int32, (2 * tok, w_restype.shape[0]), 1)
    embedded = nn(jnp.where(kinds == types, 1.0, 0.0).astype(BF16), w_restype[...])
    single = (jnp.concatenate(sums, 0) / counts.astype(F32) + embedded).astype(BF16)
    left = nn(single[:tok], w_pair[:, :width])
    right = nn(single[tok:], w_pair[:, width:])
    sides[...] = jnp.concatenate([left, right], 0).T.astype(BF16)
    move.wait()

    def group(g, carry):
        block = pair_in[g].astype(F32) + added_sides(g, sides[...], tok, False)
        normed = norm(block.astype(BF16).astype(F32), gain[...], 0).astype(BF16)
        send_group(g, normed, weights[...], mask[pl.ds(g, 1), :], wide, devices)
        return carry

    lax.fori_loop(0, groups, group, 0, unroll=UNROLL)
    send[...] = wide[...].astype(BF16).reshape(send.shape)


def first_gate_kernel(pair_in, sides, gain, w_gate, pair_out, gate_out, wide, pair, gate, sems):
    tok = pair_in.shape[0]
    wide[...] = pair_in[...].astype(F32).reshape(wide.shape)

    def group(g, carry):
        block = turned_rows(g, wide, tok).T + added_sides(g, sides[...], tok, True)
        block = block.astype(BF16)
        pair[g] = block
        normed = norm(block.astype(F32), gain[...], 0).astype(BF16)
        gate[g] = sigmoid(nn(w_gate[...], normed))
        return carry

    lax.fori_loop(0, tok // 8, group, 0)
    moves = [
        pltpu.make_async_copy(pair, pair_out, sems.at[0]),
        pltpu.make_async_copy(gate, gate_out, sems.at[1]),
    ]
    for move in moves:
        move.start()
    for move in moves:
        move.wait()


def windows_of(parts, tok):
    lane = lax.broadcasted_iota(jnp.int32, parts[0].shape, 1)
    out = []
    for w in range(len(parts) * LANES // tok):
        q, off = divmod(w * tok, LANES)
        value = parts[q] if off == 0 else pltpu.roll(parts[q], LANES - off, 1)
        if off + tok > LANES:
            value = jnp.where(lane < LANES - off, value, pltpu.roll(parts[q + 1], LANES - off, 1))
        out.append(value)
    return out


def triangle_kernel(tok, blocks, x, out, xf, lhs, rhs, moved, of):
    devices = x.shape[0]
    share = out.shape[1] * LANES // (tok * tok)
    parts = 3
    groups = tok // 8
    kinds = 2 * share
    side_len = blocks * tok
    xf[...] = x[...].astype(F32).reshape(xf.shape)
    lane = lax.broadcasted_iota(jnp.int32, (tok, LANES), 1)
    per_block = devices // blocks * x.shape[1]

    def unpack(b, carry):
        cols = pl.ds(pl.multiple_of(b * LANES, LANES), LANES)
        for kind in range(kinds):
            side, e = divmod(kind, share)
            tiles = [
                xf[pl.ds(b * per_block + kind * parts + q, tok, stride=kinds * parts), :]
                for q in range(parts)
            ]
            for w, value in enumerate(windows_of(tiles, tok)):
                if side == 0:
                    rhs[e, w * tok : (w + 1) * tok, cols] = jnp.where(lane < tok, value, 0.0).astype(BF16)
                else:
                    lhs[e, w * tok : (w + 1) * tok, cols] = value.astype(BF16)
        return carry

    lax.fori_loop(0, blocks, unpack, 0, unroll=True)

    source = lax.broadcasted_iota(jnp.int32, (side_len, blocks * LANES), 0)
    target = lax.broadcasted_iota(jnp.int32, (side_len, blocks * LANES), 1)
    block, spot = target // LANES, target % LANES
    wanted = (spot % 8) * tok + block * groups + spot // 8
    place = jnp.where((source == wanted) & (spot < tok), 1.0, 0.0).astype(BF16)
    for e in range(share):
        product = nt(lhs[e], rhs[e]).astype(BF16)
        moved[e] = nn(product, place)

    def pack(b, carry):
        cols = pl.ds(pl.multiple_of(b * LANES, LANES), LANES)
        for e in range(share):
            tiles = [None] * parts
            for w in range(8):
                value = moved[e, w * tok : (w + 1) * tok, cols]
                q, off = divmod(w * tok, LANES)
                first = value if off == 0 else pltpu.roll(value, off, 1)
                tiles[q] = first if tiles[q] is None else jnp.where(lane >= off, first, tiles[q])
                if off + tok > LANES:
                    tiles[q + 1] = first
            for q in range(parts):
                at = b * blocks * out.shape[1] + e * parts + q
                of[pl.ds(at, tok, stride=share * parts), :] = tiles[q]
        return carry

    lax.fori_loop(0, blocks, pack, 0, unroll=True)
    out[...] = of[...].astype(BF16).reshape(out.shape)


def updated_group(g, each, devices, wide, gain, w_out, pair, gate):
    parts = 3
    share = w_out.shape[1] // devices
    tiles = [
        jnp.concatenate(
            [
                wide[pl.ds(g * share * parts + e * parts + q, devices, stride=each), :]
                for q in range(parts)
            ],
            axis=1,
        )
        for e in range(share)
    ]
    normed = norm(jnp.concatenate(tiles, axis=0), gain[...], 0).astype(BF16)
    return (pair[g].astype(F32) + gate[g] * nn(w_out[...], normed)).astype(BF16)


def middle_kernel(tri, pair, gate, gain_out, w_out, mask, gain, weights, w_gate, send, pair_new, gate_new, thin, wide, here, gates, sems):
    devices, each = tri.shape[0], tri.shape[1]
    groups = pair.shape[0]
    moves = [
        (
            pltpu.make_async_copy(pair.at[g], here.at[g], sems.at[0, g]),
            pltpu.make_async_copy(gate.at[g], gates.at[g], sems.at[1, g]),
        )
        for g in range(groups)
    ]
    for both in moves:
        for move in both:
            move.start()
    thin[...] = tri[...].astype(F32).reshape(thin.shape)
    for g in range(groups):
        for move in moves[g]:
            move.wait()
        block = updated_group(g, each, devices, thin, gain_out, w_out, here, gates)
        pair_new[g] = block
        normed = norm(block.astype(F32), gain[...], 0).astype(BF16)
        send_group(g, normed, weights[...], mask[pl.ds(g, 1), :], wide, devices)
        gate_new[g] = sigmoid(nn(w_gate[...], normed))
    send[...] = wide[...].astype(BF16).reshape(send.shape)


def last_kernel(tri, pair, gate, gain_out, w_out, gain, w_up, d_pair, grad, hidden, pair_new, thin, total, there, units, pairs, small, sems, outs):
    devices, each = tri.shape[0], tri.shape[1]
    groups, span = pair.shape[0], pair.shape[2]
    move = pltpu.make_async_copy(d_pair, there, sems.at[0])
    move.start()
    thin[...] = tri[...].astype(F32).reshape(thin.shape)
    expand = total.shape[0]
    leaving = []
    for g in range(groups):
        block = updated_group(g, each, devices, thin, gain_out, w_out, pair, gate)
        pairs[g] = block
        leaving.append(pltpu.make_async_copy(pairs.at[g], pair_new.at[g], outs.at[0, g]))
        normed = norm(block.astype(F32), gain[...], 0).astype(BF16)
        up = nn(w_up[...], normed)
        first = up[:expand]
        made = (first * sigmoid(first) * up[expand:]).astype(BF16)
        units[g] = made
        leaving.append(pltpu.make_async_copy(units.at[g], hidden.at[g], outs.at[1, g]))
        leaving[-2].start()
        leaving[-1].start()
        if g == 0:
            move.wait()
        part = nn(made, there[g * span : (g + 1) * span, :])
        total[...] = part if g == 0 else total[...] + part
    small[...] = total[...].astype(BF16)
    leaving.append(pltpu.make_async_copy(small, grad, sems.at[1]))
    leaving[-1].start()
    for copy in leaving:
        copy.wait()


def down_kernel(hidden, pair, w_down, out, wide):
    tok = out.shape[0]

    def group(g, carry):
        result = (pair[g].astype(F32) + nn(w_down[...], hidden[g])).T
        for n in range(8):
            wide[pl.ds(g * 8 + n, tok, stride=tok), :] = result[n * tok : (n + 1) * tok]
        return carry

    lax.fori_loop(0, hidden.shape[0], group, 0)
    out[...] = wide[...].astype(BF16).reshape(out.shape)


def call(kernel, outs, scratch, name, cost, *args, far=(), far_out=(), scalar=(), scalar_out=()):
    space = [
        pltpu.SMEM if n in scalar else pltpu.HBM if n in far else pltpu.VMEM for n in range(len(args))
    ]
    args = [
        pltpu.with_memory_space_constraint(arg, pltpu.HBM) if n in far else arg
        for n, arg in enumerate(args)
    ]
    many = isinstance(outs, tuple)
    out_space = [
        pltpu.HBM if n in far_out else pltpu.SMEM if n in scalar_out else pltpu.VMEM for n in range(len(outs) if many else 1)
    ]
    out_specs = tuple(pl.BlockSpec(memory_space=s) for s in out_space)
    listed = [
        pltpu.HBM(o.shape, o.dtype) if n in far_out else o
        for n, o in enumerate(outs if many else (outs,))
    ]
    outs = tuple(listed) if many else listed[0]
    return pl.pallas_call(
        kernel,
        out_shape=outs,
        in_specs=[pl.BlockSpec(memory_space=s) for s in space],
        out_specs=out_specs if many else out_specs[0],
        scratch_shapes=scratch,
        compiler_params=PARAMS,
        name=name,
        cost_estimate=pl.CostEstimate(flops=cost, bytes_accessed=4 * 2**20, transcendentals=10**6),
    )(*args)


def local(
    atom_feats,
    atom_token,
    atom_counts,
    restype,
    pair_in,
    pair_mask,
    w_atom,
    w_restype,
    w_pair,
    ln_tri,
    w_tri_in,
    ln_tri_out,
    w_tri_out,
    ln_trans,
    w_up,
    w_down,
    d_pair,
):
    n_row, n_col = lax.axis_size("row"), lax.axis_size("col")
    devices = n_row * n_col
    tok = pair_in.shape[1]
    width = pair_in.shape[3]
    inner = w_tri_out.shape[1]
    expand = w_down.shape[0]
    share = inner // devices
    count = tok * tok
    groups = tok // 8
    span = 8 * tok

    shape = jax.ShapeDtypeStruct
    cost = 400 * 10**6
    feats = call(
        spread_kernel,
        shape((devices,) + atom_feats.shape[1:], BF16),
        [pltpu.VMEM((n_col,) + atom_feats.shape[1:], BF16), pltpu.SemaphoreType.DMA((n_row,))],
        "spread",
        cost // 100,
        atom_feats[0],
        far_out=(0,),
    )
    feats = exchange(feats, ("row", "col")).reshape(-1, atom_feats.shape[-1])

    plain, tokens, bounds = call(
        prepare_kernel,
        (
            shape((groups, width, span), BF16),
            shape((2 * tok, 4), jnp.int32),
            shape((4,), jnp.int32),
        ),
        [
            pltpu.VMEM((count, width), F32),
            pltpu.VMEM((groups, width, span), BF16),
            pltpu.SemaphoreType.DMA,
        ],
        "prepare",
        cost,
        jnp.stack([lax.axis_index("row"), lax.axis_index("col")]).astype(jnp.int32),
        pair_in[0],
        atom_counts,
        restype,
        far_out=(0,),
        scalar=(0,),
        scalar_out=(2,),
    )
    valid = pair_mask[0].astype(F32)
    mask = valid.reshape(groups, span)

    def column(gain):
        return jnp.broadcast_to(gain[:, None], (gain.shape[0], span))

    def side_weights(weights):
        blocks = weights[:, : 4 * inner].reshape(width, 2, 2, devices, share)
        return blocks.transpose(2, 1, 4, 3, 0).reshape(4 * inner, width)

    def by_owner(values, update):
        if update == 0:
            order = values.reshape((n_col, n_row, share) + values.shape[1:]).swapaxes(0, 1)
        else:
            order = values.reshape((n_row, n_col, share) + values.shape[1:])
        return jnp.moveaxis(order, 2, 0).reshape(values.shape)

    rows_out = 2 * share * count // LANES
    rows_back = share * count // LANES
    send_shape = shape((devices, rows_out, LANES), BF16)
    back_shape = shape((devices, rows_back, LANES), BF16)
    wide = pltpu.VMEM((devices * rows_out, LANES), F32)
    thin = pltpu.VMEM((devices * rows_back, LANES), F32)
    flat = shape((groups, width, span), BF16)
    flat_wide = shape((groups, width, span), F32)
    here = pltpu.VMEM(flat.shape, BF16)
    gates = pltpu.VMEM(flat.shape, F32)

    def triangle(value):
        blocks = n_row
        return call(
            functools.partial(triangle_kernel, tok, blocks),
            back_shape,
            [
                wide,
                pltpu.VMEM((share, blocks * tok, blocks * LANES), BF16),
                pltpu.VMEM((share, blocks * tok, blocks * LANES), BF16),
                pltpu.VMEM((share, blocks * tok, blocks * LANES), F32),
                thin,
            ],
            "triangle",
            cost,
            value,
        )

    send, sides = call(
        front_kernel,
        (send_shape, shape((width, 2 * tok), BF16)),
        [wide, here, pltpu.SemaphoreType.DMA],
        "front",
        cost,
        bounds,
        feats,
        tokens,
        w_atom,
        w_restype,
        w_pair,
        plain,
        mask,
        column(ln_tri[0]),
        side_weights(w_tri_in[0]),
        far=(6,),
        scalar=(0,),
    )
    arrived = exchange(send, ("col", "row"))
    arrived, sides, pair_in, d_pair, valid, w_tri_in, w_tri_out, ln_tri, ln_tri_out, w_up, w_down, ln_trans = (
        lax.optimization_barrier(
            (arrived, sides, pair_in, d_pair, valid, w_tri_in, w_tri_out, ln_tri, ln_tri_out, w_up, w_down, ln_trans)
        )
    )
    tri = exchange(triangle(arrived), ("row", "col"))
    w_gates = w_tri_in[:, :, 4 * inner :].swapaxes(1, 2)
    w_outs = [by_owner(w_tri_out[u], u).T for u in range(2)]
    gains_out = [column(by_owner(ln_tri_out[u], u)) for u in range(2)]
    pair, gate = call(
        first_gate_kernel,
        (flat, flat_wide),
        [pltpu.VMEM((count, width), F32), here, gates, pltpu.SemaphoreType.DMA((2,))],
        "first_gate",
        cost,
        pair_in[0],
        sides,
        column(ln_tri[0]),
        w_gates[0],
        far_out=(0, 1),
    )
    turned_grad = call(
        turn_kernel,
        shape((count, width), BF16),
        [pltpu.VMEM((count, width), F32), pltpu.VMEM((count, width), BF16), pltpu.SemaphoreType.DMA],
        "turn",
        cost,
        d_pair[0],
        far_out=(0,),
    )
    late = [gains_out[1], w_outs[1], column(ln_trans), w_up.T, w_down.T, turned_grad]
    ready = [
        gains_out[0],
        w_outs[0],
        valid.T.reshape(groups, span),
        column(ln_tri[1]),
        side_weights(w_tri_in[1]),
        w_gates[1],
    ]
    ready, late = lax.optimization_barrier((ready, late))
    send, pair, gate = call(
        middle_kernel,
        (send_shape, flat, flat_wide),
        [thin, wide, here, gates, pltpu.SemaphoreType.DMA((2, groups))],
        "middle",
        cost,
        tri,
        pair,
        gate,
        *ready,
        far=(1, 2),
    )
    arrived = exchange(send, ("row", "col"))
    tri = exchange(triangle(arrived), ("row", "col"))
    grad, hidden, pair = call(
        last_kernel,
        (shape((expand, width), BF16), shape((groups, expand, span), BF16), flat),
        [
            thin,
            pltpu.VMEM((expand, width), F32),
            pltpu.VMEM((count, width), BF16),
            pltpu.VMEM((groups, expand, span), BF16),
            here,
            pltpu.VMEM((expand, width), BF16),
            pltpu.SemaphoreType.DMA((2,)),
            pltpu.SemaphoreType.DMA((2, groups)),
        ],
        "last",
        2 * cost,
        tri,
        pair,
        gate,
        late[0],
        late[1],
        late[2],
        late[3],
        late[5],
        far=(7,),
        far_out=(0, 1, 2),
    )
    everyone = devices * lax.axis_size("rep")
    grad = exchange(grad.reshape(everyone, expand // everyone, width), ("row", "col", "rep"))
    result = call(
        down_kernel,
        shape((tok, tok, width), BF16),
        [pltpu.VMEM((count, width), F32)],
        "down",
        cost,
        hidden,
        pair,
        late[4],
    )
    return (result[None], jnp.sum(grad.astype(F32), axis=0))


def solution(mesh):
    return jax.shard_map(
        local,
        mesh=mesh,
        in_specs=(
            P("rep", ("row", "col"), None),
            P("rep", ("row", "col")),
            P("rep", None),
            P("rep", None),
            P("rep", "row", "col", None),
            P("rep", "row", "col"),
            P(),
            P(),
            P(),
            P(),
            P(),
            P(),
            P(),
            P(),
            P(),
            P(),
            P("rep", "row", "col", None),
        ),
        out_specs=(P("rep", "row", "col", None), P(("row", "col", "rep"), None)),
        check_vma=False,
    )
```

time: 167 us -> 150 us (0.90)
  blocking collectives: 23.4 us -> 64.7 us
  waiting for transfers between devices: 60.4 us -> 22.6 us
  starting transfers between devices: 30.6 us -> 21.4 us
  local copies, waits for them, and re-layouts: 11.9 us -> 5.96 us
  Pallas kernels: 37.2 us -> 32.8 us
    all_to_all x1 -> x3, blocking collectives: 23.4 us -> 64.7 us  [exchange(): return lax.all_to_all(value, axes, 0, 0, tiled=True)]
    all_to_all x5 -> x3, waiting for transfers between devices: 60.4 us -> 22.6 us  [exchange(): return lax.all_to_all(value, axes, 0, 0, tiled=True)]
    all_to_all x5 -> x3, starting transfers between devices: 30.6 us -> 21.4 us  [exchange(): return lax.all_to_all(value, axes, 0, 0, tiled=True)]
    pallas_call x8 -> x10, Pallas kernels: 37.2 us -> 32.8 us  [call(): pl.pallas_call(kernel, out_shape=outs, in_specs=[pl.BlockSpec(memory_spac...]
    unnamed x49 -> x37, local copies, waits for them, and re-layouts: 7.59 us -> 3.67 us
  transfers between devices with their start and end apart: 5 -> 3, of which waited for: 5 -> 3; matrix products, arithmetic and copies ran while one was open for 2% -> 2% of each run, Pallas kernels for 4% -> 7%
where the time goes in v1:
time: 150 us
  blocking collectives  64.7 us (43%)
  Pallas kernels  32.8 us (22%)
  waiting for transfers between devices  22.6 us (15%)
  starting transfers between devices  21.4 us (14%)
  local copies, waits for them, and re-layouts  5.96 us (4%)
    all_to_all x3, blocking collectives, exchange(): return lax.all_to_all(value, axes, 0, 0, tiled=True)  64.7 us
    pallas_call x10, Pallas kernels, call(): pl.pallas_call(kernel, out_shape=outs, in_specs=[pl.BlockSpec(memory_spac...  32.8 us
    all_to_all x3, waiting for transfers between devices, exchange(): return lax.all_to_all(value, axes, 0, 0, tiled=True)  22.6 us
    all_to_all x3, starting transfers between devices, exchange(): return lax.all_to_all(value, axes, 0, 0, tiled=True)  21.4 us
    unnamed x37, local copies, waits for them, and re-layouts  3.67 us
  transfers between devices with their start and end apart: 3, of which 3 were waited for; matrix products, arithmetic and copies ran while one was open for 2% of the time, Pallas kernels for 7%

profile of v1, /device:TPU:1, one launch (start us, length us, event | category | flops | bytes accessed | tf_op | source)
XLA Modules:
  0.0 149.6 jit_solution(6451784417223567881)
XLA Ops:
  0.6 0.7 copy-done.7
  1.3 1.0 spread.1
  2.4 10.5 %all-to-all-start = ((bf16[64,48,128]{2,1,0:T(8,128)(2,1)}), bf16[64,48,128]{2,1,0:T(8,128)(2,1)S(1)}, u32[]{:S(2)}, u32[]{:S(2)}) async-start(bf16[64,48,128]{2,1,0:T(8,128)(2,1)} %spread.1), calls=%async_computation | async-start | bytes 1572864 | tf_op jit(solution)/shard_map/all_to_all | solution.py:36
  13.0 0.2 copy.54
  13.3 2.7 %prepare.1 = (bf16[6,128,384]{2,1,0:T(8,128)(2,1)}, s32[96,4]{1,0:T(8,128)S(1)}, s32[4]{0:T(128)S(1)}) custom-call(s32[2]{0:T(128)S(1)} %pad_add_fusion.place, bf16[48,48,128]{2,1,0:T(8,128)(2,1)S(1)} %bitcast.57, s32[1,384]{1,0:T(1,128)S(1)} %copy-done.8, s32[1,384]{1,0:T(1,128)S(1)} %copy-done.9), custom_call_target="tpu_custom_call" | custom-call | flops 400000000 | bytes 4194304 | tf_op jit(solution)/shard_map/prepare/pallas_call | solution.py:380
  16.0 12.0 %all-to-all-done = bf16[64,48,128]{2,1,0:T(8,128)(2,1)S(1)} async-done(((bf16[64,48,128]{2,1,0:T(8,128)(2,1)}), bf16[64,48,128]{2,1,0:T(8,128)(2,1)S(1)}, u32[]{:S(2)}, u32[]{:S(2)}) %all-to-all-start) | async-done | bytes 786464 | tf_op jit(solution)/shard_map/all_to_all | solution.py:36
  28.1 4.6 %front.1 = (bf16[64,72,128]{2,1,0:T(8,128)(2,1)S(1)}, bf16[128,96]{1,0:T(8,128)(2,1)S(1)}) custom-call(s32[4]{0:T(128)S(1)} %get-tuple-element.39.bounds, bf16[3072,128]{1,0:T(8,128)(2,1)S(1)} %bitcast.49, s32[96,4]{1,0:T(8,128)S(1)} %get-tuple-element.40.tokens, bf16[128,384]{1,0:T(8,128)(2,1)S(1)} %copy-done.3, bf16[32,384]{1,0:T(8,128)(2,1)S(1)} %copy-done.4, ...), custom_call_target="tpu_custom_call" | custom-call | flops 400000000 | bytes 4194304 | tf_op jit(solution)/shard_map/front/pallas_call | solution.py:380
  32.7 23.4 %all_to_all.30.x = bf16[64,72,128]{2,1,0:T(8,128)(2,1)S(1)} all-to-all(bf16[64,72,128]{2,1,0:T(8,128)(2,1)S(1)} %get-tuple-element.42), channel_id=1, replica_groups=mesh['row'=8,'col'=8,'rep'=2] {'col','row'}, dimensions={0} | all-to-all | bytes 2359296 | tf_op jit(solution)/shard_map/all_to_all | solution.py:36
  56.2 3.7 %triangle.2 = bf16[64,36,128]{2,1,0:T(8,128)(2,1)} custom-call(bf16[64,72,128]{2,1,0:T(8,128)(2,1)S(1)} %all_to_all.30.x), custom_call_target="tpu_custom_call" | custom-call | flops 400000000 | bytes 4194304 | tf_op jit(solution)/shard_map/triangle/pallas_call | solution.py:380
  59.9 4.9 %all-to-all-start.2 = ((bf16[64,36,128]{2,1,0:T(8,128)(2,1)}), bf16[64,36,128]{2,1,0:T(8,128)(2,1)S(1)}, u32[]{:S(2)}, u32[]{:S(2)}) async-start(bf16[64,36,128]{2,1,0:T(8,128)(2,1)} %triangle.2), calls=%async_computation.2 | async-start | bytes 1310720 | tf_op jit(solution)/shard_map/all_to_all | solution.py:36
  64.8 0.2 copy.42
  65.3 0.1 reshape_squeeze.14
  65.4 0.1 copy.49
  65.6 0.1 reshape_squeeze.12
  65.8 0.1 copy.43
  66.0 0.1 copy.51
  66.3 0.1 copy.53
  66.4 0.2 copy.52
  66.7 1.3 turn.1.d_pair
  68.5 3.7 %first_gate.1 = (bf16[6,128,384]{2,1,0:T(8,128)(2,1)}, f32[6,128,384]{2,1,0:T(8,128)}) custom-call(bf16[48,48,128]{2,1,0:T(8,128)(2,1)S(1)} %bitcast.58, bf16[128,96]{1,0:T(8,128)(2,1)S(1)} %get-tuple-element.46.sides, f32[128,384]{1,0:T(8,128)S(1)} %broadcast_in_dim.47.gain, bf16[128,128]{1,0:T(8,128)(2,1)S(1)} %get-tuple-element.81.w_gate), custom_call_target="tpu_custom_call" | custom-call | flops 400000000 | bytes 4194304 | tf_op jit(solution)/shard_map/first_gate/pallas_call | solution.py:380
  72.2 6.4 %all-to-all-done.2.tri = bf16[64,36,128]{2,1,0:T(8,128)(2,1)S(1)} async-done(((bf16[64,36,128]{2,1,0:T(8,128)(2,1)}), bf16[64,36,128]{2,1,0:T(8,128)(2,1)S(1)}, u32[]{:S(2)}, u32[]{:S(2)}) %all-to-all-start.2) | async-done | bytes 589856 | tf_op jit(solution)/shard_map/all_to_all | solution.py:36
  78.6 4.7 %middle.1 = (bf16[64,72,128]{2,1,0:T(8,128)(2,1)S(1)}, bf16[6,128,384]{2,1,0:T(8,128)(2,1)S(1)}, f32[6,128,384]{2,1,0:T(8,128)S(1)}) custom-call(bf16[64,36,128]{2,1,0:T(8,128)(2,1)S(1)} %all-to-all-done.2.tri, bf16[6,128,384]{2,1,0:T(8,128)(2,1)} %get-tuple-element.49.pair, f32[6,128,384]{2,1,0:T(8,128)} %get-tuple-element.50.gate, ...), custom_call_target="tpu_custom_call" | custom-call | flops 400000000 | bytes 4194304 | tf_op jit(solution)/shard_map/middle/pallas_call | solution.py:380
  83.3 23.4 %all_to_all.31.x = bf16[64,72,128]{2,1,0:T(8,128)(2,1)S(1)} all-to-all(bf16[64,72,128]{2,1,0:T(8,128)(2,1)S(1)} %get-tuple-element.64), channel_id=1, replica_groups=mesh['row'=8,'col'=8,'rep'=2] {'row','col'}, dimensions={0} | all-to-all | bytes 2359296 | tf_op jit(solution)/shard_map/all_to_all | solution.py:36
  106.7 2.8 %triangle.3 = bf16[64,36,128]{2,1,0:T(8,128)(2,1)S(1)} custom-call(bf16[64,72,128]{2,1,0:T(8,128)(2,1)S(1)} %all_to_all.31.x), custom_call_target="tpu_custom_call" | custom-call | flops 400000000 | bytes 4194304 | tf_op jit(solution)/shard_map/triangle/pallas_call | solution.py:380
  109.6 17.9 %all_to_all.32.tri = bf16[64,36,128]{2,1,0:T(8,128)(2,1)S(1)} all-to-all(bf16[64,36,128]{2,1,0:T(8,128)(2,1)S(1)} %triangle.3), channel_id=1, replica_groups=mesh['row'=8,'col'=8,'rep'=2] {'row','col'}, dimensions={0} | all-to-all | bytes 1179648 | tf_op jit(solution)/shard_map/all_to_all | solution.py:36
  127.5 5.4 %last.1 = (bf16[512,128]{1,0:T(8,128)(2,1)}, bf16[6,512,384]{2,1,0:T(8,128)(2,1)}, bf16[6,128,384]{2,1,0:T(8,128)(2,1)}) custom-call(bf16[64,36,128]{2,1,0:T(8,128)(2,1)S(1)} %all_to_all.32.tri, bf16[6,128,384]{2,1,0:T(8,128)(2,1)S(1)} %get-tuple-element.65.pair, f32[6,128,384]{2,1,0:T(8,128)S(1)} %get-tuple-element.66.gate, ...), custom_call_target="tpu_custom_call" | custom-call | flops 800000000 | bytes 4194304 | tf_op jit(solution)/shard_map/last/pallas_call | solution.py:380
  132.9 6.0 %all-to-all-start.5 = ((bf16[128,4,128]{2,1,0:T(4,128)(2,1)}), bf16[128,4,128]{2,1,0:T(4,128)(2,1)S(1)}, u32[]{:S(2)}, u32[]{:S(2)}) async-start(bf16[128,4,128]{2,1,0:T(4,128)(2,1)} %bitcast.66), calls=%async_computation.5 | async-start | bytes 262144 | tf_op jit(solution)/shard_map/all_to_all | solution.py:36
  138.9 1.7 %copy-done = bf16[6,512,384]{2,1,0:T(8,128)(2,1)S(1)} copy-done((bf16[6,512,384]{2,1,0:T(8,128)(2,1)S(1)}, bf16[6,512,384]{2,1,0:T(8,128)(2,1)}, u32[]{:S(2)}) %copy-start) | copy-done | bytes 2359320
  140.6 1.1 copy-done.1
  141.7 2.9 %down.1 = bf16[48,48,128]{2,1,0:T(8,128)(2,1)} custom-call(bf16[6,512,384]{2,1,0:T(8,128)(2,1)S(1)} %copy-done, bf16[6,128,384]{2,1,0:T(8,128)(2,1)S(1)} %copy-done.1, bf16[128,512]{1,0:T(8,128)(2,1)S(1)} %bitcast.51), custom_call_target="tpu_custom_call" | custom-call | flops 400000000 | bytes 4194304 | tf_op jit(solution)/shard_map/down/pallas_call | solution.py:380
  144.6 4.3 %all-to-all-done.5 = bf16[128,4,128]{2,1,0:T(4,128)(2,1)S(1)} async-done(((bf16[128,4,128]{2,1,0:T(4,128)(2,1)}), bf16[128,4,128]{2,1,0:T(4,128)(2,1)S(1)}, u32[]{:S(2)}, u32[]{:S(2)}) %all-to-all-start.5) | async-done | bytes 131104 | tf_op jit(solution)/shard_map/all_to_all | solution.py:36
  148.8 0.7 convert_reduce_fusion
  (62 shorter events, 1.3 us)
Async XLA Ops:
  0.6 0.7 copy-start.7
  2.3 10.6 %copy-start.14 = (s32[1,48,48]{2,1,0:T(8,128)S(1)}, s32[1,48,48]{2,1,0:T(8,128)}, u32[]{:S(2)}) copy-start(s32[1,48,48]{2,1,0:T(8,128)} %param.21) | copy-start | bytes 27652
  2.3 10.7 %slice-start = ((bf16[2,128,640]{2,1,0:T(8,128)(2,1)}), bf16[1,128,640]{2,1,0:T(8,128)(2,1)S(1)}, s32[]{:S(2)}) async-start(bf16[2,128,640]{2,1,0:T(8,128)(2,1)} %param.26), calls=%async_computation.6 | async-start | bytes 327680 | tf_op jit(solution)/shard_map/slice | solution.py:517
  2.3 11.0 %copy-start.6 = (bf16[1,48,48,128]{3,2,1,0:T(8,128)(2,1)S(1)}, bf16[1,48,48,128]{3,2,1,0:T(8,128)(2,1)}, u32[]{:S(2)}) copy-start(bf16[1,48,48,128]{3,2,1,0:T(8,128)(2,1)} %param.20) | copy-start | bytes 1769476
  2.3 11.0 %copy-start.8 = (s32[1,384]{1,0:T(1,128)S(1)}, s32[1,384]{1,0:T(1,128)}, u32[]{:S(2)}) copy-start(s32[1,384]{1,0:T(1,128)} %counts.1) | copy-start | bytes 4612
  2.4 11.0 %copy-start.9 = (s32[1,384]{1,0:T(1,128)S(1)}, s32[1,384]{1,0:T(1,128)}, u32[]{:S(2)}) copy-start(s32[1,384]{1,0:T(1,128)} %types.1) | copy-start | bytes 4612
  2.4 25.6 %all-to-all-start = ((bf16[64,48,128]{2,1,0:T(8,128)(2,1)}), bf16[64,48,128]{2,1,0:T(8,128)(2,1)S(1)}, u32[]{:S(2)}, u32[]{:S(2)}) async-start(bf16[64,48,128]{2,1,0:T(8,128)(2,1)} %spread.1), calls=%async_computation | async-start | bytes 1572864 | tf_op jit(solution)/shard_map/all_to_all | solution.py:36
  13.1 2.8 %copy-start.15 = (f32[2,128]{1,0:T(2,128)S(1)}, f32[2,128]{1,0:T(2,128)}, u32[]{:S(2)}) copy-start(f32[2,128]{1,0:T(2,128)} %param.25) | copy-start | bytes 3076
  13.2 14.9 %copy-start.2 = (bf16[384,256]{1,0:T(8,128)(2,1)S(1)}, bf16[384,256]{1,0:T(8,128)(2,1)}, u32[]{:S(2)}) copy-start(bf16[384,256]{1,0:T(8,128)(2,1)} %w_pair.1) | copy-start | bytes 589828
  13.2 14.9 %copy-start.3 = (bf16[128,384]{1,0:T(8,128)(2,1)S(1)}, bf16[128,384]{1,0:T(8,128)(2,1)}, u32[]{:S(2)}) copy-start(bf16[128,384]{1,0:T(8,128)(2,1)} %w_atom.1) | copy-start | bytes 294916
  13.2 14.9 %copy-start.4 = (bf16[32,384]{1,0:T(8,128)(2,1)S(1)}, bf16[32,384]{1,0:T(8,128)(2,1)}, u32[]{:S(2)}) copy-start(bf16[32,384]{1,0:T(8,128)(2,1)} %w_restype.1) | copy-start | bytes 73732
  56.2 8.6 %copy-start.13 = (bf16[2,128,128]{2,1,0:T(8,128)(2,1)S(1)}, bf16[2,128,128]{2,1,0:T(8,128)(2,1)}, u32[]{:S(2)}) copy-start(bf16[2,128,128]{2,1,0:T(8,128)(2,1)} %param.28) | copy-start | bytes 196612
  59.9 5.0 %copy-start.10 = (bf16[2,128,640]{2,1,0:T(8,128)(2,1)S(1)}, bf16[2,128,640]{2,1,0:T(8,128)(2,1)}, u32[]{:S(2)}) copy-start(bf16[2,128,640]{2,1,0:T(8,128)(2,1)} %param.26) | copy-start | bytes 983044
  59.9 5.2 %copy-start.16 = (f32[2,128]{1,0:T(2,128)S(1)}, f32[2,128]{1,0:T(2,128)}, u32[]{:S(2)}) copy-start(f32[2,128]{1,0:T(2,128)} %param.27) | copy-start | bytes 3076
  59.9 6.4 %copy-start.12 = (bf16[512,128]{1,0:T(8,128)(2,1)S(1)}, bf16[512,128]{1,0:T(8,128)(2,1)}, u32[]{:S(2)}) copy-start(bf16[512,128]{1,0:T(8,128)(2,1)} %param.31) | copy-start | bytes 393220
  59.9 18.7 %all-to-all-start.2 = ((bf16[64,36,128]{2,1,0:T(8,128)(2,1)}), bf16[64,36,128]{2,1,0:T(8,128)(2,1)S(1)}, u32[]{:S(2)}, u32[]{:S(2)}) async-start(bf16[64,36,128]{2,1,0:T(8,128)(2,1)} %triangle.2), calls=%async_computation.2 | async-start | bytes 1310720 | tf_op jit(solution)/shard_map/all_to_all | solution.py:36
  64.8 1.6 %copy-start.11 = (bf16[128,1024]{1,0:T(8,128)(2,1)S(1)}, bf16[128,1024]{1,0:T(8,128)(2,1)}, u32[]{:S(2)}) copy-start(bf16[128,1024]{1,0:T(8,128)(2,1)} %param.30) | copy-start | bytes 786436
  65.1 1.6 %copy-start.5 = (bf16[1,48,48,128]{3,2,1,0:T(8,128)(2,1)S(1)}, bf16[1,48,48,128]{3,2,1,0:T(8,128)(2,1)}, u32[]{:S(2)}) copy-start(bf16[1,48,48,128]{3,2,1,0:T(8,128)(2,1)} %param.32) | copy-start | bytes 1769476
  66.7 1.6 %copy-start.17 = (f32[128]{0:T(128)S(1)}, f32[128]{0:T(128)}, u32[]{:S(2)}) copy-start(f32[128]{0:T(128)} %param.29) | copy-start | bytes 1540
  132.9 16.0 %all-to-all-start.5 = ((bf16[128,4,128]{2,1,0:T(4,128)(2,1)}), bf16[128,4,128]{2,1,0:T(4,128)(2,1)S(1)}, u32[]{:S(2)}, u32[]{:S(2)}) async-start(bf16[128,4,128]{2,1,0:T(4,128)(2,1)} %bitcast.66), calls=%async_computation.5 | async-start | bytes 262144 | tf_op jit(solution)/shard_map/all_to_all | solution.py:36
  138.9 1.7 %copy-start = (bf16[6,512,384]{2,1,0:T(8,128)(2,1)S(1)}, bf16[6,512,384]{2,1,0:T(8,128)(2,1)}, u32[]{:S(2)}) copy-start(bf16[6,512,384]{2,1,0:T(8,128)(2,1)} %get-tuple-element.72.hidden) | copy-start | bytes 7077892
  140.6 1.1 copy-start.1

commit v2 on v1

--- a/solution.py
+++ b/solution.py
@@ -5,11 +5,12 @@
 from jax import lax
 from jax.experimental import pallas as pl
 from jax.experimental.pallas import tpu as pltpu
-from jax.sharding import PartitionSpec as P
+from jax.sharding import Mesh, PartitionSpec as P
 
 F32, BF16 = jnp.float32, jnp.bfloat16
 LANES = 128
-UNROLL = 6
+ROW, COL = ("x", "core"), ("y", "zl")
+TOGETHER = 2
 PARAMS = pltpu.CompilerParams(vmem_limit_bytes=20 * 2**20)
 
 
@@ -36,18 +37,37 @@
     return lax.all_to_all(value, axes, 0, 0, tiled=True)
 
 
-def send_group(g, normed, weights, mask_row, wide, devices):
+def send_groups(first, normed, weights, mask, wide, devices):
     proj = nn(weights, normed)
     half = proj.shape[0] // 2
-    sides = sigmoid(proj[:half]) * proj[half:] * mask_row
+    span = mask.shape[1]
+    count = proj.shape[1] // span
+    valid = jnp.concatenate([mask[pl.ds(first + n, 1), :] for n in range(count)], axis=1)
+    sides = sigmoid(proj[:half]) * proj[half:] * valid
     rows = wide.shape[0] // devices
-    parts = sides.shape[1] // LANES
+    parts = span // LANES
     kinds = half // devices
-    for kind in range(kinds):
-        for q in range(parts):
-            wide[pl.ds((g * kinds + kind) * parts + q, devices, stride=rows), :] = sides[
-                kind * devices : (kind + 1) * devices, q * LANES : (q + 1) * LANES
-            ]
+    for n in range(count):
+        for kind in range(kinds):
+            for q in range(parts):
+                at = n * span + q * LANES
+                wide[pl.ds(((first + n) * kinds + kind) * parts + q, devices, stride=rows), :] = sides[
+                    kind * devices : (kind + 1) * devices, at : at + LANES
+                ]
+
+
+def beside(array, first):
+    return jnp.concatenate([array[first + n] for n in range(TOGETHER)], axis=1)
+
+
+def widened(gain):
+    return jnp.concatenate([gain[...]] * TOGETHER, axis=1)
+
+
+def apart(array, first, value):
+    span = value.shape[1] // TOGETHER
+    for n in range(TOGETHER):
+        array[first + n] = value[:, n * span : (n + 1) * span]
 
 
 def spread_kernel(value, out, copies, sems):
@@ -63,7 +83,7 @@
         move.wait()
 
 
-def prepare_kernel(place, pair_in, counts, types, plain, tokens, bounds, wide, made, sem):
+def prepare_kernel(chunk, place, pair_in, counts, types, w_restype, plain, tokens, bounds, chosen, embedded, wide, made, sem):
     tok, width = pair_in.shape[0], pair_in.shape[2]
     span = 8 * tok
     wide[...] = pair_in[...].astype(F32).reshape(wide.shape)
@@ -92,6 +112,9 @@
         total(token == mine, numbers),
         total(token == mine, kinds),
     ]
+    kind = lax.broadcasted_iota(jnp.int32, (2 * tok, w_restype.shape[0]), 1)
+    picked = jnp.where(kind == columns[3].astype(jnp.int32), 1.0, 0.0).astype(BF16)
+    embedded[...] = nn(picked, w_restype[...])
     lane = lax.broadcasted_iota(jnp.int32, tokens.shape, 1)
     table = jnp.zeros(tokens.shape, F32)
     for n, column in enumerate(columns):
@@ -101,8 +124,12 @@
     for k in range(2):
         first = place[k] * tok
         start = jnp.sum(jnp.where(every < first, counts[...], 0))
-        bounds[2 * k] = start // 16 * 16
-        bounds[2 * k + 1] = jnp.sum(jnp.where(every < first + tok, counts[...], 0))
+        end = jnp.sum(jnp.where(every < first + tok, counts[...], 0))
+        bounds[2 * k] = start // chunk
+        bounds[2 * k + 1] = (end + chunk - 1) // chunk
+    bounds[4] = place[0] % 2
+    for g in range(tok // 8):
+        chosen[g] = choice(g, tok, False)
     move.wait()
 
 
@@ -127,57 +154,53 @@
     move.wait()
 
 
-def added_sides(g, sides, tok, turned):
+def choice(g, tok, turned):
     shape = (2 * tok, 8 * tok)
     source = lax.broadcasted_iota(jnp.int32, shape, 0)
     token = lax.broadcasted_iota(jnp.int32, shape, 1)
     high, low = g * 8 + token // tok, token % tok
     left, right = (low, high) if turned else (high, low)
     wanted = (source == left) | (source == right + tok)
-    return nn(sides, jnp.where(wanted, 1.0, 0.0).astype(BF16))
-
-
-def front_kernel(bounds, feats, tokens, w_atom, w_restype, w_pair, plain, mask, gain, weights, send, sides, wide, pair_in, sem):
+    return jnp.where(wanted, 1.0, 0.0).astype(BF16)
+
+
+def front_kernel(bounds, same, other, tokens, embedded, w_atom, w_pair, plain, chosen, mask, gain, weights, send, sides, wide, feats, pair_in, sem):
     groups, width, span = plain.shape
     tok = span // 8
     devices = send.shape[0]
     move = pltpu.make_async_copy(plain, pair_in, sem)
     move.start()
-    chunk = 384
-    last = feats.shape[0] - chunk
+    chunks, chunk = feats.shape[0], feats.shape[1]
+    for n in range(chunks // 2):
+        feats[2 * n + bounds[4]] = same[n * chunk : (n + 1) * chunk, :]
+        feats[2 * n + 1 - bounds[4]] = other[n * chunk : (n + 1) * chunk, :]
 
     def pool(n, sums):
         out = []
         for k in range(2):
-            base = bounds[2 * k] + n * chunk
-            at = pl.multiple_of(jnp.minimum(base, last), 16)
-            act = jnp.maximum(nn(feats[pl.ds(at, chunk), :], w_atom[...]), 0.0).astype(BF16)
-            atoms = lax.broadcasted_iota(jnp.int32, (tok, chunk), 1) + at
+            q = bounds[2 * k] + n
+            act = jnp.maximum(nn(feats[jnp.minimum(q, chunks - 1)], w_atom[...]), 0.0).astype(BF16)
+            atoms = lax.broadcasted_iota(jnp.int32, (tok, chunk), 1) + q * chunk
             starts = tokens[k * tok : (k + 1) * tok, 0:1]
             ends = tokens[k * tok : (k + 1) * tok, 1:2]
-            mine = (atoms >= jnp.maximum(starts, base)) & (atoms < ends)
+            mine = (atoms >= starts) & (atoms < ends)
             out.append(sums[k] + nn(jnp.where(mine, 1.0, 0.0).astype(BF16), act))
         return tuple(out)
 
     steps = jnp.maximum(bounds[1] - bounds[0], bounds[3] - bounds[2])
     zero = jnp.zeros((tok, w_atom.shape[1]), F32)
-    sums = lax.fori_loop(0, (steps + chunk - 1) // chunk, pool, (zero, zero))
-    counts, types = tokens[:, 2:3], tokens[:, 3:4]
-    kinds = lax.broadcasted_iota(jnp.int32, (2 * tok, w_restype.shape[0]), 1)
-    embedded = nn(jnp.where(kinds == types, 1.0, 0.0).astype(BF16), w_restype[...])
-    single = (jnp.concatenate(sums, 0) / counts.astype(F32) + embedded).astype(BF16)
+    sums = lax.fori_loop(0, steps, pool, (zero, zero))
+    counts = tokens[:, 2:3].astype(F32)
+    single = (jnp.concatenate(sums, 0) / counts + embedded[...]).astype(BF16)
     left = nn(single[:tok], w_pair[:, :width])
     right = nn(single[tok:], w_pair[:, width:])
     sides[...] = jnp.concatenate([left, right], 0).T.astype(BF16)
     move.wait()
 
-    def group(g, carry):
-        block = pair_in[g].astype(F32) + added_sides(g, sides[...], tok, False)
-        normed = norm(block.astype(BF16).astype(F32), gain[...], 0).astype(BF16)
-        send_group(g, normed, weights[...], mask[pl.ds(g, 1), :], wide, devices)
-        return carry
-
-    lax.fori_loop(0, groups, group, 0, unroll=UNROLL)
+    for g in range(0, groups, TOGETHER):
+        block = beside(pair_in, g).astype(F32) + nn(sides[...], beside(chosen, g))
+        normed = norm(block.astype(BF16).astype(F32), widened(gain), 0).astype(BF16)
+        send_groups(g, normed, weights[...], mask, wide, devices)
     send[...] = wide[...].astype(BF16).reshape(send.shape)
 
 
@@ -186,11 +209,11 @@
     wide[...] = pair_in[...].astype(F32).reshape(wide.shape)
 
     def group(g, carry):
-        block = turned_rows(g, wide, tok).T + added_sides(g, sides[...], tok, True)
+        block = turned_rows(g, wide, tok).T + nn(sides[...], choice(g, tok, True))
         block = block.astype(BF16)
         pair[g] = block
         normed = norm(block.astype(F32), gain[...], 0).astype(BF16)
-        gate[g] = sigmoid(nn(w_gate[...], normed))
+        gate[g] = sigmoid(nn(w_gate[...], normed)).astype(BF16)
         return carry
 
     lax.fori_loop(0, tok // 8, group, 0)
@@ -204,14 +227,16 @@
         move.wait()
 
 
-def windows_of(parts, tok):
+def windows_of(parts, tok, start):
     lane = lax.broadcasted_iota(jnp.int32, parts[0].shape, 1)
     out = []
     for w in range(len(parts) * LANES // tok):
         q, off = divmod(w * tok, LANES)
-        value = parts[q] if off == 0 else pltpu.roll(parts[q], LANES - off, 1)
+        turn = (start - off) % LANES
+        value = parts[q] if turn == 0 else pltpu.roll(parts[q], turn, 1)
         if off + tok > LANES:
-            value = jnp.where(lane < LANES - off, value, pltpu.roll(parts[q + 1], LANES - off, 1))
+            rest = parts[q + 1] if turn == 0 else pltpu.roll(parts[q + 1], turn, 1)
+            value = jnp.where(lane < start + LANES - off, value, rest)
         out.append(value)
     return out
 
@@ -227,67 +252,72 @@
     lane = lax.broadcasted_iota(jnp.int32, (tok, LANES), 1)
     per_block = devices // blocks * x.shape[1]
 
-    def unpack(b, carry):
-        cols = pl.ds(pl.multiple_of(b * LANES, LANES), LANES)
+    half = LANES // 2
+    used = lane % half < tok
+    for b in range(0, blocks, 2):
+        cols = slice(b * half, b * half + LANES)
         for kind in range(kinds):
             side, e = divmod(kind, share)
-            tiles = [
-                xf[pl.ds(b * per_block + kind * parts + q, tok, stride=kinds * parts), :]
-                for q in range(parts)
-            ]
-            for w, value in enumerate(windows_of(tiles, tok)):
+            pairs = []
+            for n in range(2):
+                tiles = [
+                    xf[pl.ds((b + n) * per_block + kind * parts + q, tok, stride=kinds * parts), :]
+                    for q in range(parts)
+                ]
+                pairs.append(windows_of(tiles, tok, n * half))
+            for w in range(8):
+                value = jnp.where(lane < half, pairs[0][w], pairs[1][w])
+                rows = slice(w * tok, (w + 1) * tok)
                 if side == 0:
-                    rhs[e, w * tok : (w + 1) * tok, cols] = jnp.where(lane < tok, value, 0.0).astype(BF16)
+                    rhs[e, rows, cols] = jnp.where(used, value, 0.0).astype(BF16)
                 else:
-                    lhs[e, w * tok : (w + 1) * tok, cols] = value.astype(BF16)
-        return carry
-
-    lax.fori_loop(0, blocks, unpack, 0, unroll=True)
-
-    source = lax.broadcasted_iota(jnp.int32, (side_len, blocks * LANES), 0)
-    target = lax.broadcasted_iota(jnp.int32, (side_len, blocks * LANES), 1)
-    block, spot = target // LANES, target % LANES
+                    lhs[e, rows, cols] = value.astype(BF16)
+
+    width = blocks * half
+    source = lax.broadcasted_iota(jnp.int32, (side_len, width), 0)
+    target = lax.broadcasted_iota(jnp.int32, (side_len, width), 1)
+    block, spot = target // half, target % half
     wanted = (spot % 8) * tok + block * groups + spot // 8
     place = jnp.where((source == wanted) & (spot < tok), 1.0, 0.0).astype(BF16)
     for e in range(share):
         product = nt(lhs[e], rhs[e]).astype(BF16)
         moved[e] = nn(product, place)
 
-    def pack(b, carry):
-        cols = pl.ds(pl.multiple_of(b * LANES, LANES), LANES)
+    for b in range(blocks):
+        at, start = b // 2 * LANES, b % 2 * half
         for e in range(share):
             tiles = [None] * parts
             for w in range(8):
-                value = moved[e, w * tok : (w + 1) * tok, cols]
+                value = moved[e, w * tok : (w + 1) * tok, at : at + LANES]
                 q, off = divmod(w * tok, LANES)
-                first = value if off == 0 else pltpu.roll(value, off, 1)
+                turn = (off - start) % LANES
+                first = value if turn == 0 else pltpu.roll(value, turn, 1)
                 tiles[q] = first if tiles[q] is None else jnp.where(lane >= off, first, tiles[q])
                 if off + tok > LANES:
                     tiles[q + 1] = first
             for q in range(parts):
-                at = b * blocks * out.shape[1] + e * parts + q
-                of[pl.ds(at, tok, stride=share * parts), :] = tiles[q]
-        return carry
-
-    lax.fori_loop(0, blocks, pack, 0, unroll=True)
+                base = b * blocks * out.shape[1] + e * parts + q
+                of[pl.ds(base, tok, stride=share * parts), :] = tiles[q]
     out[...] = of[...].astype(BF16).reshape(out.shape)
 
 
-def updated_group(g, each, devices, wide, gain, w_out, pair, gate):
+def updated_groups(first, each, devices, wide, gain, w_out, pair, gate):
     parts = 3
     share = w_out.shape[1] // devices
     tiles = [
         jnp.concatenate(
             [
-                wide[pl.ds(g * share * parts + e * parts + q, devices, stride=each), :]
+                wide[pl.ds((g * share + e) * parts + q, devices, stride=each), :]
+                for g in range(first, first + TOGETHER)
                 for q in range(parts)
             ],
             axis=1,
         )
         for e in range(share)
     ]
-    normed = norm(jnp.concatenate(tiles, axis=0), gain[...], 0).astype(BF16)
-    return (pair[g].astype(F32) + gate[g] * nn(w_out[...], normed)).astype(BF16)
+    normed = norm(jnp.concatenate(tiles, axis=0), widened(gain), 0).astype(BF16)
+    change = beside(gate, first).astype(F32) * nn(w_out[...], normed)
+    return (beside(pair, first).astype(F32) + change).astype(BF16)
 
 
 def middle_kernel(tri, pair, gate, gain_out, w_out, mask, gain, weights, w_gate, send, pair_new, gate_new, thin, wide, here, gates, sems):
@@ -304,14 +334,15 @@
         for move in both:
             move.start()
     thin[...] = tri[...].astype(F32).reshape(thin.shape)
-    for g in range(groups):
-        for move in moves[g]:
-            move.wait()
-        block = updated_group(g, each, devices, thin, gain_out, w_out, here, gates)
-        pair_new[g] = block
-        normed = norm(block.astype(F32), gain[...], 0).astype(BF16)
-        send_group(g, normed, weights[...], mask[pl.ds(g, 1), :], wide, devices)
-        gate_new[g] = sigmoid(nn(w_gate[...], normed))
+    for g in range(0, groups, TOGETHER):
+        for both in moves[g : g + TOGETHER]:
+            for move in both:
+                move.wait()
+        block = updated_groups(g, each, devices, thin, gain_out, w_out, here, gates)
+        apart(pair_new, g, block)
+        normed = norm(block.astype(F32), widened(gain), 0).astype(BF16)
+        send_groups(g, normed, weights[...], mask, wide, devices)
+        apart(gate_new, g, sigmoid(nn(w_gate[...], normed)).astype(BF16))
     send[...] = wide[...].astype(BF16).reshape(send.shape)
 
 
@@ -323,21 +354,24 @@
     thin[...] = tri[...].astype(F32).reshape(thin.shape)
     expand = total.shape[0]
     leaving = []
-    for g in range(groups):
-        block = updated_group(g, each, devices, thin, gain_out, w_out, pair, gate)
-        pairs[g] = block
-        leaving.append(pltpu.make_async_copy(pairs.at[g], pair_new.at[g], outs.at[0, g]))
-        normed = norm(block.astype(F32), gain[...], 0).astype(BF16)
+    for g in range(0, groups, TOGETHER):
+        block = updated_groups(g, each, devices, thin, gain_out, w_out, pair, gate)
+        apart(pairs, g, block)
+        normed = norm(block.astype(F32), widened(gain), 0).astype(BF16)
         up = nn(w_up[...], normed)
         first = up[:expand]
         made = (first * sigmoid(first) * up[expand:]).astype(BF16)
-        units[g] = made
-        leaving.append(pltpu.make_async_copy(units.at[g], hidden.at[g], outs.at[1, g]))
-        leaving[-2].start()
-        leaving[-1].start()
+        apart(units, g, made)
+        for n in range(g, g + TOGETHER):
+            for copy in (
+                pltpu.make_async_copy(pairs.at[n], pair_new.at[n], outs.at[0, n]),
+                pltpu.make_async_copy(units.at[n], hidden.at[n], outs.at[1, n]),
+            ):
+                copy.start()
+                leaving.append(copy)
         if g == 0:
             move.wait()
-        part = nn(made, there[g * span : (g + 1) * span, :])
+        part = nn(made, there[g * span : (g + TOGETHER) * span, :])
         total[...] = part if g == 0 else total[...] + part
     small[...] = total[...].astype(BF16)
     leaving.append(pltpu.make_async_copy(small, grad, sems.at[1]))
@@ -408,7 +442,7 @@
     w_down,
     d_pair,
 ):
-    n_row, n_col = lax.axis_size("row"), lax.axis_size("col")
+    n_row, n_col = lax.axis_size(ROW), lax.axis_size(COL)
     devices = n_row * n_col
     tok = pair_in.shape[1]
     width = pair_in.shape[3]
@@ -421,23 +455,26 @@
 
     shape = jax.ShapeDtypeStruct
     cost = 400 * 10**6
-    feats = call(
+    half = devices // 2
+    spread = call(
         spread_kernel,
-        shape((devices,) + atom_feats.shape[1:], BF16),
-        [pltpu.VMEM((n_col,) + atom_feats.shape[1:], BF16), pltpu.SemaphoreType.DMA((n_row,))],
+        shape((half,) + atom_feats.shape[1:], BF16),
+        [pltpu.VMEM((n_row,) + atom_feats.shape[1:], BF16), pltpu.SemaphoreType.DMA((half // n_row,))],
         "spread",
         cost // 100,
         atom_feats[0],
         far_out=(0,),
     )
-    feats = exchange(feats, ("row", "col")).reshape(-1, atom_feats.shape[-1])
-
-    plain, tokens, bounds = call(
-        prepare_kernel,
+    same = exchange(spread, ("x", "y", "zl")).reshape(-1, atom_feats.shape[-1])
+
+    plain, tokens, bounds, chosen, embedded = call(
+        functools.partial(prepare_kernel, n_col * atom_feats.shape[1]),
         (
             shape((groups, width, span), BF16),
             shape((2 * tok, 4), jnp.int32),
-            shape((4,), jnp.int32),
+            shape((5,), jnp.int32),
+            shape((groups, 2 * tok, span), BF16),
+            shape((2 * tok, w_restype.shape[1]), F32),
         ),
         [
             pltpu.VMEM((count, width), F32),
@@ -446,14 +483,17 @@
         ],
         "prepare",
         cost,
-        jnp.stack([lax.axis_index("row"), lax.axis_index("col")]).astype(jnp.int32),
+        jnp.stack([lax.axis_index(ROW), lax.axis_index(COL)]).astype(jnp.int32),
         pair_in[0],
         atom_counts,
         restype,
+        w_restype,
         far_out=(0,),
         scalar=(0,),
         scalar_out=(2,),
     )
+    same, bounds = lax.optimization_barrier((same, bounds))
+    other = lax.ppermute(same, "core", [(0, 1), (1, 0)])
     valid = pair_mask[0].astype(F32)
     mask = valid.reshape(groups, span)
 
@@ -478,9 +518,8 @@
     wide = pltpu.VMEM((devices * rows_out, LANES), F32)
     thin = pltpu.VMEM((devices * rows_back, LANES), F32)
     flat = shape((groups, width, span), BF16)
-    flat_wide = shape((groups, width, span), F32)
     here = pltpu.VMEM(flat.shape, BF16)
-    gates = pltpu.VMEM(flat.shape, F32)
+    gates = here
 
     def triangle(value):
         blocks = n_row
@@ -489,9 +528,9 @@
             back_shape,
             [
                 wide,
-                pltpu.VMEM((share, blocks * tok, blocks * LANES), BF16),
-                pltpu.VMEM((share, blocks * tok, blocks * LANES), BF16),
-                pltpu.VMEM((share, blocks * tok, blocks * LANES), F32),
+                pltpu.VMEM((share, blocks * tok, blocks * LANES // 2), BF16),
+                pltpu.VMEM((share, blocks * tok, blocks * LANES // 2), BF16),
+                pltpu.VMEM((share, blocks * tok, blocks * LANES // 2), F32),
                 thin,
             ],
             "triangle",
@@ -502,35 +541,37 @@
     send, sides = call(
         front_kernel,
         (send_shape, shape((width, 2 * tok), BF16)),
-        [wide, here, pltpu.SemaphoreType.DMA],
+        [wide, pltpu.VMEM((n_row, n_col * atom_feats.shape[1], atom_feats.shape[2]), BF16), here, pltpu.SemaphoreType.DMA],
         "front",
         cost,
         bounds,
-        feats,
+        same,
+        other,
         tokens,
+        embedded,
         w_atom,
-        w_restype,
         w_pair,
         plain,
+        chosen,
         mask,
         column(ln_tri[0]),
         side_weights(w_tri_in[0]),
-        far=(6,),
+        far=(7,),
         scalar=(0,),
     )
-    arrived = exchange(send, ("col", "row"))
+    arrived = exchange(send, COL + ROW)
     arrived, sides, pair_in, d_pair, valid, w_tri_in, w_tri_out, ln_tri, ln_tri_out, w_up, w_down, ln_trans = (
         lax.optimization_barrier(
             (arrived, sides, pair_in, d_pair, valid, w_tri_in, w_tri_out, ln_tri, ln_tri_out, w_up, w_down, ln_trans)
         )
     )
-    tri = exchange(triangle(arrived), ("row", "col"))
+    tri = exchange(triangle(arrived), ROW + COL)
     w_gates = w_tri_in[:, :, 4 * inner :].swapaxes(1, 2)
     w_outs = [by_owner(w_tri_out[u], u).T for u in range(2)]
     gains_out = [column(by_owner(ln_tri_out[u], u)) for u in range(2)]
     pair, gate = call(
         first_gate_kernel,
-        (flat, flat_wide),
+        (flat, flat),
         [pltpu.VMEM((count, width), F32), here, gates, pltpu.SemaphoreType.DMA((2,))],
         "first_gate",
         cost,
@@ -561,7 +602,7 @@
     ready, late = lax.optimization_barrier((ready, late))
     send, pair, gate = call(
         middle_kernel,
-        (send_shape, flat, flat_wide),
+        (send_shape, flat, flat),
         [thin, wide, here, gates, pltpu.SemaphoreType.DMA((2, groups))],
         "middle",
         cost,
@@ -571,8 +612,8 @@
         *ready,
         far=(1, 2),
     )
-    arrived = exchange(send, ("row", "col"))
-    tri = exchange(triangle(arrived), ("row", "col"))
+    arrived = exchange(send, ROW + COL)
+    tri = exchange(triangle(arrived), ROW + COL)
     grad, hidden, pair = call(
         last_kernel,
         (shape((expand, width), BF16), shape((groups, expand, span), BF16), flat),
@@ -600,7 +641,7 @@
         far_out=(0, 1, 2),
     )
     everyone = devices * lax.axis_size("rep")
-    grad = exchange(grad.reshape(everyone, expand // everyone, width), ("row", "col", "rep"))
+    grad = exchange(grad.reshape(everyone, expand // everyone, width), ROW + COL + ("rep",))
     result = call(
         down_kernel,
         shape((tok, tok, width), BF16),
@@ -615,28 +656,24 @@
 
 
 def solution(mesh):
+    rows, cols, reps = (mesh.shape[name] for name in ("row", "col", "rep"))
+    parts = Mesh(
+        mesh.devices.reshape(rows // 2, 2, cols // 2, 2, reps), ROW + COL + ("rep",)
+    )
+    pair = P("rep", ROW, COL, None)
     return jax.shard_map(
         local,
-        mesh=mesh,
+        mesh=parts,
         in_specs=(
-            P("rep", ("row", "col"), None),
-            P("rep", ("row", "col")),
+            P("rep", ROW + COL, None),
+            P("rep", ROW + COL),
             P("rep", None),
             P("rep", None),
-            P("rep", "row", "col", None),
-            P("rep", "row", "col"),
-            P(),
-            P(),
-            P(),
-            P(),
-            P(),
-            P(),
-            P(),
-            P(),
-            P(),
-            P(),
-            P("rep", "row", "col", None),
+            pair,
+            P("rep", ROW, COL),
+            *[P()] * 10,
+            pair,
         ),
-        out_specs=(P("rep", "row", "col", None), P(("row", "col", "rep"), None)),
+        out_specs=(pair, P(ROW + COL + ("rep",), None)),
         check_vma=False,
     )

time: 150 us -> 144 us (0.960)
  waiting for transfers between devices: 22.6 us -> 18.5 us
  Pallas kernels: 32.8 us -> 29.5 us
    all_to_all x3, waiting for transfers between devices: 22.6 us -> 17.5 us  [exchange(): return lax.all_to_all(value, axes, 0, 0, tiled=True)]
    pallas_call x10, Pallas kernels: 32.8 us -> 29.5 us  [call(): pl.pallas_call(kernel, out_shape=outs, in_specs=[pl.BlockSpec(memory_spac...]
    ppermute x0 -> x1, starting transfers between devices: none -> 2.04 us  [local(): other = lax.ppermute(same, 'core', [(0, 1), (1, 0)])]
  transfers between devices with their start and end apart: 3 -> 4, of which waited for: 3 -> 4; matrix products, arithmetic and copies ran while one was open for 2% -> 2% of each run, Pallas kernels for 7% -> 7%
where the time goes in v2:
time: 144 us; the launch traced here: 143 us
  blocking collectives  64.8 us (45%)
  Pallas kernels  29.5 us (20%)
  starting transfers between devices  22.2 us (15%)
  waiting for transfers between devices  18.5 us (13%)
  local copies, waits for them, and re-layouts  5.96 us (4%)
    all_to_all x3, blocking collectives, exchange(): return lax.all_to_all(value, axes, 0, 0, tiled=True)  64.8 us
    pallas_call x10, Pallas kernels, call(): pl.pallas_call(kernel, out_shape=outs, in_specs=[pl.BlockSpec(memory_spac...  29.5 us
    all_to_all x3, starting transfers between devices, exchange(): return lax.all_to_all(value, axes, 0, 0, tiled=True)  20.1 us
    all_to_all x3, waiting for transfers between devices, exchange(): return lax.all_to_all(value, axes, 0, 0, tiled=True)  17.5 us
    unnamed x37, local copies, waits for them, and re-layouts  3.66 us
  transfers between devices with their start and end apart: 4, of which 4 were waited for; matrix products, arithmetic and copies ran while one was open for 2% of the time, Pallas kernels for 7%

profile of v2, /device:TPU:1, one launch (start us, length us, event | category | flops | bytes accessed | tf_op | source)
XLA Modules:
  0.0 142.8 jit_solution(8245877626779260323)
XLA Ops:
  0.6 0.7 copy-done.7
  1.4 0.8 spread.1
  2.2 9.2 %all-to-all-start = ((bf16[32,48,128]{2,1,0:T(8,128)(2,1)}), bf16[32,48,128]{2,1,0:T(8,128)(2,1)S(1)}, u32[]{:S(2)}, u32[]{:S(2)}) async-start(bf16[32,48,128]{2,1,0:T(8,128)(2,1)} %spread.1), calls=%async_computation | async-start | bytes 786432 | tf_op jit(solution)/shard_map/all_to_all | solution.py:37
  11.5 2.9 %prepare.1 = (bf16[6,128,384]{2,1,0:T(8,128)(2,1)}, s32[96,4]{1,0:T(8,128)S(1)}, s32[5]{0:T(128)S(1)}, bf16[6,96,384]{2,1,0:T(8,128)(2,1)S(1)}, f32[96,384]{1,0:T(8,128)S(1)}) custom-call(s32[2]{0:T(128)S(1)} %pad_add_fusion.place, bf16[48,48,128]{2,1,0:T(8,128)(2,1)S(1)} %bitcast.58, s32[1,384]{1,0:T(1,128)S(1)} %copy-done.8, s32[1,384]{1,0:T(1,128)S(1)} %copy-done.9, ...), custom_call_target="tpu_custom_call" | custom-call | flops 400000000 | bytes 4194304 | tf_op jit(solution)/shard_map/prepare/pallas_call | solution.py:414
  14.5 6.6 %all-to-all-done = bf16[32,48,128]{2,1,0:T(8,128)(2,1)S(1)} async-done(((bf16[32,48,128]{2,1,0:T(8,128)(2,1)}), bf16[32,48,128]{2,1,0:T(8,128)(2,1)S(1)}, u32[]{:S(2)}, u32[]{:S(2)}) %all-to-all-start) | async-done | bytes 393248 | tf_op jit(solution)/shard_map/all_to_all | solution.py:37
  21.0 2.0 %collective-permute-start = (bf16[1536,128]{1,0:T(8,128)(2,1)S(1)}, bf16[1536,128]{1,0:T(8,128)(2,1)S(1)}, u32[]{:S(2)}, u32[]{:S(2)}) collective-permute-start(bf16[1536,128]{1,0:T(8,128)(2,1)S(1)} %bitcast.49), channel_id=1, source_target_pairs={{0,16},{16,0},{1,17},{17,1},{2,18},{18,2},{3,19},{19,3},{4,20},{20... | collective-permute-start | bytes 1179656 | tf_op jit(solution)/shard_map/ppermute | solution.py:496
  23.1 0.2 copy.54
  23.4 1.0 collective-permute-done.other
  24.5 3.9 %front.1 = (bf16[64,72,128]{2,1,0:T(8,128)(2,1)S(1)}, bf16[128,96]{1,0:T(8,128)(2,1)S(1)}) custom-call(s32[5]{0:T(128)S(1)} %get-tuple-element.44.bounds, bf16[1536,128]{1,0:T(8,128)(2,1)S(1)} %bitcast.50, bf16[1536,128]{1,0:T(8,128)(2,1)S(1)} %collective-permute-done.other, s32[96,4]{1,0:T(8,128)S(1)} %get-tuple-element.46.tokens, ...), custom_call_target="tpu_custom_call" | custom-call | flops 400000000 | bytes 4194304 | tf_op jit(solution)/shard_map/front/pallas_call | solution.py:414
  28.4 23.6 %all_to_all.30.x = bf16[64,72,128]{2,1,0:T(8,128)(2,1)S(1)} all-to-all(bf16[64,72,128]{2,1,0:T(8,128)(2,1)S(1)} %get-tuple-element.50), channel_id=1, replica_groups=mesh['x'=4,'core'=2,'y'=4,'zl'=2,'rep'=2] {'y','zl','x','core'}, dimensions={0} | all-to-all | bytes 2359296 | tf_op jit(solution)/shard_map/all_to_all | solution.py:37
  52.0 3.4 %triangle.2 = bf16[64,36,128]{2,1,0:T(8,128)(2,1)} custom-call(bf16[64,72,128]{2,1,0:T(8,128)(2,1)S(1)} %all_to_all.30.x), custom_call_target="tpu_custom_call" | custom-call | flops 400000000 | bytes 4194304 | tf_op jit(solution)/shard_map/triangle/pallas_call | solution.py:414
  55.4 4.9 %all-to-all-start.2 = ((bf16[64,36,128]{2,1,0:T(8,128)(2,1)}), bf16[64,36,128]{2,1,0:T(8,128)(2,1)S(1)}, u32[]{:S(2)}, u32[]{:S(2)}) async-start(bf16[64,36,128]{2,1,0:T(8,128)(2,1)} %triangle.2), calls=%async_computation.2 | async-start | bytes 1310720 | tf_op jit(solution)/shard_map/all_to_all | solution.py:37
  60.4 0.2 copy.42
  60.9 0.1 reshape_squeeze.14
  61.2 0.1 reshape_squeeze.12
  61.4 0.1 copy.43
  61.9 0.1 copy.53
  62.0 0.2 copy.52
  62.2 1.3 turn.1.d_pair
  64.0 3.5 %first_gate.1 = (bf16[6,128,384]{2,1,0:T(8,128)(2,1)}, bf16[6,128,384]{2,1,0:T(8,128)(2,1)}) custom-call(bf16[48,48,128]{2,1,0:T(8,128)(2,1)S(1)} %bitcast.59, bf16[128,96]{1,0:T(8,128)(2,1)S(1)} %get-tuple-element.54.sides, f32[128,384]{1,0:T(8,128)S(1)} %broadcast_in_dim.47.gain, bf16[128,128]{1,0:T(8,128)(2,1)S(1)} %get-tuple-element.89.w_gate), custom_call_target="tpu_custom_call" | custom-call | flops 400000000 | bytes 4194304 | tf_op jit(solution)/shard_map/first_gate/pallas_call | solution.py:414
  67.5 6.6 %all-to-all-done.2.tri = bf16[64,36,128]{2,1,0:T(8,128)(2,1)S(1)} async-done(((bf16[64,36,128]{2,1,0:T(8,128)(2,1)}), bf16[64,36,128]{2,1,0:T(8,128)(2,1)S(1)}, u32[]{:S(2)}, u32[]{:S(2)}) %all-to-all-start.2) | async-done | bytes 589856 | tf_op jit(solution)/shard_map/all_to_all | solution.py:37
  74.2 3.8 %middle.1 = (bf16[64,72,128]{2,1,0:T(8,128)(2,1)S(1)}, bf16[6,128,384]{2,1,0:T(8,128)(2,1)S(1)}, bf16[6,128,384]{2,1,0:T(8,128)(2,1)S(1)}) custom-call(bf16[64,36,128]{2,1,0:T(8,128)(2,1)S(1)} %all-to-all-done.2.tri, bf16[6,128,384]{2,1,0:T(8,128)(2,1)} %get-tuple-element.57.pair, bf16[6,128,384]{2,1,0:T(8,128)(2,1)} %get-tuple-element.58.gate, ...), custom_call_target="tpu_custom_call" | custom-call | flops 400000000 | bytes 4194304 | tf_op jit(solution)/shard_map/middle/pallas_call | solution.py:414
  77.9 23.4 %all_to_all.31.x = bf16[64,72,128]{2,1,0:T(8,128)(2,1)S(1)} all-to-all(bf16[64,72,128]{2,1,0:T(8,128)(2,1)S(1)} %get-tuple-element.72), channel_id=1, replica_groups=mesh['x'=4,'core'=2,'y'=4,'zl'=2,'rep'=2] {'x','core','y','zl'}, dimensions={0} | all-to-all | bytes 2359296 | tf_op jit(solution)/shard_map/all_to_all | solution.py:37
  101.4 2.6 %triangle.3 = bf16[64,36,128]{2,1,0:T(8,128)(2,1)S(1)} custom-call(bf16[64,72,128]{2,1,0:T(8,128)(2,1)S(1)} %all_to_all.31.x), custom_call_target="tpu_custom_call" | custom-call | flops 400000000 | bytes 4194304 | tf_op jit(solution)/shard_map/triangle/pallas_call | solution.py:414
  104.0 17.9 %all_to_all.32.tri = bf16[64,36,128]{2,1,0:T(8,128)(2,1)S(1)} all-to-all(bf16[64,36,128]{2,1,0:T(8,128)(2,1)S(1)} %triangle.3), channel_id=1, replica_groups=mesh['x'=4,'core'=2,'y'=4,'zl'=2,'rep'=2] {'x','core','y','zl'}, dimensions={0} | all-to-all | bytes 1179648 | tf_op jit(solution)/shard_map/all_to_all | solution.py:37
  121.8 4.4 %last.1 = (bf16[512,128]{1,0:T(8,128)(2,1)}, bf16[6,512,384]{2,1,0:T(8,128)(2,1)}, bf16[6,128,384]{2,1,0:T(8,128)(2,1)}) custom-call(bf16[64,36,128]{2,1,0:T(8,128)(2,1)S(1)} %all_to_all.32.tri, bf16[6,128,384]{2,1,0:T(8,128)(2,1)S(1)} %get-tuple-element.73.pair, bf16[6,128,384]{2,1,0:T(8,128)(2,1)S(1)} %get-tuple-element.74.gate, ...), custom_call_target="tpu_custom_call" | custom-call | flops 800000000 | bytes 4194304 | tf_op jit(solution)/shard_map/last/pallas_call | solution.py:414
  126.2 6.0 %all-to-all-start.5 = ((bf16[128,4,128]{2,1,0:T(4,128)(2,1)}), bf16[128,4,128]{2,1,0:T(4,128)(2,1)S(1)}, u32[]{:S(2)}, u32[]{:S(2)}) async-start(bf16[128,4,128]{2,1,0:T(4,128)(2,1)} %bitcast.67), calls=%async_computation.5 | async-start | bytes 262144 | tf_op jit(solution)/shard_map/all_to_all | solution.py:37
  132.2 1.7 %copy-done = bf16[6,512,384]{2,1,0:T(8,128)(2,1)S(1)} copy-done((bf16[6,512,384]{2,1,0:T(8,128)(2,1)S(1)}, bf16[6,512,384]{2,1,0:T(8,128)(2,1)}, u32[]{:S(2)}) %copy-start) | copy-done | bytes 2359320
  133.9 1.1 copy-done.1
  134.9 2.9 %down.1 = bf16[48,48,128]{2,1,0:T(8,128)(2,1)} custom-call(bf16[6,512,384]{2,1,0:T(8,128)(2,1)S(1)} %copy-done, bf16[6,128,384]{2,1,0:T(8,128)(2,1)S(1)} %copy-done.1, bf16[128,512]{1,0:T(8,128)(2,1)S(1)} %bitcast.52), custom_call_target="tpu_custom_call" | custom-call | flops 400000000 | bytes 4194304 | tf_op jit(solution)/shard_map/down/pallas_call | solution.py:414
  137.8 4.3 %all-to-all-done.5 = bf16[128,4,128]{2,1,0:T(4,128)(2,1)S(1)} async-done(((bf16[128,4,128]{2,1,0:T(4,128)(2,1)}), bf16[128,4,128]{2,1,0:T(4,128)(2,1)S(1)}, u32[]{:S(2)}, u32[]{:S(2)}) %all-to-all-start.5) | async-done | bytes 131104 | tf_op jit(solution)/shard_map/all_to_all | solution.py:37
  142.1 0.7 convert_reduce_fusion
  (64 shorter events, 1.6 us)
Async XLA Ops:
  0.6 0.7 copy-start.7
  1.3 10.2 %copy-start.5 = (bf16[1,48,48,128]{3,2,1,0:T(8,128)(2,1)S(1)}, bf16[1,48,48,128]{3,2,1,0:T(8,128)(2,1)}, u32[]{:S(2)}) copy-start(bf16[1,48,48,128]{3,2,1,0:T(8,128)(2,1)} %param.20) | copy-start | bytes 1769476
  1.3 10.2 %copy-start.6 = (bf16[32,384]{1,0:T(8,128)(2,1)S(1)}, bf16[32,384]{1,0:T(8,128)(2,1)}, u32[]{:S(2)}) copy-start(bf16[32,384]{1,0:T(8,128)(2,1)} %w_restype.1) | copy-start | bytes 73732
  1.3 10.2 %copy-start.8 = (s32[1,384]{1,0:T(1,128)S(1)}, s32[1,384]{1,0:T(1,128)}, u32[]{:S(2)}) copy-start(s32[1,384]{1,0:T(1,128)} %counts.1) | copy-start | bytes 4612
  1.3 10.2 %copy-start.9 = (s32[1,384]{1,0:T(1,128)S(1)}, s32[1,384]{1,0:T(1,128)}, u32[]{:S(2)}) copy-start(s32[1,384]{1,0:T(1,128)} %types.1) | copy-start | bytes 4612
  2.2 20.9 %copy-start.14 = (s32[1,48,48]{2,1,0:T(8,128)S(1)}, s32[1,48,48]{2,1,0:T(8,128)}, u32[]{:S(2)}) copy-start(s32[1,48,48]{2,1,0:T(8,128)} %param.21) | copy-start | bytes 27652
  2.2 18.8 %all-to-all-start = ((bf16[32,48,128]{2,1,0:T(8,128)(2,1)}), bf16[32,48,128]{2,1,0:T(8,128)(2,1)S(1)}, u32[]{:S(2)}, u32[]{:S(2)}) async-start(bf16[32,48,128]{2,1,0:T(8,128)(2,1)} %spread.1), calls=%async_computation | async-start | bytes 786432 | tf_op jit(solution)/shard_map/all_to_all | solution.py:37
  11.4 11.7 %slice-start = ((bf16[2,128,640]{2,1,0:T(8,128)(2,1)}), bf16[1,128,640]{2,1,0:T(8,128)(2,1)S(1)}, s32[]{:S(2)}) async-start(bf16[2,128,640]{2,1,0:T(8,128)(2,1)} %param.26), calls=%async_computation.6 | async-start | bytes 327680 | tf_op jit(solution)/shard_map/slice | solution.py:558
  11.5 11.8 %copy-start.15 = (f32[2,128]{1,0:T(2,128)S(1)}, f32[2,128]{1,0:T(2,128)}, u32[]{:S(2)}) copy-start(f32[2,128]{1,0:T(2,128)} %param.25) | copy-start | bytes 3076
  14.4 10.1 %copy-start.2 = (bf16[384,256]{1,0:T(8,128)(2,1)S(1)}, bf16[384,256]{1,0:T(8,128)(2,1)}, u32[]{:S(2)}) copy-start(bf16[384,256]{1,0:T(8,128)(2,1)} %w_pair.1) | copy-start | bytes 589828
  14.4 10.1 %copy-start.3 = (bf16[128,384]{1,0:T(8,128)(2,1)S(1)}, bf16[128,384]{1,0:T(8,128)(2,1)}, u32[]{:S(2)}) copy-start(bf16[128,384]{1,0:T(8,128)(2,1)} %w_atom.1) | copy-start | bytes 294916
  21.0 3.4 %collective-permute-start = (bf16[1536,128]{1,0:T(8,128)(2,1)S(1)}, bf16[1536,128]{1,0:T(8,128)(2,1)S(1)}, u32[]{:S(2)}, u32[]{:S(2)}) collective-permute-start(bf16[1536,128]{1,0:T(8,128)(2,1)S(1)} %bitcast.49), channel_id=1, source_target_pairs={{0,16},{16,0},{1,17},{17,1},{2,18},{18,2},{3,19},{19,3},{4,20},{20... | collective-permute-start | bytes 1179656 | tf_op jit(solution)/shard_map/ppermute | solution.py:496
  52.0 8.4 %copy-start.13 = (bf16[2,128,128]{2,1,0:T(8,128)(2,1)S(1)}, bf16[2,128,128]{2,1,0:T(8,128)(2,1)}, u32[]{:S(2)}) copy-start(bf16[2,128,128]{2,1,0:T(8,128)(2,1)} %param.28) | copy-start | bytes 196612
  55.4 5.0 %copy-start.10 = (bf16[2,128,640]{2,1,0:T(8,128)(2,1)S(1)}, bf16[2,128,640]{2,1,0:T(8,128)(2,1)}, u32[]{:S(2)}) copy-start(bf16[2,128,640]{2,1,0:T(8,128)(2,1)} %param.26) | copy-start | bytes 983044
  55.4 5.2 %copy-start.16 = (f32[2,128]{1,0:T(2,128)S(1)}, f32[2,128]{1,0:T(2,128)}, u32[]{:S(2)}) copy-start(f32[2,128]{1,0:T(2,128)} %param.27) | copy-start | bytes 3076
  55.4 6.4 %copy-start.12 = (bf16[512,128]{1,0:T(8,128)(2,1)S(1)}, bf16[512,128]{1,0:T(8,128)(2,1)}, u32[]{:S(2)}) copy-start(bf16[512,128]{1,0:T(8,128)(2,1)} %param.31) | copy-start | bytes 393220
  55.4 18.7 %all-to-all-start.2 = ((bf16[64,36,128]{2,1,0:T(8,128)(2,1)}), bf16[64,36,128]{2,1,0:T(8,128)(2,1)S(1)}, u32[]{:S(2)}, u32[]{:S(2)}) async-start(bf16[64,36,128]{2,1,0:T(8,128)(2,1)} %triangle.2), calls=%async_computation.2 | async-start | bytes 1310720 | tf_op jit(solution)/shard_map/all_to_all | solution.py:37
  60.4 1.6 %copy-start.11 = (bf16[128,1024]{1,0:T(8,128)(2,1)S(1)}, bf16[128,1024]{1,0:T(8,128)(2,1)}, u32[]{:S(2)}) copy-start(bf16[128,1024]{1,0:T(8,128)(2,1)} %param.30) | copy-start | bytes 786436
  60.6 1.6 %copy-start.4 = (bf16[1,48,48,128]{3,2,1,0:T(8,128)(2,1)S(1)}, bf16[1,48,48,128]{3,2,1,0:T(8,128)(2,1)}, u32[]{:S(2)}) copy-start(bf16[1,48,48,128]{3,2,1,0:T(8,128)(2,1)} %param.32) | copy-start | bytes 1769476
  62.2 1.6 %copy-start.17 = (f32[128]{0:T(128)S(1)}, f32[128]{0:T(128)}, u32[]{:S(2)}) copy-start(f32[128]{0:T(128)} %param.29) | copy-start | bytes 1540
  126.2 15.9 %all-to-all-start.5 = ((bf16[128,4,128]{2,1,0:T(4,128)(2,1)}), bf16[128,4,128]{2,1,0:T(4,128)(2,1)S(1)}, u32[]{:S(2)}, u32[]{:S(2)}) async-start(bf16[128,4,128]{2,1,0:T(4,128)(2,1)} %bitcast.67), calls=%async_computation.5 | async-start | bytes 262144 | tf_op jit(solution)/shard_map/all_to_all | solution.py:37
  132.2 1.7 %copy-start = (bf16[6,512,384]{2,1,0:T(8,128)(2,1)S(1)}, bf16[6,512,384]{2,1,0:T(8,128)(2,1)}, u32[]{:S(2)}) copy-start(bf16[6,512,384]{2,1,0:T(8,128)(2,1)} %get-tuple-element.80.hidden) | copy-start | bytes 7077892
  133.9 1.1 copy-start.1

commit v3 on v2

--- a/solution.py
+++ b/solution.py
@@ -10,8 +10,8 @@
 F32, BF16 = jnp.float32, jnp.bfloat16
 LANES = 128
 ROW, COL = ("x", "core"), ("y", "zl")
-TOGETHER = 2
-PARAMS = pltpu.CompilerParams(vmem_limit_bytes=20 * 2**20)
+FRONT, LATE = 6, 3
+PARAMS = pltpu.CompilerParams(vmem_limit_bytes=32 * 2**20)
 
 
 def nt(a, b):
@@ -56,31 +56,18 @@
                 ]
 
 
-def beside(array, first):
-    return jnp.concatenate([array[first + n] for n in range(TOGETHER)], axis=1)
-
-
-def widened(gain):
-    return jnp.concatenate([gain[...]] * TOGETHER, axis=1)
+def beside(array, first, count):
+    return jnp.concatenate([array[first + n] for n in range(count)], axis=1)
+
+
+def widened(gain, count):
+    return jnp.concatenate([gain[...]] * count, axis=1)
 
 
 def apart(array, first, value):
-    span = value.shape[1] // TOGETHER
-    for n in range(TOGETHER):
+    span = array.shape[2]
+    for n in range(value.shape[1] // span):
         array[first + n] = value[:, n * span : (n + 1) * span]
-
-
-def spread_kernel(value, out, copies, sems):
-    several = copies.shape[0]
-    copies[...] = jnp.broadcast_to(value[...], copies.shape)
-    moves = [
-        pltpu.make_async_copy(copies, out.at[pl.ds(n * several, several)], sems.at[n])
-        for n in range(out.shape[0] // several)
-    ]
-    for move in moves:
-        move.start()
-    for move in moves:
-        move.wait()
 
 
 def prepare_kernel(chunk, place, pair_in, counts, types, w_restype, plain, tokens, bounds, chosen, embedded, wide, made, sem):
@@ -197,9 +184,9 @@
     sides[...] = jnp.concatenate([left, right], 0).T.astype(BF16)
     move.wait()
 
-    for g in range(0, groups, TOGETHER):
-        block = beside(pair_in, g).astype(F32) + nn(sides[...], beside(chosen, g))
-        normed = norm(block.astype(BF16).astype(F32), widened(gain), 0).astype(BF16)
+    for g in range(0, groups, FRONT):
+        block = beside(pair_in, g, FRONT).astype(F32) + nn(sides[...], beside(chosen, g, FRONT))
+        normed = norm(block.astype(BF16).astype(F32), widened(gain, FRONT), 0).astype(BF16)
         send_groups(g, normed, weights[...], mask, wide, devices)
     send[...] = wide[...].astype(BF16).reshape(send.shape)
 
@@ -241,10 +228,11 @@
     return out
 
 
-def triangle_kernel(tok, blocks, x, out, xf, lhs, rhs, moved, of):
+def triangle_kernel(tok, blocks, x, out, xf, lhs, rhs, moved, of, made, sems):
     devices = x.shape[0]
     share = out.shape[1] * LANES // (tok * tok)
     parts = 3
+    each = out.shape[1]
     groups = tok // 8
     kinds = 2 * share
     side_len = blocks * tok
@@ -283,6 +271,7 @@
         product = nt(lhs[e], rhs[e]).astype(BF16)
         moved[e] = nn(product, place)
 
+    leaving = []
     for b in range(blocks):
         at, start = b // 2 * LANES, b % 2 * half
         for e in range(share):
@@ -298,7 +287,17 @@
             for q in range(parts):
                 base = b * blocks * out.shape[1] + e * parts + q
                 of[pl.ds(base, tok, stride=share * parts), :] = tiles[q]
-    out[...] = of[...].astype(BF16).reshape(out.shape)
+        if made is None:
+            continue
+        here = pl.ds(b * blocks, blocks)
+        rows = slice(b * blocks * each, (b + 1) * blocks * each)
+        made[here] = of[rows].astype(BF16).reshape(blocks, each, LANES)
+        leaving.append(pltpu.make_async_copy(made.at[here], out.at[here], sems.at[b]))
+        leaving[-1].start()
+    for copy in leaving:
+        copy.wait()
+    if made is None:
+        out[...] = of[...].astype(BF16).reshape(out.shape)
 
 
 def updated_groups(first, each, devices, wide, gain, w_out, pair, gate):
@@ -308,16 +307,16 @@
         jnp.concatenate(
             [
                 wide[pl.ds((g * share + e) * parts + q, devices, stride=each), :]
-                for g in range(first, first + TOGETHER)
+                for g in range(first, first + LATE)
                 for q in range(parts)
             ],
             axis=1,
         )
         for e in range(share)
     ]
-    normed = norm(jnp.concatenate(tiles, axis=0), widened(gain), 0).astype(BF16)
-    change = beside(gate, first).astype(F32) * nn(w_out[...], normed)
-    return (beside(pair, first).astype(F32) + change).astype(BF16)
+    normed = norm(jnp.concatenate(tiles, axis=0), widened(gain, LATE), 0).astype(BF16)
+    change = beside(gate, first, LATE).astype(F32) * nn(w_out[...], normed)
+    return (beside(pair, first, LATE).astype(F32) + change).astype(BF16)
 
 
 def middle_kernel(tri, pair, gate, gain_out, w_out, mask, gain, weights, w_gate, send, pair_new, gate_new, thin, wide, here, gates, sems):
@@ -334,13 +333,13 @@
         for move in both:
             move.start()
     thin[...] = tri[...].astype(F32).reshape(thin.shape)
-    for g in range(0, groups, TOGETHER):
-        for both in moves[g : g + TOGETHER]:
+    for g in range(0, groups, LATE):
+        for both in moves[g : g + LATE]:
             for move in both:
                 move.wait()
         block = updated_groups(g, each, devices, thin, gain_out, w_out, here, gates)
         apart(pair_new, g, block)
-        normed = norm(block.astype(F32), widened(gain), 0).astype(BF16)
+        normed = norm(block.astype(F32), widened(gain, LATE), 0).astype(BF16)
         send_groups(g, normed, weights[...], mask, wide, devices)
         apart(gate_new, g, sigmoid(nn(w_gate[...], normed)).astype(BF16))
     send[...] = wide[...].astype(BF16).reshape(send.shape)
@@ -354,15 +353,15 @@
     thin[...] = tri[...].astype(F32).reshape(thin.shape)
     expand = total.shape[0]
     leaving = []
-    for g in range(0, groups, TOGETHER):
+    for g in range(0, groups, LATE):
         block = updated_groups(g, each, devices, thin, gain_out, w_out, pair, gate)
         apart(pairs, g, block)
-        normed = norm(block.astype(F32), widened(gain), 0).astype(BF16)
+        normed = norm(block.astype(F32), widened(gain, LATE), 0).astype(BF16)
         up = nn(w_up[...], normed)
         first = up[:expand]
         made = (first * sigmoid(first) * up[expand:]).astype(BF16)
         apart(units, g, made)
-        for n in range(g, g + TOGETHER):
+        for n in range(g, g + LATE):
             for copy in (
                 pltpu.make_async_copy(pairs.at[n], pair_new.at[n], outs.at[0, n]),
                 pltpu.make_async_copy(units.at[n], hidden.at[n], outs.at[1, n]),
@@ -371,7 +370,7 @@
                 leaving.append(copy)
         if g == 0:
             move.wait()
-        part = nn(made, there[g * span : (g + TOGETHER) * span, :])
+        part = nn(made, there[g * span : (g + LATE) * span, :])
         total[...] = part if g == 0 else total[...] + part
     small[...] = total[...].astype(BF16)
     leaving.append(pltpu.make_async_copy(small, grad, sems.at[1]))
@@ -456,15 +455,7 @@
     shape = jax.ShapeDtypeStruct
     cost = 400 * 10**6
     half = devices // 2
-    spread = call(
-        spread_kernel,
-        shape((half,) + atom_feats.shape[1:], BF16),
-        [pltpu.VMEM((n_row,) + atom_feats.shape[1:], BF16), pltpu.SemaphoreType.DMA((half // n_row,))],
-        "spread",
-        cost // 100,
-        atom_feats[0],
-        far_out=(0,),
-    )
+    spread = jnp.broadcast_to(atom_feats, (half,) + atom_feats.shape[1:])
     same = exchange(spread, ("x", "y", "zl")).reshape(-1, atom_feats.shape[-1])
 
     plain, tokens, bounds, chosen, embedded = call(
@@ -521,10 +512,14 @@
     here = pltpu.VMEM(flat.shape, BF16)
     gates = here
 
-    def triangle(value):
+    def triangle(value, leaves):
         blocks = n_row
+        kernel = functools.partial(triangle_kernel, tok, blocks)
+        if not leaves:
+            kernel = lambda *refs: triangle_kernel(tok, blocks, *refs, None, None)
+        extra = [pltpu.VMEM(back_shape.shape, BF16), pltpu.SemaphoreType.DMA((blocks,))]
         return call(
-            functools.partial(triangle_kernel, tok, blocks),
+            kernel,
             back_shape,
             [
                 wide,
@@ -532,10 +527,12 @@
                 pltpu.VMEM((share, blocks * tok, blocks * LANES // 2), BF16),
                 pltpu.VMEM((share, blocks * tok, blocks * LANES // 2), F32),
                 thin,
+                *(extra if leaves else []),
             ],
             "triangle",
             cost,
             value,
+            far_out=(0,) if leaves else (),
         )
 
     send, sides = call(
@@ -565,7 +562,7 @@
             (arrived, sides, pair_in, d_pair, valid, w_tri_in, w_tri_out, ln_tri, ln_tri_out, w_up, w_down, ln_trans)
         )
     )
-    tri = exchange(triangle(arrived), ROW + COL)
+    tri = exchange(triangle(arrived, True), ROW + COL)
     w_gates = w_tri_in[:, :, 4 * inner :].swapaxes(1, 2)
     w_outs = [by_owner(w_tri_out[u], u).T for u in range(2)]
     gains_out = [column(by_owner(ln_tri_out[u], u)) for u in range(2)]
@@ -613,7 +610,7 @@
         far=(1, 2),
     )
     arrived = exchange(send, ROW + COL)
-    tri = exchange(triangle(arrived), ROW + COL)
+    tri = exchange(triangle(arrived, False), ROW + COL)
     grad, hidden, pair = call(
         last_kernel,
         (shape((expand, width), BF16), shape((groups, expand, span), BF16), flat),

time: 144 us -> 143 us (level)
  Pallas kernels: 29.5 us -> 27.5 us
    pallas_call x10 -> x9, Pallas kernels: 29.5 us -> 27.5 us  [call(): pl.pallas_call(kernel, out_shape=outs, in_specs=[pl.BlockSpec(memory_spac...]
    broadcast_in_dim x0 -> x1, local copies, waits for them, and re-layouts: none -> 1.56 us  [local(): spread = jnp.broadcast_to(atom_feats, (half,) + atom_feats.shape[1:])]
    unnamed x37 -> x35, local copies, waits for them, and re-layouts: 3.66 us -> 2.97 us
where the time goes in v3:
time: 143 us; the launch traced here: 142 us
  blocking collectives  65 us (45%)
  Pallas kernels  27.5 us (19%)
  starting transfers between devices  22.3 us (16%)
  waiting for transfers between devices  18.5 us (13%)
  local copies, waits for them, and re-layouts  6.83 us (5%)
    all_to_all x3, blocking collectives, exchange(): return lax.all_to_all(value, axes, 0, 0, tiled=True)  65 us
    pallas_call x9, Pallas kernels, call(): pl.pallas_call(kernel, out_shape=outs, in_specs=[pl.BlockSpec(memory_spac...  27.5 us
    all_to_all x3, starting transfers between devices, exchange(): return lax.all_to_all(value, axes, 0, 0, tiled=True)  20.3 us
    all_to_all x3, waiting for transfers between devices, exchange(): return lax.all_to_all(value, axes, 0, 0, tiled=True)  17.5 us
    unnamed x35, local copies, waits for them, and re-layouts  2.97 us
  transfers between devices with their start and end apart: 4, of which 4 were waited for; matrix products, arithmetic and copies ran while one was open for 2% of the time, Pallas kernels for 7%

profile of v3, /device:TPU:1, one launch (start us, length us, event | category | flops | bytes accessed | tf_op | source)
XLA Modules:
  0.0 142.1 jit_solution(12424453202119198852)
XLA Ops:
  0.7 1.6 %broadcast_in_dim.52 = bf16[32,48,128]{2,1,0:T(8,128)(2,1)} broadcast(bf16[48,128]{1,0:T(8,128)(2,1)} %bitcast.72), dimensions={1,2} | broadcast | bytes 405504 | tf_op jit(solution)/shard_map/broadcast_in_dim | solution.py:458
  2.2 9.4 %all-to-all-start = ((bf16[32,48,128]{2,1,0:T(8,128)(2,1)}), bf16[32,48,128]{2,1,0:T(8,128)(2,1)S(1)}, u32[]{:S(2)}, u32[]{:S(2)}) async-start(bf16[32,48,128]{2,1,0:T(8,128)(2,1)} %broadcast_in_dim.52), calls=%async_computation | async-start | bytes 786432 | tf_op jit(solution)/shard_map/all_to_all | solution.py:37
  11.7 2.9 %prepare.1 = (bf16[6,128,384]{2,1,0:T(8,128)(2,1)}, s32[96,4]{1,0:T(8,128)S(1)}, s32[5]{0:T(128)S(1)}, bf16[6,96,384]{2,1,0:T(8,128)(2,1)S(1)}, f32[96,384]{1,0:T(8,128)S(1)}) custom-call(s32[2]{0:T(128)S(1)} %pad_add_fusion.place, bf16[48,48,128]{2,1,0:T(8,128)(2,1)S(1)} %bitcast.58, s32[1,384]{1,0:T(1,128)S(1)} %copy-done.7, s32[1,384]{1,0:T(1,128)S(1)} %copy-done.8, ...), custom_call_target="tpu_custom_call" | custom-call | flops 400000000 | bytes 4194304 | tf_op jit(solution)/shard_map/prepare/pallas_call | solution.py:413
  14.6 6.6 %all-to-all-done = bf16[32,48,128]{2,1,0:T(8,128)(2,1)S(1)} async-done(((bf16[32,48,128]{2,1,0:T(8,128)(2,1)}), bf16[32,48,128]{2,1,0:T(8,128)(2,1)S(1)}, u32[]{:S(2)}, u32[]{:S(2)}) %all-to-all-start) | async-done | bytes 393248 | tf_op jit(solution)/shard_map/all_to_all | solution.py:37
  21.2 2.0 %collective-permute-start = (bf16[1536,128]{1,0:T(8,128)(2,1)S(1)}, bf16[1536,128]{1,0:T(8,128)(2,1)S(1)}, u32[]{:S(2)}, u32[]{:S(2)}) collective-permute-start(bf16[1536,128]{1,0:T(8,128)(2,1)S(1)} %bitcast.49), channel_id=1, source_target_pairs={{0,16},{16,0},{1,17},{17,1},{2,18},{18,2},{3,19},{19,3},{4,20},{20... | collective-permute-start | bytes 1179656 | tf_op jit(solution)/shard_map/ppermute | solution.py:487
  23.3 0.2 copy.54
  23.6 1.0 collective-permute-done.other
  24.7 3.6 %front.1 = (bf16[64,72,128]{2,1,0:T(8,128)(2,1)S(1)}, bf16[128,96]{1,0:T(8,128)(2,1)S(1)}) custom-call(s32[5]{0:T(128)S(1)} %get-tuple-element.44.bounds, bf16[1536,128]{1,0:T(8,128)(2,1)S(1)} %bitcast.50, bf16[1536,128]{1,0:T(8,128)(2,1)S(1)} %collective-permute-done.other, s32[96,4]{1,0:T(8,128)S(1)} %get-tuple-element.46.tokens, ...), custom_call_target="tpu_custom_call" | custom-call | flops 400000000 | bytes 4194304 | tf_op jit(solution)/shard_map/front/pallas_call | solution.py:413
  28.3 23.6 %all_to_all.30.x = bf16[64,72,128]{2,1,0:T(8,128)(2,1)S(1)} all-to-all(bf16[64,72,128]{2,1,0:T(8,128)(2,1)S(1)} %get-tuple-element.50), channel_id=1, replica_groups=mesh['x'=4,'core'=2,'y'=4,'zl'=2,'rep'=2] {'y','zl','x','core'}, dimensions={0} | all-to-all | bytes 2359296 | tf_op jit(solution)/shard_map/all_to_all | solution.py:37
  51.8 3.3 %triangle.2 = bf16[64,36,128]{2,1,0:T(8,128)(2,1)} custom-call(bf16[64,72,128]{2,1,0:T(8,128)(2,1)S(1)} %all_to_all.30.x), custom_call_target="tpu_custom_call" | custom-call | flops 400000000 | bytes 4194304 | tf_op jit(solution)/shard_map/triangle/pallas_call | solution.py:413
  55.2 4.9 %all-to-all-start.2 = ((bf16[64,36,128]{2,1,0:T(8,128)(2,1)}), bf16[64,36,128]{2,1,0:T(8,128)(2,1)S(1)}, u32[]{:S(2)}, u32[]{:S(2)}) async-start(bf16[64,36,128]{2,1,0:T(8,128)(2,1)} %triangle.2), calls=%async_computation.2 | async-start | bytes 1310720 | tf_op jit(solution)/shard_map/all_to_all | solution.py:37
  60.2 0.2 copy.42
  60.6 0.1 reshape_squeeze.14
  60.7 0.1 copy.49
  61.0 0.1 reshape_squeeze.12
  61.1 0.1 copy.43
  61.6 0.1 copy.53
  61.7 0.2 copy.52
  62.0 1.3 turn.1.d_pair
  63.8 3.5 %first_gate.1 = (bf16[6,128,384]{2,1,0:T(8,128)(2,1)}, bf16[6,128,384]{2,1,0:T(8,128)(2,1)}) custom-call(bf16[48,48,128]{2,1,0:T(8,128)(2,1)S(1)} %bitcast.59, bf16[128,96]{1,0:T(8,128)(2,1)S(1)} %get-tuple-element.54.sides, f32[128,384]{1,0:T(8,128)S(1)} %broadcast_in_dim.56.gain, bf16[128,128]{1,0:T(8,128)(2,1)S(1)} %get-tuple-element.89.w_gate), custom_call_target="tpu_custom_call" | custom-call | flops 400000000 | bytes 4194304 | tf_op jit(solution)/shard_map/first_gate/pallas_call | solution.py:413
  67.3 6.6 %all-to-all-done.2.tri = bf16[64,36,128]{2,1,0:T(8,128)(2,1)S(1)} async-done(((bf16[64,36,128]{2,1,0:T(8,128)(2,1)}), bf16[64,36,128]{2,1,0:T(8,128)(2,1)S(1)}, u32[]{:S(2)}, u32[]{:S(2)}) %all-to-all-start.2) | async-done | bytes 589856 | tf_op jit(solution)/shard_map/all_to_all | solution.py:37
  73.9 3.5 %middle.1 = (bf16[64,72,128]{2,1,0:T(8,128)(2,1)S(1)}, bf16[6,128,384]{2,1,0:T(8,128)(2,1)S(1)}, bf16[6,128,384]{2,1,0:T(8,128)(2,1)S(1)}) custom-call(bf16[64,36,128]{2,1,0:T(8,128)(2,1)S(1)} %all-to-all-done.2.tri, bf16[6,128,384]{2,1,0:T(8,128)(2,1)} %get-tuple-element.57.pair, bf16[6,128,384]{2,1,0:T(8,128)(2,1)} %get-tuple-element.58.gate, ...), custom_call_target="tpu_custom_call" | custom-call | flops 400000000 | bytes 4194304 | tf_op jit(solution)/shard_map/middle/pallas_call | solution.py:413
  77.4 23.6 %all_to_all.31.refs_0_ = bf16[64,72,128]{2,1,0:T(8,128)(2,1)S(1)} all-to-all(bf16[64,72,128]{2,1,0:T(8,128)(2,1)S(1)} %get-tuple-element.72), channel_id=1, replica_groups=mesh['x'=4,'core'=2,'y'=4,'zl'=2,'rep'=2] {'x','core','y','zl'}, dimensions={0} | all-to-all | bytes 2359296 | tf_op jit(solution)/shard_map/all_to_all | solution.py:37
  101.0 2.6 %triangle.3 = bf16[64,36,128]{2,1,0:T(8,128)(2,1)S(1)} custom-call(bf16[64,72,128]{2,1,0:T(8,128)(2,1)S(1)} %all_to_all.31.refs_0_), custom_call_target="tpu_custom_call" | custom-call | flops 400000000 | bytes 4194304 | tf_op jit(solution)/shard_map/triangle/pallas_call | solution.py:413
  103.5 17.9 %all_to_all.32.tri = bf16[64,36,128]{2,1,0:T(8,128)(2,1)S(1)} all-to-all(bf16[64,36,128]{2,1,0:T(8,128)(2,1)S(1)} %triangle.3), channel_id=1, replica_groups=mesh['x'=4,'core'=2,'y'=4,'zl'=2,'rep'=2] {'x','core','y','zl'}, dimensions={0} | all-to-all | bytes 1179648 | tf_op jit(solution)/shard_map/all_to_all | solution.py:37
  121.4 4.1 %last.1 = (bf16[512,128]{1,0:T(8,128)(2,1)}, bf16[6,512,384]{2,1,0:T(8,128)(2,1)}, bf16[6,128,384]{2,1,0:T(8,128)(2,1)}) custom-call(bf16[64,36,128]{2,1,0:T(8,128)(2,1)S(1)} %all_to_all.32.tri, bf16[6,128,384]{2,1,0:T(8,128)(2,1)S(1)} %get-tuple-element.73.pair, bf16[6,128,384]{2,1,0:T(8,128)(2,1)S(1)} %get-tuple-element.74.gate, ...), custom_call_target="tpu_custom_call" | custom-call | flops 800000000 | bytes 4194304 | tf_op jit(solution)/shard_map/last/pallas_call | solution.py:413
  125.5 6.0 %all-to-all-start.5 = ((bf16[128,4,128]{2,1,0:T(4,128)(2,1)}), bf16[128,4,128]{2,1,0:T(4,128)(2,1)S(1)}, u32[]{:S(2)}, u32[]{:S(2)}) async-start(bf16[128,4,128]{2,1,0:T(4,128)(2,1)} %bitcast.66), calls=%async_computation.5 | async-start | bytes 262144 | tf_op jit(solution)/shard_map/all_to_all | solution.py:37
  131.5 1.7 %copy-done = bf16[6,512,384]{2,1,0:T(8,128)(2,1)S(1)} copy-done((bf16[6,512,384]{2,1,0:T(8,128)(2,1)S(1)}, bf16[6,512,384]{2,1,0:T(8,128)(2,1)}, u32[]{:S(2)}) %copy-start) | copy-done | bytes 2359320
  133.1 1.1 copy-done.1
  134.2 2.9 %down.1 = bf16[48,48,128]{2,1,0:T(8,128)(2,1)} custom-call(bf16[6,512,384]{2,1,0:T(8,128)(2,1)S(1)} %copy-done, bf16[6,128,384]{2,1,0:T(8,128)(2,1)S(1)} %copy-done.1, bf16[128,512]{1,0:T(8,128)(2,1)S(1)} %bitcast.52), custom_call_target="tpu_custom_call" | custom-call | flops 400000000 | bytes 4194304 | tf_op jit(solution)/shard_map/down/pallas_call | solution.py:413
  137.1 4.3 %all-to-all-done.5 = bf16[128,4,128]{2,1,0:T(4,128)(2,1)S(1)} async-done(((bf16[128,4,128]{2,1,0:T(4,128)(2,1)}), bf16[128,4,128]{2,1,0:T(4,128)(2,1)S(1)}, u32[]{:S(2)}, u32[]{:S(2)}) %all-to-all-start.5) | async-done | bytes 131104 | tf_op jit(solution)/shard_map/all_to_all | solution.py:37
  141.4 0.7 convert_reduce_fusion
  (62 shorter events, 1.4 us)
Async XLA Ops:
  0.6 11.1 %copy-start.5 = (bf16[1,48,48,128]{3,2,1,0:T(8,128)(2,1)S(1)}, bf16[1,48,48,128]{3,2,1,0:T(8,128)(2,1)}, u32[]{:S(2)}) copy-start(bf16[1,48,48,128]{3,2,1,0:T(8,128)(2,1)} %param.20) | copy-start | bytes 1769476
  0.6 11.1 %copy-start.6 = (bf16[32,384]{1,0:T(8,128)(2,1)S(1)}, bf16[32,384]{1,0:T(8,128)(2,1)}, u32[]{:S(2)}) copy-start(bf16[32,384]{1,0:T(8,128)(2,1)} %w_restype.1) | copy-start | bytes 73732
  0.7 11.1 %copy-start.8 = (s32[1,384]{1,0:T(1,128)S(1)}, s32[1,384]{1,0:T(1,128)}, u32[]{:S(2)}) copy-start(s32[1,384]{1,0:T(1,128)} %types.1) | copy-start | bytes 4612
  0.7 11.0 %copy-start.7 = (s32[1,384]{1,0:T(1,128)S(1)}, s32[1,384]{1,0:T(1,128)}, u32[]{:S(2)}) copy-start(s32[1,384]{1,0:T(1,128)} %counts.1) | copy-start | bytes 4612
  2.2 21.0 %copy-start.13 = (s32[1,48,48]{2,1,0:T(8,128)S(1)}, s32[1,48,48]{2,1,0:T(8,128)}, u32[]{:S(2)}) copy-start(s32[1,48,48]{2,1,0:T(8,128)} %param.21) | copy-start | bytes 27652
  2.2 19.0 %all-to-all-start = ((bf16[32,48,128]{2,1,0:T(8,128)(2,1)}), bf16[32,48,128]{2,1,0:T(8,128)(2,1)S(1)}, u32[]{:S(2)}, u32[]{:S(2)}) async-start(bf16[32,48,128]{2,1,0:T(8,128)(2,1)} %broadcast_in_dim.52), calls=%async_computation | async-start | bytes 786432 | tf_op jit(solution)/shard_map/all_to_all | solution.py:37
  11.6 11.7 %slice-start = ((bf16[2,128,640]{2,1,0:T(8,128)(2,1)}), bf16[1,128,640]{2,1,0:T(8,128)(2,1)S(1)}, s32[]{:S(2)}) async-start(bf16[2,128,640]{2,1,0:T(8,128)(2,1)} %param.26), calls=%async_computation.6 | async-start | bytes 327680 | tf_op jit(solution)/shard_map/slice | solution.py:555
  11.7 11.8 %copy-start.14 = (f32[2,128]{1,0:T(2,128)S(1)}, f32[2,128]{1,0:T(2,128)}, u32[]{:S(2)}) copy-start(f32[2,128]{1,0:T(2,128)} %param.25) | copy-start | bytes 3076
  14.6 10.1 %copy-start.2 = (bf16[384,256]{1,0:T(8,128)(2,1)S(1)}, bf16[384,256]{1,0:T(8,128)(2,1)}, u32[]{:S(2)}) copy-start(bf16[384,256]{1,0:T(8,128)(2,1)} %w_pair.1) | copy-start | bytes 589828
  14.6 10.1 %copy-start.3 = (bf16[128,384]{1,0:T(8,128)(2,1)S(1)}, bf16[128,384]{1,0:T(8,128)(2,1)}, u32[]{:S(2)}) copy-start(bf16[128,384]{1,0:T(8,128)(2,1)} %w_atom.1) | copy-start | bytes 294916
  21.2 3.4 %collective-permute-start = (bf16[1536,128]{1,0:T(8,128)(2,1)S(1)}, bf16[1536,128]{1,0:T(8,128)(2,1)S(1)}, u32[]{:S(2)}, u32[]{:S(2)}) collective-permute-start(bf16[1536,128]{1,0:T(8,128)(2,1)S(1)} %bitcast.49), channel_id=1, source_target_pairs={{0,16},{16,0},{1,17},{17,1},{2,18},{18,2},{3,19},{19,3},{4,20},{20... | collective-permute-start | bytes 1179656 | tf_op jit(solution)/shard_map/ppermute | solution.py:487
  51.8 8.3 %copy-start.12 = (bf16[2,128,128]{2,1,0:T(8,128)(2,1)S(1)}, bf16[2,128,128]{2,1,0:T(8,128)(2,1)}, u32[]{:S(2)}) copy-start(bf16[2,128,128]{2,1,0:T(8,128)(2,1)} %param.28) | copy-start | bytes 196612
  55.1 5.0 %copy-start.9 = (bf16[2,128,640]{2,1,0:T(8,128)(2,1)S(1)}, bf16[2,128,640]{2,1,0:T(8,128)(2,1)}, u32[]{:S(2)}) copy-start(bf16[2,128,640]{2,1,0:T(8,128)(2,1)} %param.26) | copy-start | bytes 983044
  55.2 5.3 %copy-start.15 = (f32[2,128]{1,0:T(2,128)S(1)}, f32[2,128]{1,0:T(2,128)}, u32[]{:S(2)}) copy-start(f32[2,128]{1,0:T(2,128)} %param.27) | copy-start | bytes 3076
  55.2 6.4 %copy-start.11 = (bf16[512,128]{1,0:T(8,128)(2,1)S(1)}, bf16[512,128]{1,0:T(8,128)(2,1)}, u32[]{:S(2)}) copy-start(bf16[512,128]{1,0:T(8,128)(2,1)} %param.31) | copy-start | bytes 393220
  55.2 18.7 %all-to-all-start.2 = ((bf16[64,36,128]{2,1,0:T(8,128)(2,1)}), bf16[64,36,128]{2,1,0:T(8,128)(2,1)S(1)}, u32[]{:S(2)}, u32[]{:S(2)}) async-start(bf16[64,36,128]{2,1,0:T(8,128)(2,1)} %triangle.2), calls=%async_computation.2 | async-start | bytes 1310720 | tf_op jit(solution)/shard_map/all_to_all | solution.py:37
  60.1 1.6 %copy-start.10 = (bf16[128,1024]{1,0:T(8,128)(2,1)S(1)}, bf16[128,1024]{1,0:T(8,128)(2,1)}, u32[]{:S(2)}) copy-start(bf16[128,1024]{1,0:T(8,128)(2,1)} %param.30) | copy-start | bytes 786436
  60.4 1.6 %copy-start.4 = (bf16[1,48,48,128]{3,2,1,0:T(8,128)(2,1)S(1)}, bf16[1,48,48,128]{3,2,1,0:T(8,128)(2,1)}, u32[]{:S(2)}) copy-start(bf16[1,48,48,128]{3,2,1,0:T(8,128)(2,1)} %param.32) | copy-start | bytes 1769476
  62.0 1.6 %copy-start.16 = (f32[128]{0:T(128)S(1)}, f32[128]{0:T(128)}, u32[]{:S(2)}) copy-start(f32[128]{0:T(128)} %param.29) | copy-start | bytes 1540
  125.5 15.9 %all-to-all-start.5 = ((bf16[128,4,128]{2,1,0:T(4,128)(2,1)}), bf16[128,4,128]{2,1,0:T(4,128)(2,1)S(1)}, u32[]{:S(2)}, u32[]{:S(2)}) async-start(bf16[128,4,128]{2,1,0:T(4,128)(2,1)} %bitcast.66), calls=%async_computation.5 | async-start | bytes 262144 | tf_op jit(solution)/shard_map/all_to_all | solution.py:37
  131.5 1.7 %copy-start = (bf16[6,512,384]{2,1,0:T(8,128)(2,1)S(1)}, bf16[6,512,384]{2,1,0:T(8,128)(2,1)}, u32[]{:S(2)}) copy-start(bf16[6,512,384]{2,1,0:T(8,128)(2,1)} %get-tuple-element.80.hidden) | copy-start | bytes 7077892
  133.1 1.1 copy-start.1

commit v4 on v3

--- a/solution.py
+++ b/solution.py
@@ -267,12 +267,13 @@
     block, spot = target // half, target % half
     wanted = (spot % 8) * tok + block * groups + spot // 8
     place = jnp.where((source == wanted) & (spot < tok), 1.0, 0.0).astype(BF16)
-    for e in range(share):
-        product = nt(lhs[e], rhs[e]).astype(BF16)
-        moved[e] = nn(product, place)
-
+    products = [nt(lhs[e], rhs[e]).astype(BF16) for e in range(share)]
     leaving = []
     for b in range(blocks):
+        if b % (blocks // 2) == 0:
+            some = slice(b * half, (b + blocks // 2) * half)
+            for e in range(share):
+                moved[e, :, some] = nn(products[e], place[:, some])
         at, start = b // 2 * LANES, b % 2 * half
         for e in range(share):
             tiles = [None] * parts
@@ -300,7 +301,7 @@
         out[...] = of[...].astype(BF16).reshape(out.shape)
 
 
-def updated_groups(first, each, devices, wide, gain, w_out, pair, gate):
+def change_of(first, each, devices, wide, gain, w_out):
     parts = 3
     share = w_out.shape[1] // devices
     tiles = [
@@ -315,8 +316,12 @@
         for e in range(share)
     ]
     normed = norm(jnp.concatenate(tiles, axis=0), widened(gain, LATE), 0).astype(BF16)
-    change = beside(gate, first, LATE).astype(F32) * nn(w_out[...], normed)
-    return (beside(pair, first, LATE).astype(F32) + change).astype(BF16)
+    return nn(w_out[...], normed)
+
+
+def updated(first, change, pair, gate):
+    gated = beside(gate, first, LATE).astype(F32) * change
+    return (beside(pair, first, LATE).astype(F32) + gated).astype(BF16)
 
 
 def middle_kernel(tri, pair, gate, gain_out, w_out, mask, gain, weights, w_gate, send, pair_new, gate_new, thin, wide, here, gates, sems):
@@ -333,11 +338,14 @@
         for move in both:
             move.start()
     thin[...] = tri[...].astype(F32).reshape(thin.shape)
+    changes = [
+        change_of(g, each, devices, thin, gain_out, w_out) for g in range(0, groups, LATE)
+    ]
     for g in range(0, groups, LATE):
         for both in moves[g : g + LATE]:
             for move in both:
                 move.wait()
-        block = updated_groups(g, each, devices, thin, gain_out, w_out, here, gates)
+        block = updated(g, changes[g // LATE], here, gates)
         apart(pair_new, g, block)
         normed = norm(block.astype(F32), widened(gain, LATE), 0).astype(BF16)
         send_groups(g, normed, weights[...], mask, wide, devices)
@@ -354,12 +362,19 @@
     expand = total.shape[0]
     leaving = []
     for g in range(0, groups, LATE):
-        block = updated_groups(g, each, devices, thin, gain_out, w_out, pair, gate)
+        change = change_of(g, each, devices, thin, gain_out, w_out)
+        block = updated(g, change, pair, gate)
         apart(pairs, g, block)
         normed = norm(block.astype(F32), widened(gain, LATE), 0).astype(BF16)
-        up = nn(w_up[...], normed)
-        first = up[:expand]
-        made = (first * sigmoid(first) * up[expand:]).astype(BF16)
+        lanes = []
+        for at in range(0, normed.shape[1], span):
+            some, pieces = normed[:, at : at + span], []
+            for f in range(0, expand, LANES):
+                first = nn(w_up[f : f + LANES, :], some)
+                second = nn(w_up[expand + f : expand + f + LANES, :], some)
+                pieces.append((first * sigmoid(first) * second).astype(BF16))
+            lanes.append(jnp.concatenate(pieces, axis=0))
+        made = jnp.concatenate(lanes, axis=1)
         apart(units, g, made)
         for n in range(g, g + LATE):
             for copy in (

time: 143 us -> 142 us (level)
  no operation moved by 1% of the time
where the time goes in v4:
time: 142 us; the launch traced here: 141 us
  blocking collectives  65.4 us (46%)
  Pallas kernels  27 us (19%)
  starting transfers between devices  21.7 us (15%)
  waiting for transfers between devices  18.5 us (13%)
  local copies, waits for them, and re-layouts  6.83 us (5%)
    all_to_all x3, blocking collectives, exchange(): return lax.all_to_all(value, axes, 0, 0, tiled=True)  65.4 us
    pallas_call x9, Pallas kernels, call(): pl.pallas_call(kernel, out_shape=outs, in_specs=[pl.BlockSpec(memory_spac...  27 us
    all_to_all x3, starting transfers between devices, exchange(): return lax.all_to_all(value, axes, 0, 0, tiled=True)  19.6 us
    all_to_all x3, waiting for transfers between devices, exchange(): return lax.all_to_all(value, axes, 0, 0, tiled=True)  17.5 us
    unnamed x35, local copies, waits for them, and re-layouts  2.97 us
  transfers between devices with their start and end apart: 4, of which 4 were waited for; matrix products, arithmetic and copies ran while one was open for 2% of the time, Pallas kernels for 7%

profile of v4, /device:TPU:1, one launch (start us, length us, event | category | flops | bytes accessed | tf_op | source)
XLA Modules:
  0.0 141.3 jit_solution(3690867976174080217)
XLA Ops:
  0.7 1.6 %broadcast_in_dim.52 = bf16[32,48,128]{2,1,0:T(8,128)(2,1)} broadcast(bf16[48,128]{1,0:T(8,128)(2,1)} %bitcast.72), dimensions={1,2} | broadcast | bytes 405504 | tf_op jit(solution)/shard_map/broadcast_in_dim | solution.py:473
  2.2 9.4 %all-to-all-start = ((bf16[32,48,128]{2,1,0:T(8,128)(2,1)}), bf16[32,48,128]{2,1,0:T(8,128)(2,1)S(1)}, u32[]{:S(2)}, u32[]{:S(2)}) async-start(bf16[32,48,128]{2,1,0:T(8,128)(2,1)} %broadcast_in_dim.52), calls=%async_computation | async-start | bytes 786432 | tf_op jit(solution)/shard_map/all_to_all | solution.py:37
  11.7 2.9 %prepare.1 = (bf16[6,128,384]{2,1,0:T(8,128)(2,1)}, s32[96,4]{1,0:T(8,128)S(1)}, s32[5]{0:T(128)S(1)}, bf16[6,96,384]{2,1,0:T(8,128)(2,1)S(1)}, f32[96,384]{1,0:T(8,128)S(1)}) custom-call(s32[2]{0:T(128)S(1)} %pad_add_fusion.place, bf16[48,48,128]{2,1,0:T(8,128)(2,1)S(1)} %bitcast.58, s32[1,384]{1,0:T(1,128)S(1)} %copy-done.7, s32[1,384]{1,0:T(1,128)S(1)} %copy-done.8, ...), custom_call_target="tpu_custom_call" | custom-call | flops 400000000 | bytes 4194304 | tf_op jit(solution)/shard_map/prepare/pallas_call | solution.py:428
  14.6 6.6 %all-to-all-done = bf16[32,48,128]{2,1,0:T(8,128)(2,1)S(1)} async-done(((bf16[32,48,128]{2,1,0:T(8,128)(2,1)}), bf16[32,48,128]{2,1,0:T(8,128)(2,1)S(1)}, u32[]{:S(2)}, u32[]{:S(2)}) %all-to-all-start) | async-done | bytes 393248 | tf_op jit(solution)/shard_map/all_to_all | solution.py:37
  21.2 2.0 %collective-permute-start = (bf16[1536,128]{1,0:T(8,128)(2,1)S(1)}, bf16[1536,128]{1,0:T(8,128)(2,1)S(1)}, u32[]{:S(2)}, u32[]{:S(2)}) collective-permute-start(bf16[1536,128]{1,0:T(8,128)(2,1)S(1)} %bitcast.49), channel_id=1, source_target_pairs={{0,16},{16,0},{1,17},{17,1},{2,18},{18,2},{3,19},{19,3},{4,20},{20... | collective-permute-start | bytes 1179656 | tf_op jit(solution)/shard_map/ppermute | solution.py:502
  23.3 0.2 copy.54
  23.6 1.0 collective-permute-done.other
  24.7 3.6 %front.1 = (bf16[64,72,128]{2,1,0:T(8,128)(2,1)S(1)}, bf16[128,96]{1,0:T(8,128)(2,1)S(1)}) custom-call(s32[5]{0:T(128)S(1)} %get-tuple-element.44.bounds, bf16[1536,128]{1,0:T(8,128)(2,1)S(1)} %bitcast.50, bf16[1536,128]{1,0:T(8,128)(2,1)S(1)} %collective-permute-done.other, s32[96,4]{1,0:T(8,128)S(1)} %get-tuple-element.46.tokens, ...), custom_call_target="tpu_custom_call" | custom-call | flops 400000000 | bytes 4194304 | tf_op jit(solution)/shard_map/front/pallas_call | solution.py:428
  28.3 24.1 %all_to_all.30.x = bf16[64,72,128]{2,1,0:T(8,128)(2,1)S(1)} all-to-all(bf16[64,72,128]{2,1,0:T(8,128)(2,1)S(1)} %get-tuple-element.50), channel_id=1, replica_groups=mesh['x'=4,'core'=2,'y'=4,'zl'=2,'rep'=2] {'y','zl','x','core'}, dimensions={0} | all-to-all | bytes 2359296 | tf_op jit(solution)/shard_map/all_to_all | solution.py:37
  52.3 3.1 %triangle.2 = bf16[64,36,128]{2,1,0:T(8,128)(2,1)} custom-call(bf16[64,72,128]{2,1,0:T(8,128)(2,1)S(1)} %all_to_all.30.x), custom_call_target="tpu_custom_call" | custom-call | flops 400000000 | bytes 4194304 | tf_op jit(solution)/shard_map/triangle/pallas_call | solution.py:428
  55.5 4.9 %all-to-all-start.2 = ((bf16[64,36,128]{2,1,0:T(8,128)(2,1)}), bf16[64,36,128]{2,1,0:T(8,128)(2,1)S(1)}, u32[]{:S(2)}, u32[]{:S(2)}) async-start(bf16[64,36,128]{2,1,0:T(8,128)(2,1)} %triangle.2), calls=%async_computation.2 | async-start | bytes 1310720 | tf_op jit(solution)/shard_map/all_to_all | solution.py:37
  60.5 0.2 copy.42
  60.9 0.1 reshape_squeeze.14
  61.0 0.1 copy.49
  61.3 0.1 reshape_squeeze.12
  61.4 0.1 copy.43
  61.9 0.1 copy.53
  62.0 0.2 copy.52
  62.3 1.3 turn.1.d_pair
  64.1 3.5 %first_gate.1 = (bf16[6,128,384]{2,1,0:T(8,128)(2,1)}, bf16[6,128,384]{2,1,0:T(8,128)(2,1)}) custom-call(bf16[48,48,128]{2,1,0:T(8,128)(2,1)S(1)} %bitcast.59, bf16[128,96]{1,0:T(8,128)(2,1)S(1)} %get-tuple-element.54.sides, f32[128,384]{1,0:T(8,128)S(1)} %broadcast_in_dim.56.gain, bf16[128,128]{1,0:T(8,128)(2,1)S(1)} %get-tuple-element.89.w_gate), custom_call_target="tpu_custom_call" | custom-call | flops 400000000 | bytes 4194304 | tf_op jit(solution)/shard_map/first_gate/pallas_call | solution.py:428
  67.6 6.6 %all-to-all-done.2.tri = bf16[64,36,128]{2,1,0:T(8,128)(2,1)S(1)} async-done(((bf16[64,36,128]{2,1,0:T(8,128)(2,1)}), bf16[64,36,128]{2,1,0:T(8,128)(2,1)S(1)}, u32[]{:S(2)}, u32[]{:S(2)}) %all-to-all-start.2) | async-done | bytes 589856 | tf_op jit(solution)/shard_map/all_to_all | solution.py:37
  74.2 3.4 %middle.1 = (bf16[64,72,128]{2,1,0:T(8,128)(2,1)S(1)}, bf16[6,128,384]{2,1,0:T(8,128)(2,1)S(1)}, bf16[6,128,384]{2,1,0:T(8,128)(2,1)S(1)}) custom-call(bf16[64,36,128]{2,1,0:T(8,128)(2,1)S(1)} %all-to-all-done.2.tri, bf16[6,128,384]{2,1,0:T(8,128)(2,1)} %get-tuple-element.57.pair, bf16[6,128,384]{2,1,0:T(8,128)(2,1)} %get-tuple-element.58.gate, ...), custom_call_target="tpu_custom_call" | custom-call | flops 400000000 | bytes 4194304 | tf_op jit(solution)/shard_map/middle/pallas_call | solution.py:428
  77.7 23.4 %all_to_all.31.refs_0_ = bf16[64,72,128]{2,1,0:T(8,128)(2,1)S(1)} all-to-all(bf16[64,72,128]{2,1,0:T(8,128)(2,1)S(1)} %get-tuple-element.72), channel_id=1, replica_groups=mesh['x'=4,'core'=2,'y'=4,'zl'=2,'rep'=2] {'x','core','y','zl'}, dimensions={0} | all-to-all | bytes 2359296 | tf_op jit(solution)/shard_map/all_to_all | solution.py:37
  101.1 2.4 %triangle.3 = bf16[64,36,128]{2,1,0:T(8,128)(2,1)S(1)} custom-call(bf16[64,72,128]{2,1,0:T(8,128)(2,1)S(1)} %all_to_all.31.refs_0_), custom_call_target="tpu_custom_call" | custom-call | flops 400000000 | bytes 4194304 | tf_op jit(solution)/shard_map/triangle/pallas_call | solution.py:428
  103.5 17.9 %all_to_all.32.tri = bf16[64,36,128]{2,1,0:T(8,128)(2,1)S(1)} all-to-all(bf16[64,36,128]{2,1,0:T(8,128)(2,1)S(1)} %triangle.3), channel_id=1, replica_groups=mesh['x'=4,'core'=2,'y'=4,'zl'=2,'rep'=2] {'x','core','y','zl'}, dimensions={0} | all-to-all | bytes 1179648 | tf_op jit(solution)/shard_map/all_to_all | solution.py:37
  121.4 3.9 %last.1 = (bf16[512,128]{1,0:T(8,128)(2,1)}, bf16[6,512,384]{2,1,0:T(8,128)(2,1)}, bf16[6,128,384]{2,1,0:T(8,128)(2,1)}) custom-call(bf16[64,36,128]{2,1,0:T(8,128)(2,1)S(1)} %all_to_all.32.tri, bf16[6,128,384]{2,1,0:T(8,128)(2,1)S(1)} %get-tuple-element.73.pair, bf16[6,128,384]{2,1,0:T(8,128)(2,1)S(1)} %get-tuple-element.74.gate, ...), custom_call_target="tpu_custom_call" | custom-call | flops 800000000 | bytes 4194304 | tf_op jit(solution)/shard_map/last/pallas_call | solution.py:428
  125.3 5.4 %all-to-all-start.5 = ((bf16[128,4,128]{2,1,0:T(4,128)(2,1)}), bf16[128,4,128]{2,1,0:T(4,128)(2,1)S(1)}, u32[]{:S(2)}, u32[]{:S(2)}) async-start(bf16[128,4,128]{2,1,0:T(4,128)(2,1)} %bitcast.66), calls=%async_computation.5 | async-start | bytes 262144 | tf_op jit(solution)/shard_map/all_to_all | solution.py:37
  130.7 1.7 %copy-done = bf16[6,512,384]{2,1,0:T(8,128)(2,1)S(1)} copy-done((bf16[6,512,384]{2,1,0:T(8,128)(2,1)S(1)}, bf16[6,512,384]{2,1,0:T(8,128)(2,1)}, u32[]{:S(2)}) %copy-start) | copy-done | bytes 2359320
  132.3 1.1 copy-done.1
  133.4 2.9 %down.1 = bf16[48,48,128]{2,1,0:T(8,128)(2,1)} custom-call(bf16[6,512,384]{2,1,0:T(8,128)(2,1)S(1)} %copy-done, bf16[6,128,384]{2,1,0:T(8,128)(2,1)S(1)} %copy-done.1, bf16[128,512]{1,0:T(8,128)(2,1)S(1)} %bitcast.52), custom_call_target="tpu_custom_call" | custom-call | flops 400000000 | bytes 4194304 | tf_op jit(solution)/shard_map/down/pallas_call | solution.py:428
  136.3 4.3 %all-to-all-done.5 = bf16[128,4,128]{2,1,0:T(4,128)(2,1)S(1)} async-done(((bf16[128,4,128]{2,1,0:T(4,128)(2,1)}), bf16[128,4,128]{2,1,0:T(4,128)(2,1)S(1)}, u32[]{:S(2)}, u32[]{:S(2)}) %all-to-all-start.5) | async-done | bytes 131104 | tf_op jit(solution)/shard_map/all_to_all | solution.py:37
  140.6 0.7 convert_reduce_fusion
  (62 shorter events, 1.4 us)
Async XLA Ops:
  0.6 11.1 %copy-start.5 = (bf16[1,48,48,128]{3,2,1,0:T(8,128)(2,1)S(1)}, bf16[1,48,48,128]{3,2,1,0:T(8,128)(2,1)}, u32[]{:S(2)}) copy-start(bf16[1,48,48,128]{3,2,1,0:T(8,128)(2,1)} %param.20) | copy-start | bytes 1769476
  0.6 11.1 %copy-start.6 = (bf16[32,384]{1,0:T(8,128)(2,1)S(1)}, bf16[32,384]{1,0:T(8,128)(2,1)}, u32[]{:S(2)}) copy-start(bf16[32,384]{1,0:T(8,128)(2,1)} %w_restype.1) | copy-start | bytes 73732
  0.7 11.1 %copy-start.8 = (s32[1,384]{1,0:T(1,128)S(1)}, s32[1,384]{1,0:T(1,128)}, u32[]{:S(2)}) copy-start(s32[1,384]{1,0:T(1,128)} %types.1) | copy-start | bytes 4612
  0.7 11.0 %copy-start.7 = (s32[1,384]{1,0:T(1,128)S(1)}, s32[1,384]{1,0:T(1,128)}, u32[]{:S(2)}) copy-start(s32[1,384]{1,0:T(1,128)} %counts.1) | copy-start | bytes 4612
  2.2 21.0 %copy-start.13 = (s32[1,48,48]{2,1,0:T(8,128)S(1)}, s32[1,48,48]{2,1,0:T(8,128)}, u32[]{:S(2)}) copy-start(s32[1,48,48]{2,1,0:T(8,128)} %param.21) | copy-start | bytes 27652
  2.2 19.0 %all-to-all-start = ((bf16[32,48,128]{2,1,0:T(8,128)(2,1)}), bf16[32,48,128]{2,1,0:T(8,128)(2,1)S(1)}, u32[]{:S(2)}, u32[]{:S(2)}) async-start(bf16[32,48,128]{2,1,0:T(8,128)(2,1)} %broadcast_in_dim.52), calls=%async_computation | async-start | bytes 786432 | tf_op jit(solution)/shard_map/all_to_all | solution.py:37
  11.6 11.7 %slice-start = ((bf16[2,128,640]{2,1,0:T(8,128)(2,1)}), bf16[1,128,640]{2,1,0:T(8,128)(2,1)S(1)}, s32[]{:S(2)}) async-start(bf16[2,128,640]{2,1,0:T(8,128)(2,1)} %param.26), calls=%async_computation.6 | async-start | bytes 327680 | tf_op jit(solution)/shard_map/slice | solution.py:570
  11.7 11.8 %copy-start.14 = (f32[2,128]{1,0:T(2,128)S(1)}, f32[2,128]{1,0:T(2,128)}, u32[]{:S(2)}) copy-start(f32[2,128]{1,0:T(2,128)} %param.25) | copy-start | bytes 3076
  14.6 10.1 %copy-start.2 = (bf16[384,256]{1,0:T(8,128)(2,1)S(1)}, bf16[384,256]{1,0:T(8,128)(2,1)}, u32[]{:S(2)}) copy-start(bf16[384,256]{1,0:T(8,128)(2,1)} %w_pair.1) | copy-start | bytes 589828
  14.6 10.1 %copy-start.3 = (bf16[128,384]{1,0:T(8,128)(2,1)S(1)}, bf16[128,384]{1,0:T(8,128)(2,1)}, u32[]{:S(2)}) copy-start(bf16[128,384]{1,0:T(8,128)(2,1)} %w_atom.1) | copy-start | bytes 294916
  21.2 3.4 %collective-permute-start = (bf16[1536,128]{1,0:T(8,128)(2,1)S(1)}, bf16[1536,128]{1,0:T(8,128)(2,1)S(1)}, u32[]{:S(2)}, u32[]{:S(2)}) collective-permute-start(bf16[1536,128]{1,0:T(8,128)(2,1)S(1)} %bitcast.49), channel_id=1, source_target_pairs={{0,16},{16,0},{1,17},{17,1},{2,18},{18,2},{3,19},{19,3},{4,20},{20... | collective-permute-start | bytes 1179656 | tf_op jit(solution)/shard_map/ppermute | solution.py:502
  52.3 8.1 %copy-start.12 = (bf16[2,128,128]{2,1,0:T(8,128)(2,1)S(1)}, bf16[2,128,128]{2,1,0:T(8,128)(2,1)}, u32[]{:S(2)}) copy-start(bf16[2,128,128]{2,1,0:T(8,128)(2,1)} %param.28) | copy-start | bytes 196612
  55.5 5.0 %copy-start.9 = (bf16[2,128,640]{2,1,0:T(8,128)(2,1)S(1)}, bf16[2,128,640]{2,1,0:T(8,128)(2,1)}, u32[]{:S(2)}) copy-start(bf16[2,128,640]{2,1,0:T(8,128)(2,1)} %param.26) | copy-start | bytes 983044
  55.5 5.2 %copy-start.15 = (f32[2,128]{1,0:T(2,128)S(1)}, f32[2,128]{1,0:T(2,128)}, u32[]{:S(2)}) copy-start(f32[2,128]{1,0:T(2,128)} %param.27) | copy-start | bytes 3076
  55.5 6.4 %copy-start.11 = (bf16[512,128]{1,0:T(8,128)(2,1)S(1)}, bf16[512,128]{1,0:T(8,128)(2,1)}, u32[]{:S(2)}) copy-start(bf16[512,128]{1,0:T(8,128)(2,1)} %param.31) | copy-start | bytes 393220
  55.5 18.7 %all-to-all-start.2 = ((bf16[64,36,128]{2,1,0:T(8,128)(2,1)}), bf16[64,36,128]{2,1,0:T(8,128)(2,1)S(1)}, u32[]{:S(2)}, u32[]{:S(2)}) async-start(bf16[64,36,128]{2,1,0:T(8,128)(2,1)} %triangle.2), calls=%async_computation.2 | async-start | bytes 1310720 | tf_op jit(solution)/shard_map/all_to_all | solution.py:37
  60.4 1.6 %copy-start.10 = (bf16[128,1024]{1,0:T(8,128)(2,1)S(1)}, bf16[128,1024]{1,0:T(8,128)(2,1)}, u32[]{:S(2)}) copy-start(bf16[128,1024]{1,0:T(8,128)(2,1)} %param.30) | copy-start | bytes 786436
  60.7 1.6 %copy-start.4 = (bf16[1,48,48,128]{3,2,1,0:T(8,128)(2,1)S(1)}, bf16[1,48,48,128]{3,2,1,0:T(8,128)(2,1)}, u32[]{:S(2)}) copy-start(bf16[1,48,48,128]{3,2,1,0:T(8,128)(2,1)} %param.32) | copy-start | bytes 1769476
  62.3 1.6 %copy-start.16 = (f32[128]{0:T(128)S(1)}, f32[128]{0:T(128)}, u32[]{:S(2)}) copy-start(f32[128]{0:T(128)} %param.29) | copy-start | bytes 1540
  125.3 15.3 %all-to-all-start.5 = ((bf16[128,4,128]{2,1,0:T(4,128)(2,1)}), bf16[128,4,128]{2,1,0:T(4,128)(2,1)S(1)}, u32[]{:S(2)}, u32[]{:S(2)}) async-start(bf16[128,4,128]{2,1,0:T(4,128)(2,1)} %bitcast.66), calls=%async_computation.5 | async-start | bytes 262144 | tf_op jit(solution)/shard_map/all_to_all | solution.py:37
  130.7 1.7 %copy-start = (bf16[6,512,384]{2,1,0:T(8,128)(2,1)S(1)}, bf16[6,512,384]{2,1,0:T(8,128)(2,1)}, u32[]{:S(2)}) copy-start(bf16[6,512,384]{2,1,0:T(8,128)(2,1)} %get-tuple-element.80.hidden) | copy-start | bytes 7077892
  132.3 1.1 copy-start.1

commit v5 on v4

--- a/solution.py
+++ b/solution.py
@@ -44,7 +44,7 @@
     count = proj.shape[1] // span
     valid = jnp.concatenate([mask[pl.ds(first + n, 1), :] for n in range(count)], axis=1)
     sides = sigmoid(proj[:half]) * proj[half:] * valid
-    rows = wide.shape[0] // devices
+    rows = wide.shape[0] // (devices + 1)
     parts = span // LANES
     kinds = half // devices
     for n in range(count):
@@ -128,7 +128,7 @@
 def turn_kernel(d_pair, out, wide, made, sem):
     tok = d_pair.shape[0]
     span = 8 * tok
-    wide[...] = d_pair[...].astype(F32).reshape(wide.shape)
+    wide[: tok * tok] = d_pair[...].astype(F32).reshape(tok * tok, d_pair.shape[2])
 
     def grads(g, carry):
         rows = pl.ds(pl.multiple_of(g * span, span), span)
@@ -176,7 +176,8 @@
 
     steps = jnp.maximum(bounds[1] - bounds[0], bounds[3] - bounds[2])
     zero = jnp.zeros((tok, w_atom.shape[1]), F32)
-    sums = lax.fori_loop(0, steps, pool, (zero, zero))
+    sums = pool(1, pool(0, (zero, zero)))
+    sums = lax.fori_loop(2, jnp.maximum(steps, 2), pool, sums)
     counts = tokens[:, 2:3].astype(F32)
     single = (jnp.concatenate(sums, 0) / counts + embedded[...]).astype(BF16)
     left = nn(single[:tok], w_pair[:, :width])
@@ -188,12 +189,12 @@
         block = beside(pair_in, g, FRONT).astype(F32) + nn(sides[...], beside(chosen, g, FRONT))
         normed = norm(block.astype(BF16).astype(F32), widened(gain, FRONT), 0).astype(BF16)
         send_groups(g, normed, weights[...], mask, wide, devices)
-    send[...] = wide[...].astype(BF16).reshape(send.shape)
+    send[...] = wide[: devices * send.shape[1]].astype(BF16).reshape(send.shape)
 
 
 def first_gate_kernel(pair_in, sides, gain, w_gate, pair_out, gate_out, wide, pair, gate, sems):
     tok = pair_in.shape[0]
-    wide[...] = pair_in[...].astype(F32).reshape(wide.shape)
+    wide[: tok * tok] = pair_in[...].astype(F32).reshape(tok * tok, pair_in.shape[2])
 
     def group(g, carry):
         block = turned_rows(g, wide, tok).T + nn(sides[...], choice(g, tok, True))
@@ -236,7 +237,7 @@
     groups = tok // 8
     kinds = 2 * share
     side_len = blocks * tok
-    xf[...] = x[...].astype(F32).reshape(xf.shape)
+    xf[: devices * x.shape[1]] = x[...].astype(F32).reshape(devices * x.shape[1], LANES)
     lane = lax.broadcasted_iota(jnp.int32, (tok, LANES), 1)
     per_block = devices // blocks * x.shape[1]
 
@@ -298,7 +299,7 @@
     for copy in leaving:
         copy.wait()
     if made is None:
-        out[...] = of[...].astype(BF16).reshape(out.shape)
+        out[...] = of[: devices * each].astype(BF16).reshape(out.shape)
 
 
 def change_of(first, each, devices, wide, gain, w_out):
@@ -337,7 +338,7 @@
     for both in moves:
         for move in both:
             move.start()
-    thin[...] = tri[...].astype(F32).reshape(thin.shape)
+    thin[: devices * each] = tri[...].astype(F32).reshape(devices * each, LANES)
     changes = [
         change_of(g, each, devices, thin, gain_out, w_out) for g in range(0, groups, LATE)
     ]
@@ -350,7 +351,7 @@
         normed = norm(block.astype(F32), widened(gain, LATE), 0).astype(BF16)
         send_groups(g, normed, weights[...], mask, wide, devices)
         apart(gate_new, g, sigmoid(nn(w_gate[...], normed)).astype(BF16))
-    send[...] = wide[...].astype(BF16).reshape(send.shape)
+    send[...] = wide[: devices * send.shape[1]].astype(BF16).reshape(send.shape)
 
 
 def last_kernel(tri, pair, gate, gain_out, w_out, gain, w_up, d_pair, grad, hidden, pair_new, thin, total, there, units, pairs, small, sems, outs):
@@ -358,7 +359,7 @@
     groups, span = pair.shape[0], pair.shape[2]
     move = pltpu.make_async_copy(d_pair, there, sems.at[0])
     move.start()
-    thin[...] = tri[...].astype(F32).reshape(thin.shape)
+    thin[: devices * each] = tri[...].astype(F32).reshape(devices * each, LANES)
     expand = total.shape[0]
     leaving = []
     for g in range(0, groups, LATE):
@@ -404,7 +405,7 @@
         return carry
 
     lax.fori_loop(0, hidden.shape[0], group, 0)
-    out[...] = wide[...].astype(BF16).reshape(out.shape)
+    out[...] = wide[: tok * tok].astype(BF16).reshape(out.shape)
 
 
 def call(kernel, outs, scratch, name, cost, *args, far=(), far_out=(), scalar=(), scalar_out=()):
@@ -521,8 +522,9 @@
     rows_back = share * count // LANES
     send_shape = shape((devices, rows_out, LANES), BF16)
     back_shape = shape((devices, rows_back, LANES), BF16)
-    wide = pltpu.VMEM((devices * rows_out, LANES), F32)
-    thin = pltpu.VMEM((devices * rows_back, LANES), F32)
+    wide = pltpu.VMEM(((devices + 1) * rows_out, LANES), F32)
+    thin = pltpu.VMEM(((devices + 1) * rows_back, LANES), F32)
+    strided = pltpu.VMEM((count + tok, width), F32)
     flat = shape((groups, width, span), BF16)
     here = pltpu.VMEM(flat.shape, BF16)
     gates = here
@@ -584,7 +586,7 @@
     pair, gate = call(
         first_gate_kernel,
         (flat, flat),
-        [pltpu.VMEM((count, width), F32), here, gates, pltpu.SemaphoreType.DMA((2,))],
+        [strided, here, gates, pltpu.SemaphoreType.DMA((2,))],
         "first_gate",
         cost,
         pair_in[0],
@@ -596,7 +598,7 @@
     turned_grad = call(
         turn_kernel,
         shape((count, width), BF16),
-        [pltpu.VMEM((count, width), F32), pltpu.VMEM((count, width), BF16), pltpu.SemaphoreType.DMA],
+        [strided, pltpu.VMEM((count, width), BF16), pltpu.SemaphoreType.DMA],
         "turn",
         cost,
         d_pair[0],
@@ -657,7 +659,7 @@
     result = call(
         down_kernel,
         shape((tok, tok, width), BF16),
-        [pltpu.VMEM((count, width), F32)],
+        [strided],
         "down",
         cost,
         hidden,

time: 142 us -> 142 us (level)
  no operation moved by 1% of the time
where the time goes in v5:
time: 142 us
  blocking collectives  64.8 us (46%)
  Pallas kernels  27 us (19%)
  starting transfers between devices  22.6 us (16%)
  waiting for transfers between devices  18.5 us (13%)
  local copies, waits for them, and re-layouts  6.83 us (5%)
    all_to_all x3, blocking collectives, exchange(): return lax.all_to_all(value, axes, 0, 0, tiled=True)  64.8 us
    pallas_call x9, Pallas kernels, call(): pl.pallas_call(kernel, out_shape=outs, in_specs=[pl.BlockSpec(memory_spac...  27 us
    all_to_all x3, starting transfers between devices, exchange(): return lax.all_to_all(value, axes, 0, 0, tiled=True)  20.5 us
    all_to_all x3, waiting for transfers between devices, exchange(): return lax.all_to_all(value, axes, 0, 0, tiled=True)  17.5 us
    unnamed x35, local copies, waits for them, and re-layouts  2.97 us
  transfers between devices with their start and end apart: 4, of which 4 were waited for; matrix products, arithmetic and copies ran while one was open for 2% of the time, Pallas kernels for 7%

profile of v5, /device:TPU:1, one launch (start us, length us, event | category | flops | bytes accessed | tf_op | source)
XLA Modules:
  0.0 141.6 jit_solution(1088104888350403827)
XLA Ops:
  0.7 1.6 %broadcast_in_dim.52 = bf16[32,48,128]{2,1,0:T(8,128)(2,1)} broadcast(bf16[48,128]{1,0:T(8,128)(2,1)} %bitcast.72), dimensions={1,2} | broadcast | bytes 405504 | tf_op jit(solution)/shard_map/broadcast_in_dim | solution.py:474
  2.2 9.4 %all-to-all-start = ((bf16[32,48,128]{2,1,0:T(8,128)(2,1)}), bf16[32,48,128]{2,1,0:T(8,128)(2,1)S(1)}, u32[]{:S(2)}, u32[]{:S(2)}) async-start(bf16[32,48,128]{2,1,0:T(8,128)(2,1)} %broadcast_in_dim.52), calls=%async_computation | async-start | bytes 786432 | tf_op jit(solution)/shard_map/all_to_all | solution.py:37
  11.7 2.9 %prepare.1 = (bf16[6,128,384]{2,1,0:T(8,128)(2,1)}, s32[96,4]{1,0:T(8,128)S(1)}, s32[5]{0:T(128)S(1)}, bf16[6,96,384]{2,1,0:T(8,128)(2,1)S(1)}, f32[96,384]{1,0:T(8,128)S(1)}) custom-call(s32[2]{0:T(128)S(1)} %pad_add_fusion.place, bf16[48,48,128]{2,1,0:T(8,128)(2,1)S(1)} %bitcast.58, s32[1,384]{1,0:T(1,128)S(1)} %copy-done.7, s32[1,384]{1,0:T(1,128)S(1)} %copy-done.8, ...), custom_call_target="tpu_custom_call" | custom-call | flops 400000000 | bytes 4194304 | tf_op jit(solution)/shard_map/prepare/pallas_call | solution.py:429
  14.6 6.6 %all-to-all-done = bf16[32,48,128]{2,1,0:T(8,128)(2,1)S(1)} async-done(((bf16[32,48,128]{2,1,0:T(8,128)(2,1)}), bf16[32,48,128]{2,1,0:T(8,128)(2,1)S(1)}, u32[]{:S(2)}, u32[]{:S(2)}) %all-to-all-start) | async-done | bytes 393248 | tf_op jit(solution)/shard_map/all_to_all | solution.py:37
  21.2 2.0 %collective-permute-start = (bf16[1536,128]{1,0:T(8,128)(2,1)S(1)}, bf16[1536,128]{1,0:T(8,128)(2,1)S(1)}, u32[]{:S(2)}, u32[]{:S(2)}) collective-permute-start(bf16[1536,128]{1,0:T(8,128)(2,1)S(1)} %bitcast.49), channel_id=1, source_target_pairs={{0,16},{16,0},{1,17},{17,1},{2,18},{18,2},{3,19},{19,3},{4,20},{20... | collective-permute-start | bytes 1179656 | tf_op jit(solution)/shard_map/ppermute | solution.py:503
  23.3 0.2 copy.54
  23.6 1.0 collective-permute-done.other
  24.7 3.5 %front.1 = (bf16[64,72,128]{2,1,0:T(8,128)(2,1)S(1)}, bf16[128,96]{1,0:T(8,128)(2,1)S(1)}) custom-call(s32[5]{0:T(128)S(1)} %get-tuple-element.44.bounds, bf16[1536,128]{1,0:T(8,128)(2,1)S(1)} %bitcast.50, bf16[1536,128]{1,0:T(8,128)(2,1)S(1)} %collective-permute-done.other, s32[96,4]{1,0:T(8,128)S(1)} %get-tuple-element.46.tokens, ...), custom_call_target="tpu_custom_call" | custom-call | flops 400000000 | bytes 4194304 | tf_op jit(solution)/shard_map/front/pallas_call | solution.py:429
  28.2 23.5 %all_to_all.30.x = bf16[64,72,128]{2,1,0:T(8,128)(2,1)S(1)} all-to-all(bf16[64,72,128]{2,1,0:T(8,128)(2,1)S(1)} %get-tuple-element.50), channel_id=1, replica_groups=mesh['x'=4,'core'=2,'y'=4,'zl'=2,'rep'=2] {'y','zl','x','core'}, dimensions={0} | all-to-all | bytes 2359296 | tf_op jit(solution)/shard_map/all_to_all | solution.py:37
  51.7 3.1 %triangle.2 = bf16[64,36,128]{2,1,0:T(8,128)(2,1)} custom-call(bf16[64,72,128]{2,1,0:T(8,128)(2,1)S(1)} %all_to_all.30.x), custom_call_target="tpu_custom_call" | custom-call | flops 400000000 | bytes 4194304 | tf_op jit(solution)/shard_map/triangle/pallas_call | solution.py:429
  54.9 4.9 %all-to-all-start.2 = ((bf16[64,36,128]{2,1,0:T(8,128)(2,1)}), bf16[64,36,128]{2,1,0:T(8,128)(2,1)S(1)}, u32[]{:S(2)}, u32[]{:S(2)}) async-start(bf16[64,36,128]{2,1,0:T(8,128)(2,1)} %triangle.2), calls=%async_computation.2 | async-start | bytes 1310720 | tf_op jit(solution)/shard_map/all_to_all | solution.py:37
  59.9 0.2 copy.42
  60.3 0.1 reshape_squeeze.14
  60.4 0.1 copy.49
  60.7 0.1 reshape_squeeze.12
  60.8 0.1 copy.43
  61.3 0.1 copy.53
  61.4 0.2 copy.52
  61.7 1.3 turn.1.d_pair
  63.5 3.5 %first_gate.1 = (bf16[6,128,384]{2,1,0:T(8,128)(2,1)}, bf16[6,128,384]{2,1,0:T(8,128)(2,1)}) custom-call(bf16[48,48,128]{2,1,0:T(8,128)(2,1)S(1)} %bitcast.59, bf16[128,96]{1,0:T(8,128)(2,1)S(1)} %get-tuple-element.54.sides, f32[128,384]{1,0:T(8,128)S(1)} %broadcast_in_dim.56.gain, bf16[128,128]{1,0:T(8,128)(2,1)S(1)} %get-tuple-element.89.w_gate), custom_call_target="tpu_custom_call" | custom-call | flops 400000000 | bytes 4194304 | tf_op jit(solution)/shard_map/first_gate/pallas_call | solution.py:429
  67.0 6.6 %all-to-all-done.2.tri = bf16[64,36,128]{2,1,0:T(8,128)(2,1)S(1)} async-done(((bf16[64,36,128]{2,1,0:T(8,128)(2,1)}), bf16[64,36,128]{2,1,0:T(8,128)(2,1)S(1)}, u32[]{:S(2)}, u32[]{:S(2)}) %all-to-all-start.2) | async-done | bytes 589856 | tf_op jit(solution)/shard_map/all_to_all | solution.py:37
  73.6 3.4 %middle.1 = (bf16[64,72,128]{2,1,0:T(8,128)(2,1)S(1)}, bf16[6,128,384]{2,1,0:T(8,128)(2,1)S(1)}, bf16[6,128,384]{2,1,0:T(8,128)(2,1)S(1)}) custom-call(bf16[64,36,128]{2,1,0:T(8,128)(2,1)S(1)} %all-to-all-done.2.tri, bf16[6,128,384]{2,1,0:T(8,128)(2,1)} %get-tuple-element.57.pair, bf16[6,128,384]{2,1,0:T(8,128)(2,1)} %get-tuple-element.58.gate, ...), custom_call_target="tpu_custom_call" | custom-call | flops 400000000 | bytes 4194304 | tf_op jit(solution)/shard_map/middle/pallas_call | solution.py:429
  77.0 23.4 %all_to_all.31.refs_0_ = bf16[64,72,128]{2,1,0:T(8,128)(2,1)S(1)} all-to-all(bf16[64,72,128]{2,1,0:T(8,128)(2,1)S(1)} %get-tuple-element.72), channel_id=1, replica_groups=mesh['x'=4,'core'=2,'y'=4,'zl'=2,'rep'=2] {'x','core','y','zl'}, dimensions={0} | all-to-all | bytes 2359296 | tf_op jit(solution)/shard_map/all_to_all | solution.py:37
  100.5 2.4 %triangle.3 = bf16[64,36,128]{2,1,0:T(8,128)(2,1)S(1)} custom-call(bf16[64,72,128]{2,1,0:T(8,128)(2,1)S(1)} %all_to_all.31.refs_0_), custom_call_target="tpu_custom_call" | custom-call | flops 400000000 | bytes 4194304 | tf_op jit(solution)/shard_map/triangle/pallas_call | solution.py:429
  102.9 17.9 %all_to_all.32.tri = bf16[64,36,128]{2,1,0:T(8,128)(2,1)S(1)} all-to-all(bf16[64,36,128]{2,1,0:T(8,128)(2,1)S(1)} %triangle.3), channel_id=1, replica_groups=mesh['x'=4,'core'=2,'y'=4,'zl'=2,'rep'=2] {'x','core','y','zl'}, dimensions={0} | all-to-all | bytes 1179648 | tf_op jit(solution)/shard_map/all_to_all | solution.py:37
  120.8 3.9 %last.1 = (bf16[512,128]{1,0:T(8,128)(2,1)}, bf16[6,512,384]{2,1,0:T(8,128)(2,1)}, bf16[6,128,384]{2,1,0:T(8,128)(2,1)}) custom-call(bf16[64,36,128]{2,1,0:T(8,128)(2,1)S(1)} %all_to_all.32.tri, bf16[6,128,384]{2,1,0:T(8,128)(2,1)S(1)} %get-tuple-element.73.pair, bf16[6,128,384]{2,1,0:T(8,128)(2,1)S(1)} %get-tuple-element.74.gate, ...), custom_call_target="tpu_custom_call" | custom-call | flops 800000000 | bytes 4194304 | tf_op jit(solution)/shard_map/last/pallas_call | solution.py:429
  124.7 6.3 %all-to-all-start.5 = ((bf16[128,4,128]{2,1,0:T(4,128)(2,1)}), bf16[128,4,128]{2,1,0:T(4,128)(2,1)S(1)}, u32[]{:S(2)}, u32[]{:S(2)}) async-start(bf16[128,4,128]{2,1,0:T(4,128)(2,1)} %bitcast.66), calls=%async_computation.5 | async-start | bytes 262144 | tf_op jit(solution)/shard_map/all_to_all | solution.py:37
  130.9 1.7 %copy-done = bf16[6,512,384]{2,1,0:T(8,128)(2,1)S(1)} copy-done((bf16[6,512,384]{2,1,0:T(8,128)(2,1)S(1)}, bf16[6,512,384]{2,1,0:T(8,128)(2,1)}, u32[]{:S(2)}) %copy-start) | copy-done | bytes 2359320
  132.6 1.1 copy-done.1
  133.7 2.9 %down.1 = bf16[48,48,128]{2,1,0:T(8,128)(2,1)} custom-call(bf16[6,512,384]{2,1,0:T(8,128)(2,1)S(1)} %copy-done, bf16[6,128,384]{2,1,0:T(8,128)(2,1)S(1)} %copy-done.1, bf16[128,512]{1,0:T(8,128)(2,1)S(1)} %bitcast.52), custom_call_target="tpu_custom_call" | custom-call | flops 400000000 | bytes 4194304 | tf_op jit(solution)/shard_map/down/pallas_call | solution.py:429
  136.6 4.3 %all-to-all-done.5 = bf16[128,4,128]{2,1,0:T(4,128)(2,1)S(1)} async-done(((bf16[128,4,128]{2,1,0:T(4,128)(2,1)}), bf16[128,4,128]{2,1,0:T(4,128)(2,1)S(1)}, u32[]{:S(2)}, u32[]{:S(2)}) %all-to-all-start.5) | async-done | bytes 131104 | tf_op jit(solution)/shard_map/all_to_all | solution.py:37
  140.8 0.7 convert_reduce_fusion
  (62 shorter events, 1.4 us)
Async XLA Ops:
  0.6 11.1 %copy-start.5 = (bf16[1,48,48,128]{3,2,1,0:T(8,128)(2,1)S(1)}, bf16[1,48,48,128]{3,2,1,0:T(8,128)(2,1)}, u32[]{:S(2)}) copy-start(bf16[1,48,48,128]{3,2,1,0:T(8,128)(2,1)} %param.20) | copy-start | bytes 1769476
  0.6 11.1 %copy-start.6 = (bf16[32,384]{1,0:T(8,128)(2,1)S(1)}, bf16[32,384]{1,0:T(8,128)(2,1)}, u32[]{:S(2)}) copy-start(bf16[32,384]{1,0:T(8,128)(2,1)} %w_restype.1) | copy-start | bytes 73732
  0.7 11.1 %copy-start.8 = (s32[1,384]{1,0:T(1,128)S(1)}, s32[1,384]{1,0:T(1,128)}, u32[]{:S(2)}) copy-start(s32[1,384]{1,0:T(1,128)} %types.1) | copy-start | bytes 4612
  0.7 11.0 %copy-start.7 = (s32[1,384]{1,0:T(1,128)S(1)}, s32[1,384]{1,0:T(1,128)}, u32[]{:S(2)}) copy-start(s32[1,384]{1,0:T(1,128)} %counts.1) | copy-start | bytes 4612
  2.2 21.0 %copy-start.13 = (s32[1,48,48]{2,1,0:T(8,128)S(1)}, s32[1,48,48]{2,1,0:T(8,128)}, u32[]{:S(2)}) copy-start(s32[1,48,48]{2,1,0:T(8,128)} %param.21) | copy-start | bytes 27652
  2.2 19.0 %all-to-all-start = ((bf16[32,48,128]{2,1,0:T(8,128)(2,1)}), bf16[32,48,128]{2,1,0:T(8,128)(2,1)S(1)}, u32[]{:S(2)}, u32[]{:S(2)}) async-start(bf16[32,48,128]{2,1,0:T(8,128)(2,1)} %broadcast_in_dim.52), calls=%async_computation | async-start | bytes 786432 | tf_op jit(solution)/shard_map/all_to_all | solution.py:37
  11.6 11.7 %slice-start = ((bf16[2,128,640]{2,1,0:T(8,128)(2,1)}), bf16[1,128,640]{2,1,0:T(8,128)(2,1)S(1)}, s32[]{:S(2)}) async-start(bf16[2,128,640]{2,1,0:T(8,128)(2,1)} %param.26), calls=%async_computation.6 | async-start | bytes 327680 | tf_op jit(solution)/shard_map/slice | solution.py:572
  11.7 11.8 %copy-start.14 = (f32[2,128]{1,0:T(2,128)S(1)}, f32[2,128]{1,0:T(2,128)}, u32[]{:S(2)}) copy-start(f32[2,128]{1,0:T(2,128)} %param.25) | copy-start | bytes 3076
  14.6 10.1 %copy-start.2 = (bf16[384,256]{1,0:T(8,128)(2,1)S(1)}, bf16[384,256]{1,0:T(8,128)(2,1)}, u32[]{:S(2)}) copy-start(bf16[384,256]{1,0:T(8,128)(2,1)} %w_pair.1) | copy-start | bytes 589828
  14.6 10.1 %copy-start.3 = (bf16[128,384]{1,0:T(8,128)(2,1)S(1)}, bf16[128,384]{1,0:T(8,128)(2,1)}, u32[]{:S(2)}) copy-start(bf16[128,384]{1,0:T(8,128)(2,1)} %w_atom.1) | copy-start | bytes 294916
  21.2 3.4 %collective-permute-start = (bf16[1536,128]{1,0:T(8,128)(2,1)S(1)}, bf16[1536,128]{1,0:T(8,128)(2,1)S(1)}, u32[]{:S(2)}, u32[]{:S(2)}) collective-permute-start(bf16[1536,128]{1,0:T(8,128)(2,1)S(1)} %bitcast.49), channel_id=1, source_target_pairs={{0,16},{16,0},{1,17},{17,1},{2,18},{18,2},{3,19},{19,3},{4,20},{20... | collective-permute-start | bytes 1179656 | tf_op jit(solution)/shard_map/ppermute | solution.py:503
  51.7 8.1 %copy-start.12 = (bf16[2,128,128]{2,1,0:T(8,128)(2,1)S(1)}, bf16[2,128,128]{2,1,0:T(8,128)(2,1)}, u32[]{:S(2)}) copy-start(bf16[2,128,128]{2,1,0:T(8,128)(2,1)} %param.28) | copy-start | bytes 196612
  54.8 5.0 %copy-start.9 = (bf16[2,128,640]{2,1,0:T(8,128)(2,1)S(1)}, bf16[2,128,640]{2,1,0:T(8,128)(2,1)}, u32[]{:S(2)}) copy-start(bf16[2,128,640]{2,1,0:T(8,128)(2,1)} %param.26) | copy-start | bytes 983044
  54.9 5.3 %copy-start.15 = (f32[2,128]{1,0:T(2,128)S(1)}, f32[2,128]{1,0:T(2,128)}, u32[]{:S(2)}) copy-start(f32[2,128]{1,0:T(2,128)} %param.27) | copy-start | bytes 3076
  54.9 6.4 %copy-start.11 = (bf16[512,128]{1,0:T(8,128)(2,1)S(1)}, bf16[512,128]{1,0:T(8,128)(2,1)}, u32[]{:S(2)}) copy-start(bf16[512,128]{1,0:T(8,128)(2,1)} %param.31) | copy-start | bytes 393220
  54.9 18.7 %all-to-all-start.2 = ((bf16[64,36,128]{2,1,0:T(8,128)(2,1)}), bf16[64,36,128]{2,1,0:T(8,128)(2,1)S(1)}, u32[]{:S(2)}, u32[]{:S(2)}) async-start(bf16[64,36,128]{2,1,0:T(8,128)(2,1)} %triangle.2), calls=%async_computation.2 | async-start | bytes 1310720 | tf_op jit(solution)/shard_map/all_to_all | solution.py:37
  59.8 1.6 %copy-start.10 = (bf16[128,1024]{1,0:T(8,128)(2,1)S(1)}, bf16[128,1024]{1,0:T(8,128)(2,1)}, u32[]{:S(2)}) copy-start(bf16[128,1024]{1,0:T(8,128)(2,1)} %param.30) | copy-start | bytes 786436
  60.1 1.6 %copy-start.4 = (bf16[1,48,48,128]{3,2,1,0:T(8,128)(2,1)S(1)}, bf16[1,48,48,128]{3,2,1,0:T(8,128)(2,1)}, u32[]{:S(2)}) copy-start(bf16[1,48,48,128]{3,2,1,0:T(8,128)(2,1)} %param.32) | copy-start | bytes 1769476
  61.7 1.6 %copy-start.16 = (f32[128]{0:T(128)S(1)}, f32[128]{0:T(128)}, u32[]{:S(2)}) copy-start(f32[128]{0:T(128)} %param.29) | copy-start | bytes 1540
  124.7 16.2 %all-to-all-start.5 = ((bf16[128,4,128]{2,1,0:T(4,128)(2,1)}), bf16[128,4,128]{2,1,0:T(4,128)(2,1)S(1)}, u32[]{:S(2)}, u32[]{:S(2)}) async-start(bf16[128,4,128]{2,1,0:T(4,128)(2,1)} %bitcast.66), calls=%async_computation.5 | async-start | bytes 262144 | tf_op jit(solution)/shard_map/all_to_all | solution.py:37
  130.9 1.7 %copy-start = (bf16[6,512,384]{2,1,0:T(8,128)(2,1)S(1)}, bf16[6,512,384]{2,1,0:T(8,128)(2,1)}, u32[]{:S(2)}) copy-start(bf16[6,512,384]{2,1,0:T(8,128)(2,1)} %get-tuple-element.80.hidden) | copy-start | bytes 7077892
  132.6 1.1 copy-start.1

commit v6 on v5

--- a/solution.py
+++ b/solution.py
@@ -339,13 +339,13 @@
         for move in both:
             move.start()
     thin[: devices * each] = tri[...].astype(F32).reshape(devices * each, LANES)
+    for both in moves:
+        for move in both:
+            move.wait()
     changes = [
         change_of(g, each, devices, thin, gain_out, w_out) for g in range(0, groups, LATE)
     ]
     for g in range(0, groups, LATE):
-        for both in moves[g : g + LATE]:
-            for move in both:
-                move.wait()
         block = updated(g, changes[g // LATE], here, gates)
         apart(pair_new, g, block)
         normed = norm(block.astype(F32), widened(gain, LATE), 0).astype(BF16)

time: 142 us -> 142 us (level)
  no operation moved by 1% of the time
where the time goes in v6:
time: 142 us; the launch traced here: 141 us
  blocking collectives  64.8 us (46%)
  Pallas kernels  26.9 us (19%)
  starting transfers between devices  22.3 us (16%)
  waiting for transfers between devices  18.5 us (13%)
  local copies, waits for them, and re-layouts  6.83 us (5%)
    all_to_all x3, blocking collectives, exchange(): return lax.all_to_all(value, axes, 0, 0, tiled=True)  64.8 us
    pallas_call x9, Pallas kernels, call(): pl.pallas_call(kernel, out_shape=outs, in_specs=[pl.BlockSpec(memory_spac...  26.9 us
    all_to_all x3, starting transfers between devices, exchange(): return lax.all_to_all(value, axes, 0, 0, tiled=True)  20.3 us
    all_to_all x3, waiting for transfers between devices, exchange(): return lax.all_to_all(value, axes, 0, 0, tiled=True)  17.5 us
    unnamed x35, local copies, waits for them, and re-layouts  2.97 us
  transfers between devices with their start and end apart: 4, of which 4 were waited for; matrix products, arithmetic and copies ran while one was open for 2% of the time, Pallas kernels for 7%

profile of v6, /device:TPU:1, one launch (start us, length us, event | category | flops | bytes accessed | tf_op | source)
XLA Modules:
  0.0 141.3 jit_solution(11264852220521607747)
XLA Ops:
  0.7 1.6 %broadcast_in_dim.52 = bf16[32,48,128]{2,1,0:T(8,128)(2,1)} broadcast(bf16[48,128]{1,0:T(8,128)(2,1)} %bitcast.72), dimensions={1,2} | broadcast | bytes 405504 | tf_op jit(solution)/shard_map/broadcast_in_dim | solution.py:474
  2.2 9.4 %all-to-all-start = ((bf16[32,48,128]{2,1,0:T(8,128)(2,1)}), bf16[32,48,128]{2,1,0:T(8,128)(2,1)S(1)}, u32[]{:S(2)}, u32[]{:S(2)}) async-start(bf16[32,48,128]{2,1,0:T(8,128)(2,1)} %broadcast_in_dim.52), calls=%async_computation | async-start | bytes 786432 | tf_op jit(solution)/shard_map/all_to_all | solution.py:37
  11.7 2.9 %prepare.1 = (bf16[6,128,384]{2,1,0:T(8,128)(2,1)}, s32[96,4]{1,0:T(8,128)S(1)}, s32[5]{0:T(128)S(1)}, bf16[6,96,384]{2,1,0:T(8,128)(2,1)S(1)}, f32[96,384]{1,0:T(8,128)S(1)}) custom-call(s32[2]{0:T(128)S(1)} %pad_add_fusion.place, bf16[48,48,128]{2,1,0:T(8,128)(2,1)S(1)} %bitcast.58, s32[1,384]{1,0:T(1,128)S(1)} %copy-done.7, s32[1,384]{1,0:T(1,128)S(1)} %copy-done.8, ...), custom_call_target="tpu_custom_call" | custom-call | flops 400000000 | bytes 4194304 | tf_op jit(solution)/shard_map/prepare/pallas_call | solution.py:429
  14.6 6.6 %all-to-all-done = bf16[32,48,128]{2,1,0:T(8,128)(2,1)S(1)} async-done(((bf16[32,48,128]{2,1,0:T(8,128)(2,1)}), bf16[32,48,128]{2,1,0:T(8,128)(2,1)S(1)}, u32[]{:S(2)}, u32[]{:S(2)}) %all-to-all-start) | async-done | bytes 393248 | tf_op jit(solution)/shard_map/all_to_all | solution.py:37
  21.2 2.0 %collective-permute-start = (bf16[1536,128]{1,0:T(8,128)(2,1)S(1)}, bf16[1536,128]{1,0:T(8,128)(2,1)S(1)}, u32[]{:S(2)}, u32[]{:S(2)}) collective-permute-start(bf16[1536,128]{1,0:T(8,128)(2,1)S(1)} %bitcast.49), channel_id=1, source_target_pairs={{0,16},{16,0},{1,17},{17,1},{2,18},{18,2},{3,19},{19,3},{4,20},{20... | collective-permute-start | bytes 1179656 | tf_op jit(solution)/shard_map/ppermute | solution.py:503
  23.3 0.2 copy.54
  23.6 1.0 collective-permute-done.other
  24.7 3.5 %front.1 = (bf16[64,72,128]{2,1,0:T(8,128)(2,1)S(1)}, bf16[128,96]{1,0:T(8,128)(2,1)S(1)}) custom-call(s32[5]{0:T(128)S(1)} %get-tuple-element.44.bounds, bf16[1536,128]{1,0:T(8,128)(2,1)S(1)} %bitcast.50, bf16[1536,128]{1,0:T(8,128)(2,1)S(1)} %collective-permute-done.other, s32[96,4]{1,0:T(8,128)S(1)} %get-tuple-element.46.tokens, ...), custom_call_target="tpu_custom_call" | custom-call | flops 400000000 | bytes 4194304 | tf_op jit(solution)/shard_map/front/pallas_call | solution.py:429
  28.2 23.5 %all_to_all.30.x = bf16[64,72,128]{2,1,0:T(8,128)(2,1)S(1)} all-to-all(bf16[64,72,128]{2,1,0:T(8,128)(2,1)S(1)} %get-tuple-element.50), channel_id=1, replica_groups=mesh['x'=4,'core'=2,'y'=4,'zl'=2,'rep'=2] {'y','zl','x','core'}, dimensions={0} | all-to-all | bytes 2359296 | tf_op jit(solution)/shard_map/all_to_all | solution.py:37
  51.7 3.1 %triangle.2 = bf16[64,36,128]{2,1,0:T(8,128)(2,1)} custom-call(bf16[64,72,128]{2,1,0:T(8,128)(2,1)S(1)} %all_to_all.30.x), custom_call_target="tpu_custom_call" | custom-call | flops 400000000 | bytes 4194304 | tf_op jit(solution)/shard_map/triangle/pallas_call | solution.py:429
  54.9 4.9 %all-to-all-start.2 = ((bf16[64,36,128]{2,1,0:T(8,128)(2,1)}), bf16[64,36,128]{2,1,0:T(8,128)(2,1)S(1)}, u32[]{:S(2)}, u32[]{:S(2)}) async-start(bf16[64,36,128]{2,1,0:T(8,128)(2,1)} %triangle.2), calls=%async_computation.2 | async-start | bytes 1310720 | tf_op jit(solution)/shard_map/all_to_all | solution.py:37
  59.9 0.2 copy.42
  60.3 0.1 reshape_squeeze.14
  60.4 0.1 copy.49
  60.7 0.1 reshape_squeeze.12
  60.8 0.1 copy.43
  61.3 0.1 copy.53
  61.4 0.2 copy.52
  61.7 1.3 turn.1.d_pair
  63.5 3.5 %first_gate.1 = (bf16[6,128,384]{2,1,0:T(8,128)(2,1)}, bf16[6,128,384]{2,1,0:T(8,128)(2,1)}) custom-call(bf16[48,48,128]{2,1,0:T(8,128)(2,1)S(1)} %bitcast.59, bf16[128,96]{1,0:T(8,128)(2,1)S(1)} %get-tuple-element.54.sides, f32[128,384]{1,0:T(8,128)S(1)} %broadcast_in_dim.56.gain, bf16[128,128]{1,0:T(8,128)(2,1)S(1)} %get-tuple-element.89.w_gate), custom_call_target="tpu_custom_call" | custom-call | flops 400000000 | bytes 4194304 | tf_op jit(solution)/shard_map/first_gate/pallas_call | solution.py:429
  67.0 6.6 %all-to-all-done.2.tri = bf16[64,36,128]{2,1,0:T(8,128)(2,1)S(1)} async-done(((bf16[64,36,128]{2,1,0:T(8,128)(2,1)}), bf16[64,36,128]{2,1,0:T(8,128)(2,1)S(1)}, u32[]{:S(2)}, u32[]{:S(2)}) %all-to-all-start.2) | async-done | bytes 589856 | tf_op jit(solution)/shard_map/all_to_all | solution.py:37
  73.6 3.4 %middle.1 = (bf16[64,72,128]{2,1,0:T(8,128)(2,1)S(1)}, bf16[6,128,384]{2,1,0:T(8,128)(2,1)S(1)}, bf16[6,128,384]{2,1,0:T(8,128)(2,1)S(1)}) custom-call(bf16[64,36,128]{2,1,0:T(8,128)(2,1)S(1)} %all-to-all-done.2.tri, bf16[6,128,384]{2,1,0:T(8,128)(2,1)} %get-tuple-element.57.pair, bf16[6,128,384]{2,1,0:T(8,128)(2,1)} %get-tuple-element.58.gate, ...), custom_call_target="tpu_custom_call" | custom-call | flops 400000000 | bytes 4194304 | tf_op jit(solution)/shard_map/middle/pallas_call | solution.py:429
  77.0 23.4 %all_to_all.31.refs_0_ = bf16[64,72,128]{2,1,0:T(8,128)(2,1)S(1)} all-to-all(bf16[64,72,128]{2,1,0:T(8,128)(2,1)S(1)} %get-tuple-element.72), channel_id=1, replica_groups=mesh['x'=4,'core'=2,'y'=4,'zl'=2,'rep'=2] {'x','core','y','zl'}, dimensions={0} | all-to-all | bytes 2359296 | tf_op jit(solution)/shard_map/all_to_all | solution.py:37
  100.4 2.4 %triangle.3 = bf16[64,36,128]{2,1,0:T(8,128)(2,1)S(1)} custom-call(bf16[64,72,128]{2,1,0:T(8,128)(2,1)S(1)} %all_to_all.31.refs_0_), custom_call_target="tpu_custom_call" | custom-call | flops 400000000 | bytes 4194304 | tf_op jit(solution)/shard_map/triangle/pallas_call | solution.py:429
  102.8 17.8 %all_to_all.32.tri = bf16[64,36,128]{2,1,0:T(8,128)(2,1)S(1)} all-to-all(bf16[64,36,128]{2,1,0:T(8,128)(2,1)S(1)} %triangle.3), channel_id=1, replica_groups=mesh['x'=4,'core'=2,'y'=4,'zl'=2,'rep'=2] {'x','core','y','zl'}, dimensions={0} | all-to-all | bytes 1179648 | tf_op jit(solution)/shard_map/all_to_all | solution.py:37
  120.7 3.9 %last.1 = (bf16[512,128]{1,0:T(8,128)(2,1)}, bf16[6,512,384]{2,1,0:T(8,128)(2,1)}, bf16[6,128,384]{2,1,0:T(8,128)(2,1)}) custom-call(bf16[64,36,128]{2,1,0:T(8,128)(2,1)S(1)} %all_to_all.32.tri, bf16[6,128,384]{2,1,0:T(8,128)(2,1)S(1)} %get-tuple-element.73.pair, bf16[6,128,384]{2,1,0:T(8,128)(2,1)S(1)} %get-tuple-element.74.gate, ...), custom_call_target="tpu_custom_call" | custom-call | flops 800000000 | bytes 4194304 | tf_op jit(solution)/shard_map/last/pallas_call | solution.py:429
  124.6 6.0 %all-to-all-start.5 = ((bf16[128,4,128]{2,1,0:T(4,128)(2,1)}), bf16[128,4,128]{2,1,0:T(4,128)(2,1)S(1)}, u32[]{:S(2)}, u32[]{:S(2)}) async-start(bf16[128,4,128]{2,1,0:T(4,128)(2,1)} %bitcast.66), calls=%async_computation.5 | async-start | bytes 262144 | tf_op jit(solution)/shard_map/all_to_all | solution.py:37
  130.6 1.7 %copy-done = bf16[6,512,384]{2,1,0:T(8,128)(2,1)S(1)} copy-done((bf16[6,512,384]{2,1,0:T(8,128)(2,1)S(1)}, bf16[6,512,384]{2,1,0:T(8,128)(2,1)}, u32[]{:S(2)}) %copy-start) | copy-done | bytes 2359320
  132.3 1.1 copy-done.1
  133.4 2.9 %down.1 = bf16[48,48,128]{2,1,0:T(8,128)(2,1)} custom-call(bf16[6,512,384]{2,1,0:T(8,128)(2,1)S(1)} %copy-done, bf16[6,128,384]{2,1,0:T(8,128)(2,1)S(1)} %copy-done.1, bf16[128,512]{1,0:T(8,128)(2,1)S(1)} %bitcast.52), custom_call_target="tpu_custom_call" | custom-call | flops 400000000 | bytes 4194304 | tf_op jit(solution)/shard_map/down/pallas_call | solution.py:429
  136.3 4.3 %all-to-all-done.5 = bf16[128,4,128]{2,1,0:T(4,128)(2,1)S(1)} async-done(((bf16[128,4,128]{2,1,0:T(4,128)(2,1)}), bf16[128,4,128]{2,1,0:T(4,128)(2,1)S(1)}, u32[]{:S(2)}, u32[]{:S(2)}) %all-to-all-start.5) | async-done | bytes 131104 | tf_op jit(solution)/shard_map/all_to_all | solution.py:37
  140.6 0.7 convert_reduce_fusion
  (62 shorter events, 1.4 us)
Async XLA Ops:
  0.6 11.1 %copy-start.5 = (bf16[1,48,48,128]{3,2,1,0:T(8,128)(2,1)S(1)}, bf16[1,48,48,128]{3,2,1,0:T(8,128)(2,1)}, u32[]{:S(2)}) copy-start(bf16[1,48,48,128]{3,2,1,0:T(8,128)(2,1)} %param.20) | copy-start | bytes 1769476
  0.6 11.1 %copy-start.6 = (bf16[32,384]{1,0:T(8,128)(2,1)S(1)}, bf16[32,384]{1,0:T(8,128)(2,1)}, u32[]{:S(2)}) copy-start(bf16[32,384]{1,0:T(8,128)(2,1)} %w_restype.1) | copy-start | bytes 73732
  0.7 11.1 %copy-start.8 = (s32[1,384]{1,0:T(1,128)S(1)}, s32[1,384]{1,0:T(1,128)}, u32[]{:S(2)}) copy-start(s32[1,384]{1,0:T(1,128)} %types.1) | copy-start | bytes 4612
  0.7 11.0 %copy-start.7 = (s32[1,384]{1,0:T(1,128)S(1)}, s32[1,384]{1,0:T(1,128)}, u32[]{:S(2)}) copy-start(s32[1,384]{1,0:T(1,128)} %counts.1) | copy-start | bytes 4612
  2.2 21.0 %copy-start.13 = (s32[1,48,48]{2,1,0:T(8,128)S(1)}, s32[1,48,48]{2,1,0:T(8,128)}, u32[]{:S(2)}) copy-start(s32[1,48,48]{2,1,0:T(8,128)} %param.21) | copy-start | bytes 27652
  2.2 19.0 %all-to-all-start = ((bf16[32,48,128]{2,1,0:T(8,128)(2,1)}), bf16[32,48,128]{2,1,0:T(8,128)(2,1)S(1)}, u32[]{:S(2)}, u32[]{:S(2)}) async-start(bf16[32,48,128]{2,1,0:T(8,128)(2,1)} %broadcast_in_dim.52), calls=%async_computation | async-start | bytes 786432 | tf_op jit(solution)/shard_map/all_to_all | solution.py:37
  11.6 11.7 %slice-start = ((bf16[2,128,640]{2,1,0:T(8,128)(2,1)}), bf16[1,128,640]{2,1,0:T(8,128)(2,1)S(1)}, s32[]{:S(2)}) async-start(bf16[2,128,640]{2,1,0:T(8,128)(2,1)} %param.26), calls=%async_computation.6 | async-start | bytes 327680 | tf_op jit(solution)/shard_map/slice | solution.py:572
  11.7 11.8 %copy-start.14 = (f32[2,128]{1,0:T(2,128)S(1)}, f32[2,128]{1,0:T(2,128)}, u32[]{:S(2)}) copy-start(f32[2,128]{1,0:T(2,128)} %param.25) | copy-start | bytes 3076
  14.6 10.1 %copy-start.2 = (bf16[384,256]{1,0:T(8,128)(2,1)S(1)}, bf16[384,256]{1,0:T(8,128)(2,1)}, u32[]{:S(2)}) copy-start(bf16[384,256]{1,0:T(8,128)(2,1)} %w_pair.1) | copy-start | bytes 589828
  14.6 10.1 %copy-start.3 = (bf16[128,384]{1,0:T(8,128)(2,1)S(1)}, bf16[128,384]{1,0:T(8,128)(2,1)}, u32[]{:S(2)}) copy-start(bf16[128,384]{1,0:T(8,128)(2,1)} %w_atom.1) | copy-start | bytes 294916
  21.2 3.4 %collective-permute-start = (bf16[1536,128]{1,0:T(8,128)(2,1)S(1)}, bf16[1536,128]{1,0:T(8,128)(2,1)S(1)}, u32[]{:S(2)}, u32[]{:S(2)}) collective-permute-start(bf16[1536,128]{1,0:T(8,128)(2,1)S(1)} %bitcast.49), channel_id=1, source_target_pairs={{0,16},{16,0},{1,17},{17,1},{2,18},{18,2},{3,19},{19,3},{4,20},{20... | collective-permute-start | bytes 1179656 | tf_op jit(solution)/shard_map/ppermute | solution.py:503
  51.7 8.1 %copy-start.12 = (bf16[2,128,128]{2,1,0:T(8,128)(2,1)S(1)}, bf16[2,128,128]{2,1,0:T(8,128)(2,1)}, u32[]{:S(2)}) copy-start(bf16[2,128,128]{2,1,0:T(8,128)(2,1)} %param.28) | copy-start | bytes 196612
  54.8 5.0 %copy-start.9 = (bf16[2,128,640]{2,1,0:T(8,128)(2,1)S(1)}, bf16[2,128,640]{2,1,0:T(8,128)(2,1)}, u32[]{:S(2)}) copy-start(bf16[2,128,640]{2,1,0:T(8,128)(2,1)} %param.26) | copy-start | bytes 983044
  54.9 5.3 %copy-start.15 = (f32[2,128]{1,0:T(2,128)S(1)}, f32[2,128]{1,0:T(2,128)}, u32[]{:S(2)}) copy-start(f32[2,128]{1,0:T(2,128)} %param.27) | copy-start | bytes 3076
  54.9 6.4 %copy-start.11 = (bf16[512,128]{1,0:T(8,128)(2,1)S(1)}, bf16[512,128]{1,0:T(8,128)(2,1)}, u32[]{:S(2)}) copy-start(bf16[512,128]{1,0:T(8,128)(2,1)} %param.31) | copy-start | bytes 393220
  54.9 18.7 %all-to-all-start.2 = ((bf16[64,36,128]{2,1,0:T(8,128)(2,1)}), bf16[64,36,128]{2,1,0:T(8,128)(2,1)S(1)}, u32[]{:S(2)}, u32[]{:S(2)}) async-start(bf16[64,36,128]{2,1,0:T(8,128)(2,1)} %triangle.2), calls=%async_computation.2 | async-start | bytes 1310720 | tf_op jit(solution)/shard_map/all_to_all | solution.py:37
  59.8 1.6 %copy-start.10 = (bf16[128,1024]{1,0:T(8,128)(2,1)S(1)}, bf16[128,1024]{1,0:T(8,128)(2,1)}, u32[]{:S(2)}) copy-start(bf16[128,1024]{1,0:T(8,128)(2,1)} %param.30) | copy-start | bytes 786436
  60.1 1.6 %copy-start.4 = (bf16[1,48,48,128]{3,2,1,0:T(8,128)(2,1)S(1)}, bf16[1,48,48,128]{3,2,1,0:T(8,128)(2,1)}, u32[]{:S(2)}) copy-start(bf16[1,48,48,128]{3,2,1,0:T(8,128)(2,1)} %param.32) | copy-start | bytes 1769476
  61.7 1.6 %copy-start.16 = (f32[128]{0:T(128)S(1)}, f32[128]{0:T(128)}, u32[]{:S(2)}) copy-start(f32[128]{0:T(128)} %param.29) | copy-start | bytes 1540
  124.6 15.9 %all-to-all-start.5 = ((bf16[128,4,128]{2,1,0:T(4,128)(2,1)}), bf16[128,4,128]{2,1,0:T(4,128)(2,1)S(1)}, u32[]{:S(2)}, u32[]{:S(2)}) async-start(bf16[128,4,128]{2,1,0:T(4,128)(2,1)} %bitcast.66), calls=%async_computation.5 | async-start | bytes 262144 | tf_op jit(solution)/shard_map/all_to_all | solution.py:37
  130.6 1.7 %copy-start = (bf16[6,512,384]{2,1,0:T(8,128)(2,1)S(1)}, bf16[6,512,384]{2,1,0:T(8,128)(2,1)}, u32[]{:S(2)}) copy-start(bf16[6,512,384]{2,1,0:T(8,128)(2,1)} %get-tuple-element.80.hidden) | copy-start | bytes 7077892
  132.3 1.1 copy-start.1
